TPU v7x, 256 devices: a whole 4x4x8 slice. The times are simulated.
256 devices in a mesh: blk: 32 (over z, y_hi, core), head: 8 (over y_lo, x).
Axes of the slice: x: 4, y: 4 (y_hi: 2, y_lo: 2; y = y_hi * 2 + y_lo), z: 8, core: 2. Of those that a mesh axis runs over, the one named last changes fastest.
Arguments:
- queries: bfloat16 [32768, 4096], P(('blk', 'head')), may hold values from -7 to 7
- key_states: bfloat16 [32768, 1024], P(('blk', 'head')), may hold values from -4.5 to 4.5
- value_states: bfloat16 [32768, 1024], P(('blk', 'head')), may hold values from -6 to 6
- grad_output: bfloat16 [32768, 4096], P(('blk', 'head')), may hold values from -12 to 12
- segment_ids: int32 [32768], replicated, may hold values from 0 to 15, never falling along the last dimension, each value on 1 to 4096 neighbouring positions
Outputs:
- attn_out: bfloat16 [32768, 4096], P(('blk', 'head'))
- grad_queries: bfloat16 [32768, 4096], P(('blk', 'head'))
- grad_keys: bfloat16 [32768, 1024], P(('blk', 'head'))
- grad_values: bfloat16 [32768, 1024], P(('blk', 'head'))
Inputs may be any that keep to these rules, and one draw needn't show every extreme that they name: `segment_ids`: segment numbers never fall along the sequence; equal numbers mark one trajectory.
All inputs are finite; a program needn't handle non-finite values.
Results may differ from a plain program's by a relative error of at most 0.02.
Values may be sent and summed in bfloat16 or wider, within the bound.
No kernel may reach another device: no remote copies, remote signals or barrier semaphores. Data moves between devices by JAX's collectives and lax.ppermute only.
A program may use at most 64 MiB of HBM per device.

v0:
```python
import math

import jax
import jax.numpy as jnp
from jax import lax
from jax.sharding import PartitionSpec as P

QHEADS = 32
KVHEADS = 8
HEAD_DIM = 128


MASKED = -1e30


def shifted(value, axis, steps):
    count = lax.axis_size(axis)
    leading, last = (max(0, -steps), min(count, count - steps))
    return lax.ppermute(value, axis, [(source, source + steps) for source in range(leading, last)])


def shards(queries, key_states, value_states, grad_output, segment_ids):
    group_size = QHEADS // KVHEADS
    scaling = 1.0 / math.sqrt(HEAD_DIM)
    block_index = lax.axis_index("blk")
    query_local, key_local, value_local, grad_local = (
        lax.all_to_all(queries, "head", split_axis=1, concat_axis=0, tiled=True),
        lax.all_to_all(key_states, "head", split_axis=1, concat_axis=0, tiled=True),
        lax.all_to_all(value_states, "head", split_axis=1, concat_axis=0, tiled=True),
        lax.all_to_all(grad_output, "head", split_axis=1, concat_axis=0, tiled=True),
    )
    key_before, value_before = shifted((key_local, value_local), "blk", 1)
    row_count = key_local.shape[0]
    kv_local = key_local.shape[1] // HEAD_DIM
    key_ext = (
        jnp.concatenate([key_before, key_local], axis=0)
        .reshape(2 * row_count, kv_local, HEAD_DIM)
        .transpose(1, 0, 2)
    )
    value_ext = (
        jnp.concatenate([value_before, value_local], axis=0)
        .reshape(2 * row_count, kv_local, HEAD_DIM)
        .transpose(1, 0, 2)
    )
    query_heads = query_local.reshape(row_count, kv_local, group_size, HEAD_DIM).transpose(
        1, 2, 0, 3
    )
    grad_heads = grad_local.reshape(row_count, kv_local, group_size, HEAD_DIM).transpose(1, 2, 0, 3)
    padded_seg = jnp.concatenate([jnp.full((row_count,), -1, jnp.int32), segment_ids])
    first_row = block_index * row_count
    query_seg = lax.dynamic_slice_in_dim(segment_ids, first_row, row_count)
    key_seg = lax.dynamic_slice_in_dim(padded_seg, first_row, 2 * row_count)
    row_ids = jnp.arange(row_count, dtype=jnp.int32)[:, None]
    col_ids = jnp.arange(2 * row_count, dtype=jnp.int32)[None, :]
    allowed = (
        (col_ids > row_ids)
        & (col_ids <= row_ids + row_count)
        & (key_seg[None, :] == query_seg[:, None])
    )

    def one_group(inputs):
        query_group, grad_group, key_group, value_group = inputs

        def one_head(sums, head_pair):
            key_sum, value_sum = sums
            query_head, grad_head = head_pair
            scores = jnp.dot(query_head, key_group.T, preferred_element_type=jnp.float32) * scaling
            scores = jnp.where(allowed, scores, MASKED)
            row_top = jnp.max(scores, axis=1, keepdims=True)
            kept_terms = jnp.where(allowed, jnp.exp(scores - row_top), 0.0)
            log_total = row_top + jnp.log(jnp.sum(kept_terms, axis=1, keepdims=True))
            weights = jnp.where(allowed, jnp.exp(scores - log_total), 0.0).astype(jnp.bfloat16)
            output = jnp.dot(weights, value_group, preferred_element_type=jnp.float32).astype(
                jnp.bfloat16
            )
            row_dot = jnp.sum(
                grad_head.astype(jnp.float32) * output.astype(jnp.float32), axis=1, keepdims=True
            )
            grad_weights = jnp.dot(grad_head, value_group.T, preferred_element_type=jnp.float32)
            grad_scores = (weights.astype(jnp.float32) * (grad_weights - row_dot) * scaling).astype(
                jnp.bfloat16
            )
            grad_query = jnp.dot(grad_scores, key_group, preferred_element_type=jnp.float32).astype(
                jnp.bfloat16
            )
            key_term = jnp.dot(grad_scores.T, query_head, preferred_element_type=jnp.float32)
            value_term = jnp.dot(weights.T, grad_head, preferred_element_type=jnp.float32)
            return ((key_sum + key_term, value_sum + value_term), (output, grad_query))

        empty = jnp.zeros((2 * row_count, HEAD_DIM), jnp.float32)
        sums, per_head = lax.scan(one_head, (empty, empty), (query_group, grad_group))
        return (per_head[0], per_head[1], sums[0], sums[1])

    outputs, query_grads, key_sums, value_sums = lax.map(
        one_group, (query_heads, grad_heads, key_ext, value_ext)
    )
    output_local = outputs.transpose(2, 0, 1, 3).reshape(row_count, -1)
    key_back, value_back = shifted((key_sums[:, :row_count], value_sums[:, :row_count]), "blk", -1)
    key_total = key_sums[:, row_count:] + key_back
    value_total = value_sums[:, row_count:] + value_back
    query_grad_local = query_grads.transpose(2, 0, 1, 3).reshape(row_count, -1)
    key_grad_local = key_total.transpose(1, 0, 2).astype(jnp.bfloat16).reshape(row_count, -1)
    value_grad_local = value_total.transpose(1, 0, 2).astype(jnp.bfloat16).reshape(row_count, -1)
    attn_out, grad_queries, grad_keys, grad_values = (
        lax.all_to_all(output_local, "head", split_axis=0, concat_axis=1, tiled=True),
        lax.all_to_all(query_grad_local, "head", split_axis=0, concat_axis=1, tiled=True),
        lax.all_to_all(key_grad_local, "head", split_axis=0, concat_axis=1, tiled=True),
        lax.all_to_all(value_grad_local, "head", split_axis=0, concat_axis=1, tiled=True),
    )
    return (attn_out, grad_queries, grad_keys, grad_values)


def solution(mesh):
    placed = (
        P(("blk", "head"), None),
        P(("blk", "head"), None),
        P(("blk", "head"), None),
        P(("blk", "head"), None),
        P(),
    )
    return jax.shard_map(
        shards,
        mesh=mesh,
        in_specs=placed,
        out_specs=(
            P(("blk", "head"), None),
            P(("blk", "head"), None),
            P(("blk", "head"), None),
            P(("blk", "head"), None),
        ),
        check_vma=False,
    )
```

profile of v0, /device:TPU:160, one launch (start us, length us, event | category | flops | bytes accessed | tf_op | source)
XLA Modules:
  0.0 277.3 jit_solution(3258051867252446421)
XLA Ops:
  2.3 5.3 %all-to-all-start.1 = ((bf16[128,8,128]{2,0,1:T(8,128)(2,1)}), bf16[128,8,128]{2,0,1:T(8,128)(2,1)S(1)}, u32[]{:S(2)}, u32[]{:S(2)}) async-start(bf16[128,8,128]{2,0,1:T(8,128)(2,1)} %copy_bitcast_fusion.1), calls=%async_computation.1 | async-start | bytes 524288 | tf_op jit(solution)/shard_map/all_to_all | solution.py:28
  9.4 5.6 %all-to-all-done.1 = bf16[128,8,128]{2,0,1:T(8,128)(2,1)S(1)} async-done(((bf16[128,8,128]{2,0,1:T(8,128)(2,1)}), bf16[128,8,128]{2,0,1:T(8,128)(2,1)S(1)}, u32[]{:S(2)}, u32[]{:S(2)}) %all-to-all-start.1) | async-done | bytes 262176 | tf_op jit(solution)/shard_map/all_to_all | solution.py:28
  20.6 5.0 %all-to-all-done.3 = bf16[128,8,128]{2,0,1:T(8,128)(2,1)S(1)} async-done(((bf16[128,8,128]{2,0,1:T(8,128)(2,1)}), bf16[128,8,128]{2,0,1:T(8,128)(2,1)S(1)}, u32[]{:S(2)}, u32[]{:S(2)}) %all-to-all-start.3) | async-done | bytes 262176 | tf_op jit(solution)/shard_map/all_to_all | solution.py:29
  31.4 11.2 %all-to-all-done = bf16[128,8,512]{0,2,1:T(8,128)(2,1)S(1)} async-done(((bf16[128,8,512]{0,2,1:T(8,128)(2,1)}), bf16[128,8,512]{0,2,1:T(8,128)(2,1)S(1)}, u32[]{:S(2)}, u32[]{:S(2)}) %all-to-all-start) | async-done | bytes 1048608 | tf_op jit(solution)/shard_map/all_to_all | solution.py:27
  42.7 4.2 %all-to-all-start.2 = ((bf16[128,8,512]{0,2,1:T(8,128)(2,1)}), bf16[128,8,512]{0,2,1:T(8,128)(2,1)}, u32[]{:S(2)}, u32[]{:S(2)}) async-start(bf16[128,8,512]{0,2,1:T(8,128)(2,1)} %bitcast.6), calls=%async_computation.2 | async-start | bytes 2097152 | tf_op jit(solution)/shard_map/all_to_all | solution.py:30
  48.9 4.9 %collective-permute-start.1 = (bf16[1024,128]{1,0:T(8,128)(2,1)S(1)}, bf16[1024,128]{1,0:T(8,128)(2,1)S(1)}, u32[]{:S(2)}, u32[]{:S(2)}) collective-permute-start(bf16[1024,128]{1,0:T(8,128)(2,1)S(1)} %bitcast.141), channel_id=1, source_target_pairs={{0,8},{8,16},{16,24},{24,32},{32,40},{40,48},{48,56},{56,64},{64,7... | collective-permute-start | bytes 786440 | tf_op jit(solution)/shard_map/ppermute | solution.py:19
  53.9 7.5 %collective-permute-done = bf16[1024,128]{1,0:T(8,128)(2,1)S(1)} collective-permute-done((bf16[1024,128]{1,0:T(8,128)(2,1)S(1)}, bf16[1024,128]{1,0:T(8,128)(2,1)S(1)}, u32[]{:S(2)}, u32[]{:S(2)}) %collective-permute-start) | collective-permute-done | bytes 262176 | tf_op jit(solution)/shard_map/ppermute | solution.py:19
  62.2 5.1 %collective-permute-done.1 = bf16[1024,128]{1,0:T(8,128)(2,1)S(1)} collective-permute-done((bf16[1024,128]{1,0:T(8,128)(2,1)S(1)}, bf16[1024,128]{1,0:T(8,128)(2,1)S(1)}, u32[]{:S(2)}, u32[]{:S(2)}) %collective-permute-start.1) | collective-permute-done | bytes 262176 | tf_op jit(solution)/shard_map/ppermute | solution.py:19
  77.7 126.8 %while.30 = (s32[]{:T(128)}, f32[2048,128]{1,0:T(8,128)S(1)}, f32[2048,128]{1,0:T(8,128)S(1)}, bf16[4,1024,128]{1,2,0:T(8,128)(2,1)}, bf16[4,1024,128]{2,1,0:T(8...) while((s32[]{:T(128)}, f32[2048,128]{1,0:T(8,128)S(1)}, ...), condition=%wide.region_4.5_spmd.clone, body=%wide.region_0.4_spmd.clone.sunk | while | flops 3292264448 | bytes 101014256 | solution.py:91
  77.7 4.4 %fusion.56 = (f32[1024]{0:T(1024)S(1)}, f32[1024,2048]{1,0:T(8,128)S(1)}) fusion(s32[1024]{0:T(1024)S(1)} %get-tuple-element.356, s32[2048]{0:T(1024)S(1)} %get-tuple-element.357, s32[1024]{0:T(1024)S(1)} %get-tuple-element.355, bf16[2048,128]{1,0:T(8,128)(2,1)} %get-tuple-element.352, bf16[4,1024,128]{1,2,0:T(8,128)(2,1)} %get-tuple-element.351, ...), kind=kOutput, calls=%fused_computation.9.clone.1 | convolution fusion | flops 553647104 | bytes 9196032 | tf_op jit(solution)/shard_map/while/body/eval_jaxpr/while/body/eval_jaxpr/dot_general | solution.py:67
  86.1 5.9 %select_convert_fusion.2 = bf16[1024,2048]{1,0:T(8,128)(2,1)S(1)} fusion(f32[1024,2048]{1,0:T(8,128)S(1)} %get-tuple-element.314, f32[1024]{0:T(1024)S(1)} %log_add_fusion.2, s32[1024]{0:T(1024)S(1)} %get-tuple-element.356, s32[2048]{0:T(1024)S(1)} %get-tuple-element.357, s32[1024]{0:T(1024)S(1)} %get-tuple-element.355), kind=kLoop, calls=%fused_computation.4.clone.1 | loop fusion | flops 20971520 | bytes 12603392 | tf_op jit(solution)/shard_map/while/body/eval_jaxpr/while/body/eval_jaxpr/convert_element_type | solution.py:72
  101.9 4.3 %fusion.57 = bf16[4,1024,128]{2,1,0:T(8,128)(2,1)} fusion(bf16[4,1024,128]{2,1,0:T(8,128)(2,1)} %get-tuple-element.336, s32[]{:T(128)} %get-tuple-element.332, bf16[1024,2048]{1,0:T(8,128)(2,1)} %multiply_convert_fusion.2, bf16[2048,128]{1,0:T(8,128)(2,1)} %get-tuple-element.352), kind=kOutput, calls=%fused_computation.15.clone.1 | convolution fusion | flops 537001984 | bytes 4981248 | tf_op jit(solution)/shard_map/while/body/eval_jaxpr/while/body/eval_jaxpr/dot_general | solution.py:83
  109.4 4.4 %fusion.56 = (f32[1024]{0:T(1024)S(1)}, f32[1024,2048]{1,0:T(8,128)S(1)}) fusion(s32[1024]{0:T(1024)S(1)} %get-tuple-element.356, s32[2048]{0:T(1024)S(1)} %get-tuple-element.357, s32[1024]{0:T(1024)S(1)} %get-tuple-element.355, bf16[2048,128]{1,0:T(8,128)(2,1)} %get-tuple-element.352, bf16[4,1024,128]{1,2,0:T(8,128)(2,1)} %get-tuple-element.351, ...), kind=kOutput, calls=%fused_computation.9.clone.1 | convolution fusion | flops 553647104 | bytes 9196032 | tf_op jit(solution)/shard_map/while/body/eval_jaxpr/while/body/eval_jaxpr/dot_general | solution.py:67
  117.8 5.9 %select_convert_fusion.2 = bf16[1024,2048]{1,0:T(8,128)(2,1)S(1)} fusion(f32[1024,2048]{1,0:T(8,128)S(1)} %get-tuple-element.314, f32[1024]{0:T(1024)S(1)} %log_add_fusion.2, s32[1024]{0:T(1024)S(1)} %get-tuple-element.356, s32[2048]{0:T(1024)S(1)} %get-tuple-element.357, s32[1024]{0:T(1024)S(1)} %get-tuple-element.355), kind=kLoop, calls=%fused_computation.4.clone.1 | loop fusion | flops 20971520 | bytes 12603392 | tf_op jit(solution)/shard_map/while/body/eval_jaxpr/while/body/eval_jaxpr/convert_element_type | solution.py:72
  133.5 4.3 %fusion.57 = bf16[4,1024,128]{2,1,0:T(8,128)(2,1)} fusion(bf16[4,1024,128]{2,1,0:T(8,128)(2,1)} %get-tuple-element.336, s32[]{:T(128)} %get-tuple-element.332, bf16[1024,2048]{1,0:T(8,128)(2,1)} %multiply_convert_fusion.2, bf16[2048,128]{1,0:T(8,128)(2,1)} %get-tuple-element.352), kind=kOutput, calls=%fused_computation.15.clone.1 | convolution fusion | flops 537001984 | bytes 4981248 | tf_op jit(solution)/shard_map/while/body/eval_jaxpr/while/body/eval_jaxpr/dot_general | solution.py:83
  141.0 4.4 %fusion.56 = (f32[1024]{0:T(1024)S(1)}, f32[1024,2048]{1,0:T(8,128)S(1)}) fusion(s32[1024]{0:T(1024)S(1)} %get-tuple-element.356, s32[2048]{0:T(1024)S(1)} %get-tuple-element.357, s32[1024]{0:T(1024)S(1)} %get-tuple-element.355, bf16[2048,128]{1,0:T(8,128)(2,1)} %get-tuple-element.352, bf16[4,1024,128]{1,2,0:T(8,128)(2,1)} %get-tuple-element.351, ...), kind=kOutput, calls=%fused_computation.9.clone.1 | convolution fusion | flops 553647104 | bytes 9196032 | tf_op jit(solution)/shard_map/while/body/eval_jaxpr/while/body/eval_jaxpr/dot_general | solution.py:67
  149.4 5.9 %select_convert_fusion.2 = bf16[1024,2048]{1,0:T(8,128)(2,1)S(1)} fusion(f32[1024,2048]{1,0:T(8,128)S(1)} %get-tuple-element.314, f32[1024]{0:T(1024)S(1)} %log_add_fusion.2, s32[1024]{0:T(1024)S(1)} %get-tuple-element.356, s32[2048]{0:T(1024)S(1)} %get-tuple-element.357, s32[1024]{0:T(1024)S(1)} %get-tuple-element.355), kind=kLoop, calls=%fused_computation.4.clone.1 | loop fusion | flops 20971520 | bytes 12603392 | tf_op jit(solution)/shard_map/while/body/eval_jaxpr/while/body/eval_jaxpr/convert_element_type | solution.py:72
  165.2 4.3 %fusion.57 = bf16[4,1024,128]{2,1,0:T(8,128)(2,1)} fusion(bf16[4,1024,128]{2,1,0:T(8,128)(2,1)} %get-tuple-element.336, s32[]{:T(128)} %get-tuple-element.332, bf16[1024,2048]{1,0:T(8,128)(2,1)} %multiply_convert_fusion.2, bf16[2048,128]{1,0:T(8,128)(2,1)} %get-tuple-element.352), kind=kOutput, calls=%fused_computation.15.clone.1 | convolution fusion | flops 537001984 | bytes 4981248 | tf_op jit(solution)/shard_map/while/body/eval_jaxpr/while/body/eval_jaxpr/dot_general | solution.py:83
  172.7 4.4 %fusion.56 = (f32[1024]{0:T(1024)S(1)}, f32[1024,2048]{1,0:T(8,128)S(1)}) fusion(s32[1024]{0:T(1024)S(1)} %get-tuple-element.356, s32[2048]{0:T(1024)S(1)} %get-tuple-element.357, s32[1024]{0:T(1024)S(1)} %get-tuple-element.355, bf16[2048,128]{1,0:T(8,128)(2,1)} %get-tuple-element.352, bf16[4,1024,128]{1,2,0:T(8,128)(2,1)} %get-tuple-element.351, ...), kind=kOutput, calls=%fused_computation.9.clone.1 | convolution fusion | flops 553647104 | bytes 9196032 | tf_op jit(solution)/shard_map/while/body/eval_jaxpr/while/body/eval_jaxpr/dot_general | solution.py:67
  181.1 5.9 %select_convert_fusion.2 = bf16[1024,2048]{1,0:T(8,128)(2,1)S(1)} fusion(f32[1024,2048]{1,0:T(8,128)S(1)} %get-tuple-element.314, f32[1024]{0:T(1024)S(1)} %log_add_fusion.2, s32[1024]{0:T(1024)S(1)} %get-tuple-element.356, s32[2048]{0:T(1024)S(1)} %get-tuple-element.357, s32[1024]{0:T(1024)S(1)} %get-tuple-element.355), kind=kLoop, calls=%fused_computation.4.clone.1 | loop fusion | flops 20971520 | bytes 12603392 | tf_op jit(solution)/shard_map/while/body/eval_jaxpr/while/body/eval_jaxpr/convert_element_type | solution.py:72
  196.8 4.3 %fusion.57 = bf16[4,1024,128]{2,1,0:T(8,128)(2,1)} fusion(bf16[4,1024,128]{2,1,0:T(8,128)(2,1)} %get-tuple-element.336, s32[]{:T(128)} %get-tuple-element.332, bf16[1024,2048]{1,0:T(8,128)(2,1)} %multiply_convert_fusion.2, bf16[2048,128]{1,0:T(8,128)(2,1)} %get-tuple-element.352), kind=kOutput, calls=%fused_computation.15.clone.1 | convolution fusion | flops 537001984 | bytes 4981248 | tf_op jit(solution)/shard_map/while/body/eval_jaxpr/while/body/eval_jaxpr/dot_general | solution.py:83
  231.3 5.5 %all-to-all-done.6 = bf16[8,128,128]{2,1,0:T(8,128)(2,1)S(1)} async-done(((bf16[8,128,128]{2,1,0:T(8,128)(2,1)}), bf16[8,128,128]{2,1,0:T(8,128)(2,1)S(1)}, u32[]{:S(2)}, u32[]{:S(2)}) %all-to-all-start.6) | async-done | bytes 262176 | tf_op jit(solution)/shard_map/all_to_all | solution.py:107
  242.4 14.2 %all-to-all-done.4 = bf16[8,128,512]{2,1,0:T(8,128)(2,1)S(1)} async-done(((bf16[8,128,512]{2,1,0:T(8,128)(2,1)}), bf16[8,128,512]{2,1,0:T(8,128)(2,1)S(1)}, u32[]{:S(2)}, u32[]{:S(2)}) %all-to-all-start.4) | async-done | bytes 1048608 | tf_op jit(solution)/shard_map/all_to_all | solution.py:105
  266.1 9.9 %all-to-all-done.5 = bf16[8,128,512]{1,2,0:T(8,128)(2,1)S(1)} async-done(((bf16[8,128,512]{1,2,0:T(8,128)(2,1)}), bf16[8,128,512]{1,2,0:T(8,128)(2,1)S(1)}, u32[]{:S(2)}, u32[]{:S(2)}) %all-to-all-start.5) | async-done | bytes 1048608 | tf_op jit(solution)/shard_map/all_to_all | solution.py:106
  (111 shorter events, 139.2 us)
Async XLA Ops:
  1.6 47.2 %copy-start.8 = (s32[32768]{0:T(1024)S(1)}, s32[32768]{0:T(1024)}, u32[]{:S(2)}) copy-start(s32[32768]{0:T(1024)} %param.11) | copy-start | bytes 393220
  2.3 12.6 %all-to-all-start.1 = ((bf16[128,8,128]{2,0,1:T(8,128)(2,1)}), bf16[128,8,128]{2,0,1:T(8,128)(2,1)S(1)}, u32[]{:S(2)}, u32[]{:S(2)}) async-start(bf16[128,8,128]{2,0,1:T(8,128)(2,1)} %copy_bitcast_fusion.1), calls=%async_computation.1 | async-start | bytes 524288 | tf_op jit(solution)/shard_map/all_to_all | solution.py:28
  14.9 10.6 %all-to-all-start.3 = ((bf16[128,8,128]{2,0,1:T(8,128)(2,1)}), bf16[128,8,128]{2,0,1:T(8,128)(2,1)S(1)}, u32[]{:S(2)}, u32[]{:S(2)}) async-start(bf16[128,8,128]{2,0,1:T(8,128)(2,1)} %copy_bitcast_fusion), calls=%async_computation.3 | async-start | bytes 524288 | tf_op jit(solution)/shard_map/all_to_all | solution.py:29
  25.6 17.1 %all-to-all-start = ((bf16[128,8,512]{0,2,1:T(8,128)(2,1)}), bf16[128,8,512]{0,2,1:T(8,128)(2,1)S(1)}, u32[]{:S(2)}, u32[]{:S(2)}) async-start(bf16[128,8,512]{0,2,1:T(8,128)(2,1)} %bitcast), calls=%async_computation | async-start | bytes 2097152 | tf_op jit(solution)/shard_map/all_to_all | solution.py:27
  42.7 11.1 %copy-start.4 = (bf16[128,8,512]{0,2,1:T(8,128)(2,1)}, bf16[128,8,512]{0,2,1:T(8,128)(2,1)S(1)}, u32[]{:S(2)}) copy-start(bf16[128,8,512]{0,2,1:T(8,128)(2,1)S(1)} %all-to-all-done) | copy-start | bytes 3145732
  42.7 29.9 %all-to-all-start.2 = ((bf16[128,8,512]{0,2,1:T(8,128)(2,1)}), bf16[128,8,512]{0,2,1:T(8,128)(2,1)}, u32[]{:S(2)}, u32[]{:S(2)}) async-start(bf16[128,8,512]{0,2,1:T(8,128)(2,1)} %bitcast.6), calls=%async_computation.2 | async-start | bytes 2097152 | tf_op jit(solution)/shard_map/all_to_all | solution.py:30
  46.9 14.4 %collective-permute-start = (bf16[1024,128]{1,0:T(8,128)(2,1)S(1)}, bf16[1024,128]{1,0:T(8,128)(2,1)S(1)}, u32[]{:S(2)}, u32[]{:S(2)}) collective-permute-start(bf16[1024,128]{1,0:T(8,128)(2,1)S(1)} %bitcast.139), channel_id=1, source_target_pairs={{0,8},{8,16},{16,24},{24,32},{32,40},{40,48},{48,56},{56,64},{64,7... | collective-permute-start | bytes 786440 | tf_op jit(solution)/shard_map/ppermute | solution.py:19
  48.9 18.4 %collective-permute-start.1 = (bf16[1024,128]{1,0:T(8,128)(2,1)S(1)}, bf16[1024,128]{1,0:T(8,128)(2,1)S(1)}, u32[]{:S(2)}, u32[]{:S(2)}) collective-permute-start(bf16[1024,128]{1,0:T(8,128)(2,1)S(1)} %bitcast.141), channel_id=1, source_target_pairs={{0,8},{8,16},{16,24},{24,32},{32,40},{40,48},{48,56},{56,64},{64,7... | collective-permute-start | bytes 786440 | tf_op jit(solution)/shard_map/ppermute | solution.py:19
  53.8 23.9 %dynamic-slice-start = ((s32[32768]{0:T(1024)}, s32[]{:T(128)}), s32[1024]{0:T(1024)S(1)}, s32[]{:S(2)}) async-start(s32[32768]{0:T(1024)} %param.11, s32[]{:T(128)} %select_n.17), calls=%async_computation.8 | async-start | bytes 8704 | tf_op jit(solution)/shard_map/dynamic_slice | solution.py:51
  86.1 6.0 %copy-start.3 = (bf16[4,1024,128]{1,2,0:T(8,128)(2,1)S(1)}, bf16[4,1024,128]{1,2,0:T(8,128)(2,1)}, u32[]{:S(2)}) copy-start(bf16[4,1024,128]{1,2,0:T(8,128)(2,1)} %get-tuple-element.353) | copy-start | bytes 3145732 | tf_op jit(solution)/shard_map/while/body/eval_jaxpr/while
  98.0 8.9 %copy-start.2 = (bf16[1024,2048]{1,0:T(8,128)(2,1)S(1)}, bf16[1024,2048]{1,0:T(8,128)(2,1)}, u32[]{:S(2)}) copy-start(bf16[1024,2048]{1,0:T(8,128)(2,1)} %copy-done.1) | copy-start | bytes 12582916 | tf_op jit(solution)/shard_map/while/body/eval_jaxpr/while
  117.7 6.0 %copy-start.3 = (bf16[4,1024,128]{1,2,0:T(8,128)(2,1)S(1)}, bf16[4,1024,128]{1,2,0:T(8,128)(2,1)}, u32[]{:S(2)}) copy-start(bf16[4,1024,128]{1,2,0:T(8,128)(2,1)} %get-tuple-element.353) | copy-start | bytes 3145732 | tf_op jit(solution)/shard_map/while/body/eval_jaxpr/while
  129.6 8.9 %copy-start.2 = (bf16[1024,2048]{1,0:T(8,128)(2,1)S(1)}, bf16[1024,2048]{1,0:T(8,128)(2,1)}, u32[]{:S(2)}) copy-start(bf16[1024,2048]{1,0:T(8,128)(2,1)} %copy-done.1) | copy-start | bytes 12582916 | tf_op jit(solution)/shard_map/while/body/eval_jaxpr/while
  149.4 6.0 %copy-start.3 = (bf16[4,1024,128]{1,2,0:T(8,128)(2,1)S(1)}, bf16[4,1024,128]{1,2,0:T(8,128)(2,1)}, u32[]{:S(2)}) copy-start(bf16[4,1024,128]{1,2,0:T(8,128)(2,1)} %get-tuple-element.353) | copy-start | bytes 3145732 | tf_op jit(solution)/shard_map/while/body/eval_jaxpr/while
  161.3 8.9 %copy-start.2 = (bf16[1024,2048]{1,0:T(8,128)(2,1)S(1)}, bf16[1024,2048]{1,0:T(8,128)(2,1)}, u32[]{:S(2)}) copy-start(bf16[1024,2048]{1,0:T(8,128)(2,1)} %copy-done.1) | copy-start | bytes 12582916 | tf_op jit(solution)/shard_map/while/body/eval_jaxpr/while
  193.0 8.9 %copy-start.2 = (bf16[1024,2048]{1,0:T(8,128)(2,1)S(1)}, bf16[1024,2048]{1,0:T(8,128)(2,1)}, u32[]{:S(2)}) copy-start(bf16[1024,2048]{1,0:T(8,128)(2,1)} %copy-done.1) | copy-start | bytes 12582916 | tf_op jit(solution)/shard_map/while/body/eval_jaxpr/while
  204.5 35.9 %copy-start.5 = (bf16[4,1024,128]{2,1,0:T(8,128)(2,1)S(1)}, bf16[4,1024,128]{2,1,0:T(8,128)(2,1)}, u32[]{:S(2)}) copy-start(bf16[4,1024,128]{2,1,0:T(8,128)(2,1)} %get-tuple-element.90) | copy-start | bytes 3145732
  204.6 8.7 %collective-permute-start.3 = (f32[1,1024,128]{2,1,0:T(8,128)S(1)}, f32[1,1024,128]{2,1,0:T(8,128)S(1)}, u32[]{:S(2)}, u32[]{:S(2)}) collective-permute-start(f32[1,1024,128]{2,1,0:T(8,128)S(1)} %slice.19), channel_id=1, source_target_pairs={{8,0},{16,8},{24,16},{32,24},{40,32},{48,40},{56,48},{64,56},{72,6... | collective-permute-start | bytes 1572872 | tf_op jit(solution)/shard_map/ppermute | solution.py:19
  207.5 11.6 %collective-permute-start.2 = (f32[1,1024,128]{2,1,0:T(8,128)}, f32[1,1024,128]{2,1,0:T(8,128)}, u32[]{:S(2)}, u32[]{:S(2)}) collective-permute-start(f32[1,1024,128]{2,1,0:T(8,128)} %slice.17), channel_id=1, source_target_pairs={{8,0},{16,8},{24,16},{32,24},{40,32},{48,40},{56,48},{64,56},{72,6... | collective-permute-start | bytes 1572872 | tf_op jit(solution)/shard_map/ppermute | solution.py:19
  214.1 10.8 %all-to-all-start.7 = ((bf16[8,128,128]{2,1,0:T(8,128)(2,1)}), bf16[8,128,128]{2,1,0:T(8,128)(2,1)S(1)}, u32[]{:S(2)}, u32[]{:S(2)}) async-start(bf16[8,128,128]{2,1,0:T(8,128)(2,1)} %bitcast.25), calls=%async_computation.7 | async-start | bytes 524288 | tf_op jit(solution)/shard_map/all_to_all | solution.py:108
  224.9 15.5 %copy-start.6 = (bf16[8,128,128]{2,1,0:T(8,128)(2,1)}, bf16[8,128,128]{2,1,0:T(8,128)(2,1)S(1)}, u32[]{:S(2)}) copy-start(bf16[8,128,128]{2,1,0:T(8,128)(2,1)S(1)} %all-to-all-done.7) | copy-start | bytes 786436
  224.9 11.9 %all-to-all-start.6 = ((bf16[8,128,128]{2,1,0:T(8,128)(2,1)}), bf16[8,128,128]{2,1,0:T(8,128)(2,1)S(1)}, u32[]{:S(2)}, u32[]{:S(2)}) async-start(bf16[8,128,128]{2,1,0:T(8,128)(2,1)} %bitcast.21), calls=%async_computation.6 | async-start | bytes 524288 | tf_op jit(solution)/shard_map/all_to_all | solution.py:107
  236.8 19.8 %all-to-all-start.4 = ((bf16[8,128,512]{2,1,0:T(8,128)(2,1)}), bf16[8,128,512]{2,1,0:T(8,128)(2,1)S(1)}, u32[]{:S(2)}, u32[]{:S(2)}) async-start(bf16[8,128,512]{2,1,0:T(8,128)(2,1)} %copy.67), calls=%async_computation.4 | async-start | bytes 2097152 | tf_op jit(solution)/shard_map/all_to_all | solution.py:105
  256.6 19.4 %all-to-all-start.5 = ((bf16[8,128,512]{1,2,0:T(8,128)(2,1)}), bf16[8,128,512]{1,2,0:T(8,128)(2,1)S(1)}, u32[]{:S(2)}, u32[]{:S(2)}) async-start(bf16[8,128,512]{1,2,0:T(8,128)(2,1)} %copy.60), calls=%async_computation.5 | async-start | bytes 2097152 | tf_op jit(solution)/shard_map/all_to_all | solution.py:106
  (7 other events, 18.3 us)
where the time goes:
time: 279 us; the launch traced here: 277 us
  matrix products  82.1 us (29%)
  waiting for transfers between devices  72.2 us (26%)
  other arithmetic  43.2 us (15%)
  starting transfers between devices  42.5 us (15%)
  local copies, waits for them, and re-layouts  35.8 us (13%)
    convert_element_type x4, other arithmetic, one_head(): jnp.where(allowed, jnp.exp(scores - log_total), 0.0).astype(jnp.bfloat16)  23.8 us
    dot_general x4, matrix products, one_head(): jnp.dot(query_head, key_group.T, preferred_element_type=jnp.float32)  17.5 us
    dot_general x4, matrix products, one_head(): jnp.dot(grad_scores, key_group, preferred_element_type=jnp.float32)  17 us
    ppermute x4, waiting for transfers between devices, shifted(): lax.ppermute(value, axis, [(source, source + steps) for source in range(l...  16.8 us
    dot_general x4, matrix products, one_head(): jnp.dot(grad_head, value_group.T, preferred_element_type=jnp.float32)  16 us
    reduce_sum x4, other arithmetic, one_head(): log_total = row_top + jnp.log(jnp.sum(kept_terms, axis=1, keepdims=True))  16 us
    dot_general x4, matrix products, one_head(): jnp.dot(grad_scores.T, query_head, preferred_element_type=jnp.float32)  15.5 us
    all_to_all x1, waiting for transfers between devices, shards(): lax.all_to_all(output_local, 'head', split_axis=0, concat_axis=1, tiled=T...  14.2 us
  transfers between devices with their start and end apart: 12, of which 11 were waited for; matrix products, arithmetic and copies ran while one was open for 10% of the time, Pallas kernels for 0%

commit v1 on v0

v1 whole, which is shorter than its diff:
```python
import functools
import math

import jax
import jax.numpy as jnp
from jax import lax
from jax.experimental import pallas as pl
from jax.experimental.pallas import tpu as pltpu
from jax.sharding import PartitionSpec as P

HEAD_DIM = 128
WINDOW = 1024
RING = 4
TOK = 128
ROWS = RING * TOK
GROUP = 4
KV = 2
HALF = GROUP * HEAD_DIM
EXT = ROWS + WINDOW
SCALE = 1.0 / math.sqrt(HEAD_DIM)
LOG2E = math.log2(math.e)
BIG = 16384.0
BF = jnp.bfloat16
F32 = jnp.float32
NT = (((1,), (1,)), ((), ()))
TN = (((0,), (0,)), ((), ()))


def attend(g, pos_ref, qseg_ref, kseg_ref, *refs):
    qin, (kvo, kv1, kv2) = refs[:4], refs[4:7]
    outs, (dko, dk1, dk2) = refs[7:11], refs[11:14]
    kx, vx, acck, accv, qs, dos, res, qn, gn, dots, invs, s_scr, p_scr, d_scr = refs[14:]

    for src, base in ((kv2, 0), (kv1, ROWS), (kvo, 2 * ROWS)):
        for d in range(RING):
            row = pl.ds(pl.multiple_of(base + TOK * pos_ref[d], TOK), TOK)
            kx[row, :HEAD_DIM] = src[TOK * d : TOK * (d + 1), HEAD_DIM * g : HEAD_DIM * (g + 1)]
            vx[row, :HEAD_DIM] = src[
                TOK * d : TOK * (d + 1), HEAD_DIM * (KV + g) : HEAD_DIM * (KV + g + 1)
            ]
    kx[:, HEAD_DIM:] = kseg_ref[...]
    vx[:, HEAD_DIM:] = jnp.ones((EXT, HEAD_DIM), BF)
    acck[...] = jnp.zeros_like(acck)
    accv[...] = jnp.zeros_like(accv)
    for d in range(RING):
        seg = qseg_ref[pl.ds(pl.multiple_of(TOK * pos_ref[d], TOK), TOK)]
        for j in range(GROUP):
            sl = slice(TOK * j, TOK * (j + 1))
            qs[d, sl, :HEAD_DIM] = qin[d][:, HEAD_DIM * j : HEAD_DIM * (j + 1)]
            qs[d, sl, HEAD_DIM:] = seg
            dos[d, sl] = qin[d][:, HALF + HEAD_DIM * j : HALF + HEAD_DIM * (j + 1)]

    row_id = lax.broadcasted_iota(jnp.int32, (TOK, TOK), 0)
    col_id = lax.broadcasted_iota(jnp.int32, (TOK, TOK), 1)
    lower = col_id <= row_id

    def step(d, carry):
        start = pl.multiple_of(TOK * pos_ref[d], TOK)
        span = pl.ds(start, WINDOW + TOK)
        s_scr[...] = lax.dot_general(qs[d], kx[span], NT, preferred_element_type=F32)
        for j in range(GROUP):
            sl = slice(TOK * j, TOK * (j + 1))
            edge = jnp.where(lower, s_scr[sl, WINDOW:], s_scr[sl, :TOK])
            body = s_scr[sl, TOK:WINDOW]
            top = jnp.maximum(
                jnp.max(edge, axis=1, keepdims=True), jnp.max(body, axis=1, keepdims=True)
            )
            edge = jnp.exp2((edge - top) * (SCALE * LOG2E))
            p_scr[sl, :TOK] = jnp.where(lower, 0.0, edge).astype(BF)
            p_scr[sl, WINDOW:] = jnp.where(lower, edge, 0.0).astype(BF)
            p_scr[sl, TOK:WINDOW] = jnp.exp2((body - top) * (SCALE * LOG2E)).astype(BF)
        for j in range(0, ROWS, 256):
            sl = slice(j, j + 256)
            out = jnp.dot(p_scr[sl], vx[span], preferred_element_type=F32)
            inv = 1.0 / out[:, HEAD_DIM:]
            attn = (out[:, :HEAD_DIM] * inv).astype(BF)
            res[d, sl, :HEAD_DIM] = attn
            grad = dos[d, sl].astype(F32)
            dots[sl] = jnp.sum(grad * attn.astype(F32), axis=1, keepdims=True)
            invs[sl] = inv * SCALE
            qn[sl] = (qs[d, sl, :HEAD_DIM].astype(F32) * (inv * SCALE)).astype(BF)
            gn[sl] = (grad * inv).astype(BF)
        d_scr[...] = (
            (lax.dot_general(dos[d], vx[span, :HEAD_DIM], NT, preferred_element_type=F32) - dots[...])
            * p_scr[...].astype(F32)
        ).astype(BF)
        for j in range(0, ROWS, 256):
            sl = slice(j, j + 256)
            dq = jnp.dot(d_scr[sl], kx[span, :HEAD_DIM], preferred_element_type=F32)
            res[d, sl, HEAD_DIM:] = (dq * invs[sl]).astype(BF)
        acck[:, span] += lax.dot_general(qn[...], d_scr[...], TN, preferred_element_type=F32)
        accv[:, span] += lax.dot_general(gn[...], p_scr[...], TN, preferred_element_type=F32)
        return carry

    lax.fori_loop(0, RING, step, 0)

    for d in range(RING):
        for j in range(GROUP):
            sl = slice(TOK * j, TOK * (j + 1))
            outs[d][:, HEAD_DIM * j : HEAD_DIM * (j + 1)] = res[d, sl, :HEAD_DIM]
            outs[d][:, HALF + HEAD_DIM * j : HALF + HEAD_DIM * (j + 1)] = res[d, sl, HEAD_DIM:]
    for dst, base in ((dk2, 0), (dk1, ROWS), (dko, 2 * ROWS)):
        for d in range(RING):
            row = pl.ds(pl.multiple_of(base + TOK * pos_ref[d], TOK), TOK)
            sl = slice(TOK * d, TOK * (d + 1))
            dst[sl, :HEAD_DIM] = acck[:, row].T.astype(dst.dtype)
            dst[sl, HEAD_DIM:] = accv[:, row].T.astype(dst.dtype)


def call(body, name, shapes, args, scratch=(), flops=0, limit=60):
    vm = pl.BlockSpec(memory_space=pltpu.VMEM)
    sm = pl.BlockSpec(memory_space=pltpu.SMEM)
    return list(
        pl.pallas_call(
            body,
            out_shape=[jax.ShapeDtypeStruct(shape, dtype) for shape, dtype in shapes],
            in_specs=[sm if arg.ndim == 1 else vm for arg in args],
            out_specs=[vm] * len(shapes),
            scratch_shapes=[pltpu.VMEM(shape, dtype) for shape, dtype in scratch],
            compiler_params=pltpu.CompilerParams(vmem_limit_bytes=limit * 1024 * 1024),
            cost_estimate=pl.CostEstimate(
                flops=flops, bytes_accessed=4 * 1024 * 1024, transcendentals=0
            ),
            name=name,
        )(*args)
    )


def attend_call(g, pos, qseg, kseg, qin, kvs):
    return call(
        functools.partial(attend, g),
        "attend",
        [((TOK, 2 * HALF), BF)] * RING
        + [((ROWS, 2 * HEAD_DIM), F32)]
        + [((ROWS, 2 * HEAD_DIM), BF)] * 2,
        (pos, qseg, kseg, *qin, *kvs),
        [
            ((EXT, 2 * HEAD_DIM), BF),
            ((EXT, 2 * HEAD_DIM), BF),
            ((HEAD_DIM, EXT), F32),
            ((HEAD_DIM, EXT), F32),
            ((RING, ROWS, 2 * HEAD_DIM), BF),
            ((RING, ROWS, HEAD_DIM), BF),
            ((RING, ROWS, 2 * HEAD_DIM), BF),
            ((ROWS, HEAD_DIM), BF),
            ((ROWS, HEAD_DIM), BF),
            ((ROWS, 1), F32),
            ((ROWS, HEAD_DIM), F32),
            ((ROWS, WINDOW + TOK), F32),
            ((ROWS, WINDOW + TOK), BF),
            ((ROWS, WINDOW + TOK), BF),
        ],
        flops=6 * 2 * 4 * ROWS * 1152 * 256,
        limit=60,
    )


def ring_slice(here_ref, steps, width):
    at = lax.rem(here_ref[0] + (steps + RING), RING)
    return pl.ds(pl.multiple_of(at * width, width), width)


def pack_kv(here_ref, k_ref, v_ref, *outs):
    width = KV * HEAD_DIM
    for d in range(RING):
        cols = ring_slice(here_ref, d, width)
        outs[d][:, :width] = k_ref[:, cols]
        outs[d][:, width:] = v_ref[:, cols]


def pack_q(here_ref, q_ref, d_ref, *outs):
    for d in range(RING):
        cols = ring_slice(here_ref, d, KV * HALF)
        for ref, base in ((q_ref, 0), (d_ref, HALF)):
            value = ref[:, cols]
            for g in range(KV):
                outs[g * RING + d][:, base : base + HALF] = value[:, g * HALF : (g + 1) * HALF]


def add_kv(own0, one0, two0, own1, one1, two1, *outs):
    for g, (own, one, two) in enumerate(((own0, one0, two0), (own1, one1, two1))):
        for d in range(RING):
            rows = slice(TOK * d, TOK * (d + 1))
            total = own[rows] + one[rows].astype(F32) + two[rows].astype(F32)
            outs[d][:, 2 * HEAD_DIM * g : 2 * HEAD_DIM * (g + 1)] = total.astype(BF)


def assemble(here_ref, *refs):
    parts, kvs, (attn, gq, gk, gv) = refs[: 2 * RING], refs[2 * RING : 3 * RING], refs[3 * RING :]
    for d in range(RING):
        wide = ring_slice(here_ref, d, KV * HALF)
        thin = ring_slice(here_ref, d, KV * HEAD_DIM)
        for ref, base in ((attn, 0), (gq, HALF)):
            ref[:, wide] = jnp.concatenate(
                [parts[g * RING + d][:, base : base + HALF] for g in range(KV)], axis=1
            )
        for ref, base in ((gk, 0), (gv, HEAD_DIM)):
            ref[:, thin] = jnp.concatenate(
                [
                    kvs[d][:, base + 2 * HEAD_DIM * g : base + 2 * HEAD_DIM * g + HEAD_DIM]
                    for g in range(KV)
                ],
                axis=1,
            )


def shards(queries, key_states, value_states, grad_output, segment_ids):
    heads = lax.axis_size("head")
    halves = lax.axis_size("blk") * heads // RING
    head = lax.axis_index("head")
    index = head % RING
    here = jnp.full((1,), index, jnp.int32)
    half = (lax.axis_index("blk") * heads + head) // RING

    def along_ring(value, steps):
        pairs = [(i, i // RING * RING + (i + steps) % RING) for i in range(heads)]
        return lax.ppermute(value, "head", pairs)

    def along_halves(value, steps):
        pairs = [
            (i * RING + x, (i + steps) * RING + x)
            for i in range(max(0, -steps), min(halves, halves - steps))
            for x in range(RING)
        ]
        return lax.ppermute(value, ("blk", "head"), pairs)

    def around(parts, sign):
        return parts[:1] + [along_ring(parts[d], sign * d) for d in range(1, RING)]

    thin_part, wide_part = ((TOK, 2 * KV * HEAD_DIM), BF), ((TOK, 2 * HALF), BF)
    kv = call(pack_kv, "pack_kv", [thin_part] * RING, (here, key_states, value_states))
    packed = call(pack_q, "pack_q", [wide_part] * (KV * RING), (here, queries, grad_output))
    kv_own = jnp.concatenate(around(kv, 1), axis=0)
    kv_own, packed = lax.optimization_barrier((kv_own, packed))
    kvs = (kv_own, along_halves(kv_own, 1), along_halves(kv_own, 2))
    first, second = around(packed[:RING], 1), packed[RING:]
    first, second = lax.optimization_barrier((first, second))
    q_parts = (first, around(second, 1))

    padded = jnp.concatenate([jnp.full((WINDOW,), HEAD_DIM - 1, jnp.int32), segment_ids])
    key_seg = lax.dynamic_slice_in_dim(padded, half * ROWS, EXT)
    lanes = jnp.arange(HEAD_DIM, dtype=jnp.int32)[None, :]
    kseg = (key_seg[:, None] == lanes).astype(BF)
    qseg = jnp.where(key_seg[WINDOW:, None] == lanes, 0.0, -BIG).astype(BF)
    steps = jnp.arange(RING, dtype=jnp.int32)
    pos = (index - steps) % RING

    wide, thin = [], []
    for g in range(KV):
        res = attend_call(g, pos, qseg, kseg, q_parts[g], kvs)
        if g > 0:
            res, wide, thin = lax.optimization_barrier((res, wide, thin))
        thin += [res[4], along_halves(res[5], -1), along_halves(res[6], -2)]
        wide += around(res[:RING], -1)
    grads = around(call(add_kv, "add_kv", [thin_part] * RING, thin), -1)
    width = RING * KV * HALF
    return tuple(
        call(
            assemble,
            "assemble",
            [((TOK, width), BF)] * 2 + [((TOK, width // GROUP), BF)] * 2,
            (here, *wide, *grads),
        )
    )


def solution(mesh):
    placed = P(("blk", "head"), None)
    return jax.shard_map(
        shards,
        mesh=mesh,
        in_specs=(placed, placed, placed, placed, P()),
        out_specs=(placed, placed, placed, placed),
        check_vma=False,
    )
```

time: 279 us -> 116 us (0.42)
  matrix products: 82.1 us -> 0 us
  waiting for transfers between devices: 72.2 us -> 24.7 us
  other arithmetic: 43.2 us -> 2.37 us
  Pallas kernels: 0 us -> 37.9 us
  local copies, waits for them, and re-layouts: 35.8 us -> 3.81 us
  starting transfers between devices: 42.5 us -> 46.1 us
    dot_general x24 -> x0, matrix products: 82.1 us -> none  [the longest x4 17.5 us: one_head(): jnp.dot(query_head, key_group.T, preferred_element_type=jnp.float32)]
    all_to_all x8 -> x0, waiting for transfers between devices: 55.4 us -> none  [the longest x1 14.2 us: shards(): lax.all_to_all(output_local, 'head', split_axis=0, concat_axis=1, tiled=T...]
    pallas_call x0 -> x6, Pallas kernels: none -> 37.9 us  [call(): pl.pallas_call(body, out_shape=[jax.ShapeDtypeStruct(shape, dtype) for sh...]
    ppermute x4 -> x24, starting transfers between devices: 12 us -> 46.1 us  [the longest x18 27.8 us: along_ring(): return lax.ppermute(value, 'head', pairs)]
    all_to_all x8 -> x0, starting transfers between devices: 30.5 us -> none  [the longest x1 5.31 us: shards(): lax.all_to_all(key_states, 'head', split_axis=1, concat_axis=0, tiled=True)]
    convert_element_type x6 -> x2, other arithmetic: 26.3 us -> 1.81 us  [the longest x1 1.02 us: shards(): kseg = (key_seg[:, None] == lanes).astype(BF)]
    reduce_sum x4 -> x0, other arithmetic: 16 us -> none  [one_head(): log_total = row_top + jnp.log(jnp.sum(kept_terms, axis=1, keepdims=True))]
    all_to_all x9 -> x0, local copies, waits for them, and re-layouts: 13.7 us -> none  [the longest x1 2.87 us: shards(): lax.all_to_all(grad_output, 'head', split_axis=1, concat_axis=0, tiled=True)]
  transfers between devices with their start and end apart: 12 -> 24, of which waited for: 11 -> 10; matrix products, arithmetic and copies ran while one was open for 10% -> 2% of each run, Pallas kernels for 0% -> 28%
where the time goes in v1:
time: 116 us
  starting transfers between devices  46.1 us (40%)
  Pallas kernels  37.9 us (33%)
  waiting for transfers between devices  24.7 us (21%)
  local copies, waits for them, and re-layouts  3.81 us (3%)
  other arithmetic  2.37 us (2%)
    pallas_call x6, Pallas kernels, call(): pl.pallas_call(body, out_shape=[jax.ShapeDtypeStruct(shape, dtype) for sh...  37.9 us
    ppermute x18, starting transfers between devices, along_ring(): return lax.ppermute(value, 'head', pairs)  27.8 us
    ppermute x18, waiting for transfers between devices, along_ring(): return lax.ppermute(value, 'head', pairs)  23.2 us
    ppermute x6, starting transfers between devices, along_halves(): return lax.ppermute(value, ('blk', 'head'), pairs)  18.3 us
    unnamed x60, local copies, waits for them, and re-layouts  3.66 us
  transfers between devices with their start and end apart: 24, of which 10 were waited for; matrix products, arithmetic and copies ran while one was open for 2% of the time, Pallas kernels for 28%

profile of v1, /device:TPU:160, one launch (start us, length us, event | category | flops | bytes accessed | tf_op | source)
XLA Modules:
  0.0 115.8 jit_solution(17944545586521989216)
XLA Ops:
  4.0 2.7 %collective-permute-start.1 = (bf16[128,512]{1,0:T(8,128)(2,1)}, bf16[128,512]{1,0:T(8,128)(2,1)S(1)}, u32[]{:S(2)}, u32[]{:S(2)}) collective-permute-start(bf16[128,512]{1,0:T(8,128)(2,1)} %get-tuple-element.67), channel_id=1, source_target_pairs={{0,2},{1,3},{2,0},{3,1},{4,6},{5,7},{6,4},{7,5},{8,10},{9,11},{10,... | collective-permute-start | bytes 393224 | tf_op jit(solution)/shard_map/ppermute | solution.py:217
  8.2 3.0 %pack_q.1 = (bf16[128,1024]{1,0:T(8,128)(2,1)}, bf16[128,1024]{1,0:T(8,128)(2,1)}, bf16[128,1024]{1,0:T(8,128)(2,1)}, bf16[128,1024]{1,0:T(8,128)(2,1)}, bf16[12...) custom-call(s32[1]{0:T(128)} %bitcast.here_ref, ...), custom_call_target="tpu_custom_call" | custom-call | bytes 4194304 | tf_op jit(solution)/shard_map/pack_q/pallas_call | solution.py:114
  13.1 2.1 %collective-permute-start.10 = (bf16[512,512]{1,0:T(8,128)(2,1)S(1)}, bf16[512,512]{1,0:T(8,128)(2,1)S(1)}, u32[]{:S(2)}, u32[]{:S(2)}) collective-permute-start(bf16[512,512]{1,0:T(8,128)(2,1)S(1)} %pad_maximum_fusion.refs_4_), channel_id=1, source_target_pairs={{0,8},{1,9},{2,10},{3,11},{4,12},{5,13},{6,14},{7,15},{8,16},{9,17... | collective-permute-start | bytes 1572872 | tf_op jit(solution)/shard_map/ppermute | solution.py:225
  15.1 3.5 %collective-permute-start.9 = (bf16[512,512]{1,0:T(8,128)(2,1)S(1)}, bf16[512,512]{1,0:T(8,128)(2,1)S(1)}, u32[]{:S(2)}, u32[]{:S(2)}) collective-permute-start(bf16[512,512]{1,0:T(8,128)(2,1)S(1)} %pad_maximum_fusion.refs_4_), channel_id=1, source_target_pairs={{0,4},{1,5},{2,6},{3,7},{4,8},{5,9},{6,10},{7,11},{8,12},{9,13},{1... | collective-permute-start | bytes 1572872 | tf_op jit(solution)/shard_map/ppermute | solution.py:225
  21.1 2.4 %collective-permute-start.4 = (bf16[128,1024]{1,0:T(8,128)(2,1)S(1)}, bf16[128,1024]{1,0:T(8,128)(2,1)S(1)}, u32[]{:S(2)}, u32[]{:S(2)}) collective-permute-start(bf16[128,1024]{1,0:T(8,128)(2,1)S(1)} %copy-done.25), channel_id=1, source_target_pairs={{0,2},{1,3},{2,0},{3,1},{4,6},{5,7},{6,4},{7,5},{8,10},{9,11},{10,... | collective-permute-start | bytes 786440 | tf_op jit(solution)/shard_map/ppermute | solution.py:217
  26.4 2.6 %collective-permute-done.3.refs_1_ = bf16[128,1024]{1,0:T(8,128)(2,1)S(1)} collective-permute-done((bf16[128,1024]{1,0:T(8,128)(2,1)S(1)}, bf16[128,1024]{1,0:T(8,128)(2,1)S(1)}, u32[]{:S(2)}, u32[]{:S(2)}) %collective-permute-start.3) | collective-permute-done | bytes 262176 | tf_op jit(solution)/shard_map/ppermute | solution.py:217
  29.0 6.1 %collective-permute-done.4.refs_2_ = bf16[128,1024]{1,0:T(8,128)(2,1)S(1)} collective-permute-done((bf16[128,1024]{1,0:T(8,128)(2,1)S(1)}, bf16[128,1024]{1,0:T(8,128)(2,1)S(1)}, u32[]{:S(2)}, u32[]{:S(2)}) %collective-permute-start.4) | collective-permute-done | bytes 262176 | tf_op jit(solution)/shard_map/ppermute | solution.py:217
  35.8 2.7 %collective-permute-start.6 = (bf16[128,1024]{1,0:T(8,128)(2,1)S(1)}, bf16[128,1024]{1,0:T(8,128)(2,1)S(1)}, u32[]{:S(2)}, u32[]{:S(2)}) collective-permute-start(bf16[128,1024]{1,0:T(8,128)(2,1)S(1)} %copy-done.20), channel_id=1, source_target_pairs={{0,1},{1,2},{2,3},{3,0},{4,5},{5,6},{6,7},{7,4},{8,9},{9,10},{10,1... | collective-permute-start | bytes 786440 | tf_op jit(solution)/shard_map/ppermute | solution.py:217
  38.6 2.2 %collective-permute-start.7 = (bf16[128,1024]{1,0:T(8,128)(2,1)S(1)}, bf16[128,1024]{1,0:T(8,128)(2,1)S(1)}, u32[]{:S(2)}, u32[]{:S(2)}) collective-permute-start(bf16[128,1024]{1,0:T(8,128)(2,1)S(1)} %copy-done.19), channel_id=1, source_target_pairs={{0,2},{1,3},{2,0},{3,1},{4,6},{5,7},{6,4},{7,5},{8,10},{9,11},{10,... | collective-permute-start | bytes 786440 | tf_op jit(solution)/shard_map/ppermute | solution.py:217
  42.9 13.6 %attend.3 = (bf16[128,1024]{1,0:T(8,128)(2,1)}, bf16[128,1024]{1,0:T(8,128)(2,1)}, bf16[128,1024]{1,0:T(8,128)(2,1)}, bf16[128,1024]{1,0:T(8,128)(2,1)}, f32[512...) custom-call(s32[4]{0:T(128)} %and_select_fusion.pos_ref, ...), custom_call_target="tpu_custom_call" | custom-call | flops 7247757312 | bytes 4194304 | tf_op jit(solution)/shard_map/attend/pallas_call | solution.py:114
  57.9 2.2 %collective-permute-start.12 = (bf16[128,1024]{1,0:T(8,128)(2,1)}, bf16[128,1024]{1,0:T(8,128)(2,1)S(1)}, u32[]{:S(2)}, u32[]{:S(2)}) collective-permute-start(bf16[128,1024]{1,0:T(8,128)(2,1)} %get-tuple-element.103), channel_id=1, source_target_pairs={{0,2},{1,3},{2,0},{3,1},{4,6},{5,7},{6,4},{7,5},{8,10},{9,11},{10,... | collective-permute-start | bytes 786440 | tf_op jit(solution)/shard_map/ppermute | solution.py:217
  60.1 2.6 %collective-permute-start.14 = (bf16[512,256]{1,0:T(8,128)(2,1)}, bf16[512,256]{1,0:T(8,128)(2,1)S(1)}, u32[]{:S(2)}, u32[]{:S(2)}) collective-permute-start(bf16[512,256]{1,0:T(8,128)(2,1)} %get-tuple-element.106), channel_id=1, source_target_pairs={{4,0},{5,1},{6,2},{7,3},{8,4},{9,5},{10,6},{11,7},{12,8},{13,9},{1... | collective-permute-start | bytes 786440 | tf_op jit(solution)/shard_map/ppermute | solution.py:225
  62.7 4.9 %collective-permute-start.15 = (bf16[512,256]{1,0:T(8,128)(2,1)}, bf16[512,256]{1,0:T(8,128)(2,1)S(1)}, u32[]{:S(2)}, u32[]{:S(2)}) collective-permute-start(bf16[512,256]{1,0:T(8,128)(2,1)} %get-tuple-element.107), channel_id=1, source_target_pairs={{8,0},{9,1},{10,2},{11,3},{12,4},{13,5},{14,6},{15,7},{16,8},{17,9... | collective-permute-start | bytes 786440 | tf_op jit(solution)/shard_map/ppermute | solution.py:225
  67.6 13.6 %attend.2 = (bf16[128,1024]{1,0:T(8,128)(2,1)}, bf16[128,1024]{1,0:T(8,128)(2,1)}, bf16[128,1024]{1,0:T(8,128)(2,1)}, bf16[128,1024]{1,0:T(8,128)(2,1)}, f32[512...) custom-call(s32[4]{0:T(128)} %and_select_fusion.pos_ref, ...), custom_call_target="tpu_custom_call" | custom-call | flops 7247757312 | bytes 4194304 | tf_op jit(solution)/shard_map/attend/pallas_call | solution.py:114
  81.4 2.3 %collective-permute-start.19 = (bf16[512,256]{1,0:T(8,128)(2,1)}, bf16[512,256]{1,0:T(8,128)(2,1)S(1)}, u32[]{:S(2)}, u32[]{:S(2)}) collective-permute-start(bf16[512,256]{1,0:T(8,128)(2,1)} %get-tuple-element.120), channel_id=1, source_target_pairs={{4,0},{5,1},{6,2},{7,3},{8,4},{9,5},{10,6},{11,7},{12,8},{13,9},{1... | collective-permute-start | bytes 786440 | tf_op jit(solution)/shard_map/ppermute | solution.py:225
  83.7 3.0 %collective-permute-start.20 = (bf16[512,256]{1,0:T(8,128)(2,1)}, bf16[512,256]{1,0:T(8,128)(2,1)S(1)}, u32[]{:S(2)}, u32[]{:S(2)}) collective-permute-start(bf16[512,256]{1,0:T(8,128)(2,1)} %get-tuple-element.121), channel_id=1, source_target_pairs={{8,0},{9,1},{10,2},{11,3},{12,4},{13,5},{14,6},{15,7},{16,8},{17,9... | collective-permute-start | bytes 786440 | tf_op jit(solution)/shard_map/ppermute | solution.py:225
  86.7 3.3 %collective-permute-start.16 = (bf16[128,1024]{1,0:T(8,128)(2,1)}, bf16[128,1024]{1,0:T(8,128)(2,1)S(1)}, u32[]{:S(2)}, u32[]{:S(2)}) collective-permute-start(bf16[128,1024]{1,0:T(8,128)(2,1)} %get-tuple-element.113), channel_id=1, source_target_pairs={{0,3},{1,0},{2,1},{3,2},{4,7},{5,4},{6,5},{7,6},{8,11},{9,8},{10,9... | collective-permute-start | bytes 786440 | tf_op jit(solution)/shard_map/ppermute | solution.py:217
  94.1 2.4 %add_kv.1 = (bf16[128,512]{1,0:T(8,128)(2,1)}, bf16[128,512]{1,0:T(8,128)(2,1)}, bf16[128,512]{1,0:T(8,128)(2,1)}, bf16[128,512]{1,0:T(8,128)(2,1)}) custom-call(f32[512,256]{1,0:T(8,128)} %get-tuple-element.116.own0, bf16[512,256]{1,0:T(8,128)(2,1)} %copy-done.5, bf16[512,256]{1,0:T(8,128)(2,1)} %copy-done.6, f32[512,256]{1,0:T(8,128)} %get-tuple-element.119.own1, ...), custom_call_target="tpu_custom_call" | custom-call | bytes 4194304 | tf_op jit(solution)/shard_map/add_kv/pallas_call | solution.py:114
  96.4 3.3 %collective-permute-start.21 = (bf16[128,512]{1,0:T(8,128)(2,1)}, bf16[128,512]{1,0:T(8,128)(2,1)S(1)}, u32[]{:S(2)}, u32[]{:S(2)}) collective-permute-start(bf16[128,512]{1,0:T(8,128)(2,1)} %get-tuple-element.123), channel_id=1, source_target_pairs={{0,3},{1,0},{2,1},{3,2},{4,7},{5,4},{6,5},{7,6},{8,11},{9,8},{10,9... | collective-permute-start | bytes 393224 | tf_op jit(solution)/shard_map/ppermute | solution.py:217
  99.8 3.7 %collective-permute-done.16.refs_5_ = bf16[128,1024]{1,0:T(8,128)(2,1)S(1)} collective-permute-done((bf16[128,1024]{1,0:T(8,128)(2,1)}, bf16[128,1024]{1,0:T(8,128)(2,1)S(1)}, u32[]{:S(2)}, u32[]{:S(2)}) %collective-permute-start.16) | collective-permute-done | bytes 262176 | tf_op jit(solution)/shard_map/ppermute | solution.py:217
  103.6 2.6 %collective-permute-done.18.refs_7_ = bf16[128,1024]{1,0:T(8,128)(2,1)S(1)} collective-permute-done((bf16[128,1024]{1,0:T(8,128)(2,1)}, bf16[128,1024]{1,0:T(8,128)(2,1)S(1)}, u32[]{:S(2)}, u32[]{:S(2)}) %collective-permute-start.18) | collective-permute-done | bytes 262176 | tf_op jit(solution)/shard_map/ppermute | solution.py:217
  106.7 2.2 %collective-permute-done.22.refs_10_ = bf16[128,512]{1,0:T(8,128)(2,1)S(1)} collective-permute-done((bf16[128,512]{1,0:T(8,128)(2,1)}, bf16[128,512]{1,0:T(8,128)(2,1)S(1)}, u32[]{:S(2)}, u32[]{:S(2)}) %collective-permute-start.22) | collective-permute-done | bytes 131104 | tf_op jit(solution)/shard_map/ppermute | solution.py:217
  108.9 3.0 %collective-permute-done.23.refs_11_ = bf16[128,512]{1,0:T(8,128)(2,1)S(1)} collective-permute-done((bf16[128,512]{1,0:T(8,128)(2,1)}, bf16[128,512]{1,0:T(8,128)(2,1)S(1)}, u32[]{:S(2)}, u32[]{:S(2)}) %collective-permute-start.23) | collective-permute-done | bytes 131104 | tf_op jit(solution)/shard_map/ppermute | solution.py:217
  112.5 3.3 %assemble.1 = (bf16[128,4096]{1,0:T(8,128)(2,1)}, bf16[128,4096]{1,0:T(8,128)(2,1)}, bf16[128,1024]{1,0:T(8,128)(2,1)}, bf16[128,1024]{1,0:T(8,128)(2,1)}) custom-call(s32[1]{0:T(128)} %bitcast.here_ref, bf16[128,1024]{1,0:T(8,128)(2,1)} %get-tuple-element.108.refs_0_, bf16[128,1024]{1,0:T(8,128)(2,1)} %copy-done.2, bf16[128,1024]{1,0:T(8,128)(2,1)} %copy-done.3, ...), custom_call_target="tpu_custom_call" | custom-call | bytes 4194304 | tf_op jit(solution)/shard_map/assemble/pallas_call | solution.py:114
  (96 shorter events, 21.5 us)
Async XLA Ops:
  2.5 8.8 %collective-permute-start = (bf16[128,512]{1,0:T(8,128)(2,1)}, bf16[128,512]{1,0:T(8,128)(2,1)S(1)}, u32[]{:S(2)}, u32[]{:S(2)}) collective-permute-start(bf16[128,512]{1,0:T(8,128)(2,1)} %get-tuple-element.66), channel_id=1, source_target_pairs={{0,1},{1,2},{2,3},{3,0},{4,5},{5,6},{6,7},{7,4},{8,9},{9,10},{10,1... | collective-permute-start | bytes 393224 | tf_op jit(solution)/shard_map/ppermute | solution.py:217
  4.0 9.0 %collective-permute-start.1 = (bf16[128,512]{1,0:T(8,128)(2,1)}, bf16[128,512]{1,0:T(8,128)(2,1)S(1)}, u32[]{:S(2)}, u32[]{:S(2)}) collective-permute-start(bf16[128,512]{1,0:T(8,128)(2,1)} %get-tuple-element.67), channel_id=1, source_target_pairs={{0,2},{1,3},{2,0},{3,1},{4,6},{5,7},{6,4},{7,5},{8,10},{9,11},{10,... | collective-permute-start | bytes 393224 | tf_op jit(solution)/shard_map/ppermute | solution.py:217
  6.7 6.2 %collective-permute-start.2 = (bf16[128,512]{1,0:T(8,128)(2,1)}, bf16[128,512]{1,0:T(8,128)(2,1)S(1)}, u32[]{:S(2)}, u32[]{:S(2)}) collective-permute-start(bf16[128,512]{1,0:T(8,128)(2,1)} %get-tuple-element.68), channel_id=1, source_target_pairs={{0,3},{1,0},{2,1},{3,2},{4,7},{5,4},{6,5},{7,6},{8,11},{9,8},{10,9... | collective-permute-start | bytes 393224 | tf_op jit(solution)/shard_map/ppermute | solution.py:217
  13.1 28.2 %collective-permute-start.10 = (bf16[512,512]{1,0:T(8,128)(2,1)S(1)}, bf16[512,512]{1,0:T(8,128)(2,1)S(1)}, u32[]{:S(2)}, u32[]{:S(2)}) collective-permute-start(bf16[512,512]{1,0:T(8,128)(2,1)S(1)} %pad_maximum_fusion.refs_4_), channel_id=1, source_target_pairs={{0,8},{1,9},{2,10},{3,11},{4,12},{5,13},{6,14},{7,15},{8,16},{9,17... | collective-permute-start | bytes 1572872 | tf_op jit(solution)/shard_map/ppermute | solution.py:225
  15.1 26.2 %collective-permute-start.9 = (bf16[512,512]{1,0:T(8,128)(2,1)S(1)}, bf16[512,512]{1,0:T(8,128)(2,1)S(1)}, u32[]{:S(2)}, u32[]{:S(2)}) collective-permute-start(bf16[512,512]{1,0:T(8,128)(2,1)S(1)} %pad_maximum_fusion.refs_4_), channel_id=1, source_target_pairs={{0,4},{1,5},{2,6},{3,7},{4,8},{5,9},{6,10},{7,11},{8,12},{9,13},{1... | collective-permute-start | bytes 1572872 | tf_op jit(solution)/shard_map/ppermute | solution.py:225
  19.7 9.2 %collective-permute-start.3 = (bf16[128,1024]{1,0:T(8,128)(2,1)S(1)}, bf16[128,1024]{1,0:T(8,128)(2,1)S(1)}, u32[]{:S(2)}, u32[]{:S(2)}) collective-permute-start(bf16[128,1024]{1,0:T(8,128)(2,1)S(1)} %copy-done.26), channel_id=1, source_target_pairs={{0,1},{1,2},{2,3},{3,0},{4,5},{5,6},{6,7},{7,4},{8,9},{9,10},{10,1... | collective-permute-start | bytes 786440 | tf_op jit(solution)/shard_map/ppermute | solution.py:217
  21.1 14.0 %collective-permute-start.4 = (bf16[128,1024]{1,0:T(8,128)(2,1)S(1)}, bf16[128,1024]{1,0:T(8,128)(2,1)S(1)}, u32[]{:S(2)}, u32[]{:S(2)}) collective-permute-start(bf16[128,1024]{1,0:T(8,128)(2,1)S(1)} %copy-done.25), channel_id=1, source_target_pairs={{0,2},{1,3},{2,0},{3,1},{4,6},{5,7},{6,4},{7,5},{8,10},{9,11},{10,... | collective-permute-start | bytes 786440 | tf_op jit(solution)/shard_map/ppermute | solution.py:217
  23.5 12.3 %collective-permute-start.5 = (bf16[128,1024]{1,0:T(8,128)(2,1)S(1)}, bf16[128,1024]{1,0:T(8,128)(2,1)S(1)}, u32[]{:S(2)}, u32[]{:S(2)}) collective-permute-start(bf16[128,1024]{1,0:T(8,128)(2,1)S(1)} %copy-done.23), channel_id=1, source_target_pairs={{0,3},{1,0},{2,1},{3,2},{4,7},{5,4},{6,5},{7,6},{8,11},{9,8},{10,9... | collective-permute-start | bytes 786440 | tf_op jit(solution)/shard_map/ppermute | solution.py:217
  35.8 24.2 %collective-permute-start.6 = (bf16[128,1024]{1,0:T(8,128)(2,1)S(1)}, bf16[128,1024]{1,0:T(8,128)(2,1)S(1)}, u32[]{:S(2)}, u32[]{:S(2)}) collective-permute-start(bf16[128,1024]{1,0:T(8,128)(2,1)S(1)} %copy-done.20), channel_id=1, source_target_pairs={{0,1},{1,2},{2,3},{3,0},{4,5},{5,6},{6,7},{7,4},{8,9},{9,10},{10,1... | collective-permute-start | bytes 786440 | tf_op jit(solution)/shard_map/ppermute | solution.py:217
  38.6 21.5 %collective-permute-start.7 = (bf16[128,1024]{1,0:T(8,128)(2,1)S(1)}, bf16[128,1024]{1,0:T(8,128)(2,1)S(1)}, u32[]{:S(2)}, u32[]{:S(2)}) collective-permute-start(bf16[128,1024]{1,0:T(8,128)(2,1)S(1)} %copy-done.19), channel_id=1, source_target_pairs={{0,2},{1,3},{2,0},{3,1},{4,6},{5,7},{6,4},{7,5},{8,10},{9,11},{10,... | collective-permute-start | bytes 786440 | tf_op jit(solution)/shard_map/ppermute | solution.py:217
  40.7 22.0 %collective-permute-start.8 = (bf16[128,1024]{1,0:T(8,128)(2,1)S(1)}, bf16[128,1024]{1,0:T(8,128)(2,1)S(1)}, u32[]{:S(2)}, u32[]{:S(2)}) collective-permute-start(bf16[128,1024]{1,0:T(8,128)(2,1)S(1)} %copy-done.18), channel_id=1, source_target_pairs={{0,3},{1,0},{2,1},{3,2},{4,7},{5,4},{6,5},{7,6},{8,11},{9,8},{10,9... | collective-permute-start | bytes 786440 | tf_op jit(solution)/shard_map/ppermute | solution.py:217
  56.6 24.7 %collective-permute-start.11 = (bf16[128,1024]{1,0:T(8,128)(2,1)}, bf16[128,1024]{1,0:T(8,128)(2,1)S(1)}, u32[]{:S(2)}, u32[]{:S(2)}) collective-permute-start(bf16[128,1024]{1,0:T(8,128)(2,1)} %get-tuple-element.102), channel_id=1, source_target_pairs={{0,3},{1,0},{2,1},{3,2},{4,7},{5,4},{6,5},{7,6},{8,11},{9,8},{10,9... | collective-permute-start | bytes 786440 | tf_op jit(solution)/shard_map/ppermute | solution.py:217
  57.9 23.4 %collective-permute-start.12 = (bf16[128,1024]{1,0:T(8,128)(2,1)}, bf16[128,1024]{1,0:T(8,128)(2,1)S(1)}, u32[]{:S(2)}, u32[]{:S(2)}) collective-permute-start(bf16[128,1024]{1,0:T(8,128)(2,1)} %get-tuple-element.103), channel_id=1, source_target_pairs={{0,2},{1,3},{2,0},{3,1},{4,6},{5,7},{6,4},{7,5},{8,10},{9,11},{10,... | collective-permute-start | bytes 786440 | tf_op jit(solution)/shard_map/ppermute | solution.py:217
  60.1 21.3 %collective-permute-start.13 = (bf16[128,1024]{1,0:T(8,128)(2,1)}, bf16[128,1024]{1,0:T(8,128)(2,1)S(1)}, u32[]{:S(2)}, u32[]{:S(2)}) collective-permute-start(bf16[128,1024]{1,0:T(8,128)(2,1)} %get-tuple-element.104), channel_id=1, source_target_pairs={{0,1},{1,2},{2,3},{3,0},{4,5},{5,6},{6,7},{7,4},{8,9},{9,10},{10,1... | collective-permute-start | bytes 786440 | tf_op jit(solution)/shard_map/ppermute | solution.py:217
  60.1 21.2 %collective-permute-start.14 = (bf16[512,256]{1,0:T(8,128)(2,1)}, bf16[512,256]{1,0:T(8,128)(2,1)S(1)}, u32[]{:S(2)}, u32[]{:S(2)}) collective-permute-start(bf16[512,256]{1,0:T(8,128)(2,1)} %get-tuple-element.106), channel_id=1, source_target_pairs={{4,0},{5,1},{6,2},{7,3},{8,4},{9,5},{10,6},{11,7},{12,8},{13,9},{1... | collective-permute-start | bytes 786440 | tf_op jit(solution)/shard_map/ppermute | solution.py:225
  62.7 18.6 %collective-permute-start.15 = (bf16[512,256]{1,0:T(8,128)(2,1)}, bf16[512,256]{1,0:T(8,128)(2,1)S(1)}, u32[]{:S(2)}, u32[]{:S(2)}) collective-permute-start(bf16[512,256]{1,0:T(8,128)(2,1)} %get-tuple-element.107), channel_id=1, source_target_pairs={{8,0},{9,1},{10,2},{11,3},{12,4},{13,5},{14,6},{15,7},{16,8},{17,9... | collective-permute-start | bytes 786440 | tf_op jit(solution)/shard_map/ppermute | solution.py:225
  81.4 11.3 %collective-permute-start.19 = (bf16[512,256]{1,0:T(8,128)(2,1)}, bf16[512,256]{1,0:T(8,128)(2,1)S(1)}, u32[]{:S(2)}, u32[]{:S(2)}) collective-permute-start(bf16[512,256]{1,0:T(8,128)(2,1)} %get-tuple-element.120), channel_id=1, source_target_pairs={{4,0},{5,1},{6,2},{7,3},{8,4},{9,5},{10,6},{11,7},{12,8},{13,9},{1... | collective-permute-start | bytes 786440 | tf_op jit(solution)/shard_map/ppermute | solution.py:225
  83.7 9.0 %collective-permute-start.20 = (bf16[512,256]{1,0:T(8,128)(2,1)}, bf16[512,256]{1,0:T(8,128)(2,1)S(1)}, u32[]{:S(2)}, u32[]{:S(2)}) collective-permute-start(bf16[512,256]{1,0:T(8,128)(2,1)} %get-tuple-element.121), channel_id=1, source_target_pairs={{8,0},{9,1},{10,2},{11,3},{12,4},{13,5},{14,6},{15,7},{16,8},{17,9... | collective-permute-start | bytes 786440 | tf_op jit(solution)/shard_map/ppermute | solution.py:225
  86.7 16.9 %collective-permute-start.16 = (bf16[128,1024]{1,0:T(8,128)(2,1)}, bf16[128,1024]{1,0:T(8,128)(2,1)S(1)}, u32[]{:S(2)}, u32[]{:S(2)}) collective-permute-start(bf16[128,1024]{1,0:T(8,128)(2,1)} %get-tuple-element.113), channel_id=1, source_target_pairs={{0,3},{1,0},{2,1},{3,2},{4,7},{5,4},{6,5},{7,6},{8,11},{9,8},{10,9... | collective-permute-start | bytes 786440 | tf_op jit(solution)/shard_map/ppermute | solution.py:217
  90.0 13.6 %collective-permute-start.17 = (bf16[128,1024]{1,0:T(8,128)(2,1)}, bf16[128,1024]{1,0:T(8,128)(2,1)S(1)}, u32[]{:S(2)}, u32[]{:S(2)}) collective-permute-start(bf16[128,1024]{1,0:T(8,128)(2,1)} %get-tuple-element.114), channel_id=1, source_target_pairs={{0,2},{1,3},{2,0},{3,1},{4,6},{5,7},{6,4},{7,5},{8,10},{9,11},{10,... | collective-permute-start | bytes 786440 | tf_op jit(solution)/shard_map/ppermute | solution.py:217
  90.2 16.1 %collective-permute-start.18 = (bf16[128,1024]{1,0:T(8,128)(2,1)}, bf16[128,1024]{1,0:T(8,128)(2,1)S(1)}, u32[]{:S(2)}, u32[]{:S(2)}) collective-permute-start(bf16[128,1024]{1,0:T(8,128)(2,1)} %get-tuple-element.115), channel_id=1, source_target_pairs={{0,1},{1,2},{2,3},{3,0},{4,5},{5,6},{6,7},{7,4},{8,9},{9,10},{10,1... | collective-permute-start | bytes 786440 | tf_op jit(solution)/shard_map/ppermute | solution.py:217
  96.4 10.2 %collective-permute-start.21 = (bf16[128,512]{1,0:T(8,128)(2,1)}, bf16[128,512]{1,0:T(8,128)(2,1)S(1)}, u32[]{:S(2)}, u32[]{:S(2)}) collective-permute-start(bf16[128,512]{1,0:T(8,128)(2,1)} %get-tuple-element.123), channel_id=1, source_target_pairs={{0,3},{1,0},{2,1},{3,2},{4,7},{5,4},{6,5},{7,6},{8,11},{9,8},{10,9... | collective-permute-start | bytes 393224 | tf_op jit(solution)/shard_map/ppermute | solution.py:217
  99.7 9.2 %collective-permute-start.22 = (bf16[128,512]{1,0:T(8,128)(2,1)}, bf16[128,512]{1,0:T(8,128)(2,1)S(1)}, u32[]{:S(2)}, u32[]{:S(2)}) collective-permute-start(bf16[128,512]{1,0:T(8,128)(2,1)} %get-tuple-element.124), channel_id=1, source_target_pairs={{0,2},{1,3},{2,0},{3,1},{4,6},{5,7},{6,4},{7,5},{8,10},{9,11},{10,... | collective-permute-start | bytes 393224 | tf_op jit(solution)/shard_map/ppermute | solution.py:217
  103.6 8.3 %collective-permute-start.23 = (bf16[128,512]{1,0:T(8,128)(2,1)}, bf16[128,512]{1,0:T(8,128)(2,1)S(1)}, u32[]{:S(2)}, u32[]{:S(2)}) collective-permute-start(bf16[128,512]{1,0:T(8,128)(2,1)} %get-tuple-element.125), channel_id=1, source_target_pairs={{0,1},{1,2},{2,3},{3,0},{4,5},{5,6},{6,7},{7,4},{8,9},{9,10},{10,1... | collective-permute-start | bytes 393224 | tf_op jit(solution)/shard_map/ppermute | solution.py:217
  (30 other events, 280.7 us)

commit v2 on v1

--- a/solution.py
+++ b/solution.py
@@ -26,18 +26,17 @@
 TN = (((0,), (0,)), ((), ()))
 
 
-def attend(g, pos_ref, qseg_ref, kseg_ref, *refs):
+def attend(g, n_earlier, pos_ref, qseg_ref, kseg_ref, *refs):
     qin, (kvo, kv1, kv2) = refs[:4], refs[4:7]
-    outs, (dko, dk1, dk2) = refs[7:11], refs[11:14]
-    kx, vx, acck, accv, qs, dos, res, qn, gn, dots, invs, s_scr, p_scr, d_scr = refs[14:]
+    earlier, refs = refs[7 : 7 + n_earlier], refs[7 + n_earlier :]
+    outs, (dko, dk1, dk2) = refs[:4], refs[4:7]
+    kx, vx, acck, accv, qs, dos, res, qn, gn, dots, invs, s_scr, p_scr, d_scr = refs[7:]
 
     for src, base in ((kv2, 0), (kv1, ROWS), (kvo, 2 * ROWS)):
         for d in range(RING):
             row = pl.ds(pl.multiple_of(base + TOK * pos_ref[d], TOK), TOK)
-            kx[row, :HEAD_DIM] = src[TOK * d : TOK * (d + 1), HEAD_DIM * g : HEAD_DIM * (g + 1)]
-            vx[row, :HEAD_DIM] = src[
-                TOK * d : TOK * (d + 1), HEAD_DIM * (KV + g) : HEAD_DIM * (KV + g + 1)
-            ]
+            kx[row, :HEAD_DIM] = src[TOK * d : TOK * (d + 1), :HEAD_DIM]
+            vx[row, :HEAD_DIM] = src[TOK * d : TOK * (d + 1), HEAD_DIM:]
     kx[:, HEAD_DIM:] = kseg_ref[...]
     vx[:, HEAD_DIM:] = jnp.ones((EXT, HEAD_DIM), BF)
     acck[...] = jnp.zeros_like(acck)
@@ -99,24 +98,32 @@
             sl = slice(TOK * j, TOK * (j + 1))
             outs[d][:, HEAD_DIM * j : HEAD_DIM * (j + 1)] = res[d, sl, :HEAD_DIM]
             outs[d][:, HALF + HEAD_DIM * j : HALF + HEAD_DIM * (j + 1)] = res[d, sl, HEAD_DIM:]
+    for dst, src in zip((dk1, dk2), earlier):
+        dst[:, : src.shape[1]] = src[...]
     for dst, base in ((dk2, 0), (dk1, ROWS), (dko, 2 * ROWS)):
+        at = dst.shape[1] - 2 * HEAD_DIM
         for d in range(RING):
             row = pl.ds(pl.multiple_of(base + TOK * pos_ref[d], TOK), TOK)
             sl = slice(TOK * d, TOK * (d + 1))
-            dst[sl, :HEAD_DIM] = acck[:, row].T.astype(dst.dtype)
-            dst[sl, HEAD_DIM:] = accv[:, row].T.astype(dst.dtype)
-
-
-def call(body, name, shapes, args, scratch=(), flops=0, limit=60):
+            dst[sl, at : at + HEAD_DIM] = acck[:, row].T.astype(dst.dtype)
+            dst[sl, at + HEAD_DIM :] = accv[:, row].T.astype(dst.dtype)
+
+
+def call(body, name, shapes, args, scratch=(), flops=0, limit=60, space=pltpu.VMEM, aliases=None):
+    at = pl.BlockSpec(memory_space=space)
     vm = pl.BlockSpec(memory_space=pltpu.VMEM)
     sm = pl.BlockSpec(memory_space=pltpu.SMEM)
     return list(
         pl.pallas_call(
             body,
             out_shape=[jax.ShapeDtypeStruct(shape, dtype) for shape, dtype in shapes],
-            in_specs=[sm if arg.ndim == 1 else vm for arg in args],
-            out_specs=[vm] * len(shapes),
-            scratch_shapes=[pltpu.VMEM(shape, dtype) for shape, dtype in scratch],
+            in_specs=[
+                sm if arg.ndim == 1 else at if i in (aliases or {}) else vm
+                for i, arg in enumerate(args)
+            ],
+            out_specs=[at] * len(shapes),
+            scratch_shapes=list(scratch),
+            input_output_aliases=aliases or {},
             compiler_params=pltpu.CompilerParams(vmem_limit_bytes=limit * 1024 * 1024),
             cost_estimate=pl.CostEstimate(
                 flops=flops, bytes_accessed=4 * 1024 * 1024, transcendentals=0
@@ -126,32 +133,34 @@
     )
 
 
-def attend_call(g, pos, qseg, kseg, qin, kvs):
+def attend_call(g, pos, qseg, kseg, qin, kvs, earlier=()):
+    width = 2 * HEAD_DIM * (g + 1)
+    scratch = [
+        ((EXT, 2 * HEAD_DIM), BF),
+        ((EXT, 2 * HEAD_DIM), BF),
+        ((HEAD_DIM, EXT), F32),
+        ((HEAD_DIM, EXT), F32),
+        ((RING, ROWS, 2 * HEAD_DIM), BF),
+        ((RING, ROWS, HEAD_DIM), BF),
+        ((RING, ROWS, 2 * HEAD_DIM), BF),
+        ((ROWS, HEAD_DIM), BF),
+        ((ROWS, HEAD_DIM), BF),
+        ((ROWS, 1), F32),
+        ((ROWS, HEAD_DIM), F32),
+        ((ROWS, WINDOW + TOK), F32),
+        ((ROWS, WINDOW + TOK), BF),
+        ((ROWS, WINDOW + TOK), BF),
+    ]
     return call(
-        functools.partial(attend, g),
+        functools.partial(attend, g, len(earlier)),
         "attend",
         [((TOK, 2 * HALF), BF)] * RING
         + [((ROWS, 2 * HEAD_DIM), F32)]
-        + [((ROWS, 2 * HEAD_DIM), BF)] * 2,
-        (pos, qseg, kseg, *qin, *kvs),
-        [
-            ((EXT, 2 * HEAD_DIM), BF),
-            ((EXT, 2 * HEAD_DIM), BF),
-            ((HEAD_DIM, EXT), F32),
-            ((HEAD_DIM, EXT), F32),
-            ((RING, ROWS, 2 * HEAD_DIM), BF),
-            ((RING, ROWS, HEAD_DIM), BF),
-            ((RING, ROWS, 2 * HEAD_DIM), BF),
-            ((ROWS, HEAD_DIM), BF),
-            ((ROWS, HEAD_DIM), BF),
-            ((ROWS, 1), F32),
-            ((ROWS, HEAD_DIM), F32),
-            ((ROWS, WINDOW + TOK), F32),
-            ((ROWS, WINDOW + TOK), BF),
-            ((ROWS, WINDOW + TOK), BF),
-        ],
+        + [((ROWS, width), BF)] * 2,
+        (pos, qseg, kseg, *qin, *kvs, *earlier),
+        [pltpu.VMEM(shape, dtype) for shape, dtype in scratch],
         flops=6 * 2 * 4 * ROWS * 1152 * 256,
-        limit=60,
+        limit=40,
     )
 
 
@@ -161,11 +170,13 @@
 
 
 def pack_kv(here_ref, k_ref, v_ref, *outs):
-    width = KV * HEAD_DIM
-    for d in range(RING):
-        cols = ring_slice(here_ref, d, width)
-        outs[d][:, :width] = k_ref[:, cols]
-        outs[d][:, width:] = v_ref[:, cols]
+    for d in range(RING):
+        cols = ring_slice(here_ref, d, KV * HEAD_DIM)
+        for ref, base in ((k_ref, 0), (v_ref, HEAD_DIM)):
+            value = ref[:, cols]
+            for g in range(KV):
+                at = 2 * g * HEAD_DIM + base
+                outs[d][:, at : at + HEAD_DIM] = value[:, g * HEAD_DIM : (g + 1) * HEAD_DIM]
 
 
 def pack_q(here_ref, q_ref, d_ref, *outs):
@@ -177,31 +188,52 @@
                 outs[g * RING + d][:, base : base + HALF] = value[:, g * HALF : (g + 1) * HALF]
 
 
-def add_kv(own0, one0, two0, own1, one1, two1, *outs):
-    for g, (own, one, two) in enumerate(((own0, one0, two0), (own1, one1, two1))):
+def add_kv(own0, own1, one, two, *outs):
+    for g, own in enumerate((own0, own1)):
+        cols = slice(2 * HEAD_DIM * g, 2 * HEAD_DIM * (g + 1))
         for d in range(RING):
             rows = slice(TOK * d, TOK * (d + 1))
-            total = own[rows] + one[rows].astype(F32) + two[rows].astype(F32)
-            outs[d][:, 2 * HEAD_DIM * g : 2 * HEAD_DIM * (g + 1)] = total.astype(BF)
+            total = own[rows] + one[rows, cols].astype(F32) + two[rows, cols].astype(F32)
+            outs[d][:, cols] = total.astype(BF)
+
+
+def columns(index, width):
+    return pl.ds(pl.multiple_of(index * width, width), width)
+
+
+def place_wide(g, here_ref, parts, attn, gq, sem):
+    copies = []
+    for d in range(RING):
+        cols = columns(lax.rem(here_ref[0] + d, RING) * KV + g, HALF)
+        for dst, base in ((attn, 0), (gq, HALF)):
+            src = parts[d].at[:, base : base + HALF]
+            copies.append(pltpu.make_async_copy(src, dst.at[:, cols], sem.at[len(copies)]))
+    return copies
+
+
+def assemble_first(here_ref, *refs):
+    parts, (attn, gq, sem) = refs[:RING], refs[RING:]
+    copies = place_wide(0, here_ref, parts, attn, gq, sem)
+    for copy in copies:
+        copy.start()
+    for copy in copies:
+        copy.wait()
 
 
 def assemble(here_ref, *refs):
-    parts, kvs, (attn, gq, gk, gv) = refs[: 2 * RING], refs[2 * RING : 3 * RING], refs[3 * RING :]
-    for d in range(RING):
-        wide = ring_slice(here_ref, d, KV * HALF)
-        thin = ring_slice(here_ref, d, KV * HEAD_DIM)
-        for ref, base in ((attn, 0), (gq, HALF)):
-            ref[:, wide] = jnp.concatenate(
-                [parts[g * RING + d][:, base : base + HALF] for g in range(KV)], axis=1
-            )
-        for ref, base in ((gk, 0), (gv, HEAD_DIM)):
-            ref[:, thin] = jnp.concatenate(
-                [
-                    kvs[d][:, base + 2 * HEAD_DIM * g : base + 2 * HEAD_DIM * g + HEAD_DIM]
-                    for g in range(KV)
-                ],
-                axis=1,
-            )
+    parts, kvs = refs[2 : 2 + RING], refs[2 + RING : 2 + 2 * RING]
+    attn, gq, gk, gv, sem = refs[2 + 2 * RING :]
+    copies = place_wide(1, here_ref, parts, attn, gq, sem)
+    for d in range(RING):
+        for g in range(KV):
+            cols = columns(lax.rem(here_ref[0] + d, RING) * KV + g, HEAD_DIM)
+            for dst, base in ((gk, 2 * g * HEAD_DIM), (gv, (2 * g + 1) * HEAD_DIM)):
+                src = kvs[d].at[:, base : base + HEAD_DIM]
+                copies.append(pltpu.make_async_copy(src, dst.at[:, cols], sem.at[len(copies)]))
+    for copy in copies:
+        copy.start()
+    for copy in copies:
+        copy.wait()
 
 
 def shards(queries, key_states, value_states, grad_output, segment_ids):
@@ -230,11 +262,14 @@
     thin_part, wide_part = ((TOK, 2 * KV * HEAD_DIM), BF), ((TOK, 2 * HALF), BF)
     kv = call(pack_kv, "pack_kv", [thin_part] * RING, (here, key_states, value_states))
     packed = call(pack_q, "pack_q", [wide_part] * (KV * RING), (here, queries, grad_output))
-    kv_own = jnp.concatenate(around(kv, 1), axis=0)
-    kv_own, packed = lax.optimization_barrier((kv_own, packed))
-    kvs = (kv_own, along_halves(kv_own, 1), along_halves(kv_own, 2))
+    kv = around(kv, 1)
     first, second = around(packed[:RING], 1), packed[RING:]
-    first, second = lax.optimization_barrier((first, second))
+    kvs = []
+    for g in range(KV):
+        cols = slice(2 * HEAD_DIM * g, 2 * HEAD_DIM * (g + 1))
+        own = jnp.concatenate([part[:, cols] for part in kv], axis=0)
+        kvs.append((own, along_halves(own, 1), along_halves(own, 2)))
+    second, _ = lax.optimization_barrier((second, kvs[0][0]))
     q_parts = (first, around(second, 1))
 
     padded = jnp.concatenate([jnp.full((WINDOW,), HEAD_DIM - 1, jnp.int32), segment_ids])
@@ -245,21 +280,35 @@
     steps = jnp.arange(RING, dtype=jnp.int32)
     pos = (index - steps) % RING
 
-    wide, thin = [], []
-    for g in range(KV):
-        res = attend_call(g, pos, qseg, kseg, q_parts[g], kvs)
-        if g > 0:
-            res, wide, thin = lax.optimization_barrier((res, wide, thin))
-        thin += [res[4], along_halves(res[5], -1), along_halves(res[6], -2)]
-        wide += around(res[:RING], -1)
-    grads = around(call(add_kv, "add_kv", [thin_part] * RING, thin), -1)
     width = RING * KV * HALF
+    wide_out, thin_out = ((TOK, width), BF), ((TOK, width // GROUP), BF)
+    res0 = attend_call(0, pos, qseg, kseg, q_parts[0], kvs[0])
+    wide0 = around(res0[:RING], -1)
+    res1 = attend_call(1, pos, qseg, kseg, q_parts[1], kvs[1], res0[5:])
+    res1, wide0 = lax.optimization_barrier((res1, wide0))
+    one, two = along_halves(res1[5], -1), along_halves(res1[6], -2)
+    wide1 = around(res1[:RING], -1)
+    placed = call(
+        assemble_first,
+        "assemble_first",
+        [wide_out] * 2,
+        (here, *wide0),
+        [pltpu.SemaphoreType.DMA((2 * RING,))],
+        limit=16,
+        space=pl.ANY,
+    )
+    grads = call(add_kv, "add_kv", [thin_part] * RING, (res0[4], res1[4], one, two), limit=16)
+    grads = around(grads, -1)
     return tuple(
         call(
             assemble,
             "assemble",
-            [((TOK, width), BF)] * 2 + [((TOK, width // GROUP), BF)] * 2,
-            (here, *wide, *grads),
+            [wide_out] * 2 + [thin_out] * 2,
+            (here, *placed, *wide1, *grads),
+            [pltpu.SemaphoreType.DMA((6 * RING,))],
+            limit=16,
+            space=pl.ANY,
+            aliases={1: 0, 2: 1},
         )
     )
 

time: 116 us -> 96.2 us (0.83)
  Pallas kernels: 37.9 us -> 30 us
  starting transfers between devices: 46.1 us -> 41.9 us
  waiting for transfers between devices: 24.7 us -> 20.9 us
  local copies, waits for them, and re-layouts: 3.81 us -> 1.09 us
  other arithmetic: 2.37 us -> 0.45 us
    ppermute x18, waiting for transfers between devices: 23.2 us -> 10.3 us  [along_ring(): return lax.ppermute(value, 'head', pairs)]
    ppermute x6, waiting for transfers between devices: 1.53 us -> 10.6 us  [along_halves(): return lax.ppermute(value, ('blk', 'head'), pairs)]
    pallas_call x6 -> x7, Pallas kernels: 37.9 us -> 30 us  [call(): pl.pallas_call(body, out_shape=[jax.ShapeDtypeStruct(shape, dtype) for sh...]
    ppermute x18, starting transfers between devices: 27.8 us -> 22.2 us  [along_ring(): return lax.ppermute(value, 'head', pairs)]
    unnamed x60 -> x16, local copies, waits for them, and re-layouts: 3.66 us -> 0.89 us
    ppermute x6, starting transfers between devices: 18.3 us -> 19.6 us  [along_halves(): return lax.ppermute(value, ('blk', 'head'), pairs)]
  transfers between devices with their start and end apart: 24 -> 24, of which waited for: 10 -> 6; matrix products, arithmetic and copies ran while one was open for 2% -> 1% of each run, Pallas kernels for 28% -> 28%
where the time goes in v2:
time: 96.2 us; the launch traced here: 95.4 us
  starting transfers between devices  41.9 us (44%)
  Pallas kernels  30 us (31%)
  waiting for transfers between devices  20.9 us (22%)
  between operations  1.11 us (1%)
  local copies, waits for them, and re-layouts  1.09 us (1%)
    pallas_call x7, Pallas kernels, call(): pl.pallas_call(body, out_shape=[jax.ShapeDtypeStruct(shape, dtype) for sh...  30 us
    ppermute x18, starting transfers between devices, along_ring(): return lax.ppermute(value, 'head', pairs)  22.2 us
    ppermute x6, starting transfers between devices, along_halves(): return lax.ppermute(value, ('blk', 'head'), pairs)  19.6 us
    ppermute x6, waiting for transfers between devices, along_halves(): return lax.ppermute(value, ('blk', 'head'), pairs)  10.6 us
    ppermute x18, waiting for transfers between devices, along_ring(): return lax.ppermute(value, 'head', pairs)  10.3 us
  transfers between devices with their start and end apart: 24, of which 6 were waited for; matrix products, arithmetic and copies ran while one was open for 1% of the time, Pallas kernels for 28%

profile of v2, /device:TPU:160, one launch (start us, length us, event | category | flops | bytes accessed | tf_op | source)
XLA Modules:
  0.0 95.4 jit_solution(1318628598630499515)
XLA Ops:
  0.6 1.9 %pack_kv.1 = (bf16[128,512]{1,0:T(8,128)(2,1)}, bf16[128,512]{1,0:T(8,128)(2,1)}, bf16[128,512]{1,0:T(8,128)(2,1)}, bf16[128,512]{1,0:T(8,128)(2,1)}) custom-call(s32[1]{0:T(128)} %bitcast.here_ref, bf16[128,1024]{1,0:T(8,128)(2,1)} %k_ref.1, bf16[128,1024]{1,0:T(8,128)(2,1)} %v_ref.1), custom_call_target="tpu_custom_call" | custom-call | bytes 4194304 | tf_op jit(solution)/shard_map/pack_kv/pallas_call | solution.py:117
  2.5 1.5 %collective-permute-start = (bf16[128,512]{1,0:T(8,128)(2,1)}, bf16[128,512]{1,0:T(8,128)(2,1)S(1)}, u32[]{:S(2)}, u32[]{:S(2)}) collective-permute-start(bf16[128,512]{1,0:T(8,128)(2,1)} %get-tuple-element.56), channel_id=1, source_target_pairs={{0,1},{1,2},{2,3},{3,0},{4,5},{5,6},{6,7},{7,4},{8,9},{9,10},{10,1... | collective-permute-start | bytes 393224 | tf_op jit(solution)/shard_map/ppermute | solution.py:249
  4.0 2.7 %collective-permute-start.1 = (bf16[128,512]{1,0:T(8,128)(2,1)}, bf16[128,512]{1,0:T(8,128)(2,1)S(1)}, u32[]{:S(2)}, u32[]{:S(2)}) collective-permute-start(bf16[128,512]{1,0:T(8,128)(2,1)} %get-tuple-element.57), channel_id=1, source_target_pairs={{0,2},{1,3},{2,0},{3,1},{4,6},{5,7},{6,4},{7,5},{8,10},{9,11},{10,... | collective-permute-start | bytes 393224 | tf_op jit(solution)/shard_map/ppermute | solution.py:249
  6.8 1.4 %collective-permute-start.2 = (bf16[128,512]{1,0:T(8,128)(2,1)}, bf16[128,512]{1,0:T(8,128)(2,1)S(1)}, u32[]{:S(2)}, u32[]{:S(2)}) collective-permute-start(bf16[128,512]{1,0:T(8,128)(2,1)} %get-tuple-element.58), channel_id=1, source_target_pairs={{0,3},{1,0},{2,1},{3,2},{4,7},{5,4},{6,5},{7,6},{8,11},{9,8},{10,9... | collective-permute-start | bytes 393224 | tf_op jit(solution)/shard_map/ppermute | solution.py:249
  8.2 3.0 %pack_q.1 = (bf16[128,1024]{1,0:T(8,128)(2,1)}, bf16[128,1024]{1,0:T(8,128)(2,1)}, bf16[128,1024]{1,0:T(8,128)(2,1)}, bf16[128,1024]{1,0:T(8,128)(2,1)}, bf16[12...) custom-call(s32[1]{0:T(128)} %bitcast.here_ref, ...), custom_call_target="tpu_custom_call" | custom-call | bytes 4194304 | tf_op jit(solution)/shard_map/pack_q/pallas_call | solution.py:117
  14.0 1.8 %collective-permute-start.10 = (bf16[128,1024]{1,0:T(8,128)(2,1)S(1)}, bf16[128,1024]{1,0:T(8,128)(2,1)S(1)}, u32[]{:S(2)}, u32[]{:S(2)}) collective-permute-start(bf16[128,1024]{1,0:T(8,128)(2,1)S(1)} %copy-done.7), channel_id=1, source_target_pairs={{0,3},{1,0},{2,1},{3,2},{4,7},{5,4},{6,5},{7,6},{8,11},{9,8},{10,9... | collective-permute-start | bytes 786440 | tf_op jit(solution)/shard_map/ppermute | solution.py:249
  16.0 2.1 %collective-permute-start.12 = (bf16[512,256]{1,0:T(8,128)(2,1)S(1)}, bf16[512,256]{1,0:T(8,128)(2,1)S(1)}, u32[]{:S(2)}, u32[]{:S(2)}) collective-permute-start(bf16[512,256]{1,0:T(8,128)(2,1)S(1)} %pad_maximum_fusion.refs_4_), channel_id=1, source_target_pairs={{0,8},{1,9},{2,10},{3,11},{4,12},{5,13},{6,14},{7,15},{8,16},{9,17... | collective-permute-start | bytes 786440 | tf_op jit(solution)/shard_map/ppermute | solution.py:257
  18.0 3.5 %collective-permute-start.11 = (bf16[512,256]{1,0:T(8,128)(2,1)S(1)}, bf16[512,256]{1,0:T(8,128)(2,1)S(1)}, u32[]{:S(2)}, u32[]{:S(2)}) collective-permute-start(bf16[512,256]{1,0:T(8,128)(2,1)S(1)} %pad_maximum_fusion.refs_4_), channel_id=1, source_target_pairs={{0,4},{1,5},{2,6},{3,7},{4,8},{5,9},{6,10},{7,11},{8,12},{9,13},{1... | collective-permute-start | bytes 786440 | tf_op jit(solution)/shard_map/ppermute | solution.py:257
  21.7 3.8 %collective-permute-done.8.refs_1_ = bf16[128,1024]{1,0:T(8,128)(2,1)S(1)} collective-permute-done((bf16[128,1024]{1,0:T(8,128)(2,1)}, bf16[128,1024]{1,0:T(8,128)(2,1)S(1)}, u32[]{:S(2)}, u32[]{:S(2)}) %collective-permute-start.8) | collective-permute-done | bytes 262176 | tf_op jit(solution)/shard_map/ppermute | solution.py:249
  25.5 1.9 %collective-permute-start.7 = (bf16[512,256]{1,0:T(8,128)(2,1)S(1)}, bf16[512,256]{1,0:T(8,128)(2,1)S(1)}, u32[]{:S(2)}, u32[]{:S(2)}) collective-permute-start(bf16[512,256]{1,0:T(8,128)(2,1)S(1)} %pad_maximum_fusion.1.refs_4_), channel_id=1, source_target_pairs={{0,8},{1,9},{2,10},{3,11},{4,12},{5,13},{6,14},{7,15},{8,16},{9,17... | collective-permute-start | bytes 786440 | tf_op jit(solution)/shard_map/ppermute | solution.py:257
  27.4 3.5 %collective-permute-start.6 = (bf16[512,256]{1,0:T(8,128)(2,1)S(1)}, bf16[512,256]{1,0:T(8,128)(2,1)S(1)}, u32[]{:S(2)}, u32[]{:S(2)}) collective-permute-start(bf16[512,256]{1,0:T(8,128)(2,1)S(1)} %pad_maximum_fusion.1.refs_4_), channel_id=1, source_target_pairs={{0,4},{1,5},{2,6},{3,7},{4,8},{5,9},{6,10},{7,11},{8,12},{9,13},{1... | collective-permute-start | bytes 786440 | tf_op jit(solution)/shard_map/ppermute | solution.py:257
  32.2 2.5 %collective-permute-start.5 = (bf16[128,1024]{1,0:T(8,128)(2,1)S(1)}, bf16[128,1024]{1,0:T(8,128)(2,1)S(1)}, u32[]{:S(2)}, u32[]{:S(2)}) collective-permute-start(bf16[128,1024]{1,0:T(8,128)(2,1)S(1)} %copy-done.4), channel_id=1, source_target_pairs={{0,3},{1,0},{2,1},{3,2},{4,7},{5,4},{6,5},{7,6},{8,11},{9,8},{10,9... | collective-permute-start | bytes 786440 | tf_op jit(solution)/shard_map/ppermute | solution.py:249
  34.7 11.2 %attend.2 = (bf16[128,1024]{1,0:T(8,128)(2,1)S(1)}, bf16[128,1024]{1,0:T(8,128)(2,1)S(1)}, bf16[128,1024]{1,0:T(8,128)(2,1)S(1)}, bf16[128,1024]{1,0:T(8,128)(2,...) custom-call(s32[4]{0:T(128)S(1)} %and_select_fusion.pos_ref, ...), custom_call_target="tpu_custom_call" | custom-call | flops 7247757312 | bytes 4194304 | tf_op jit(solution)/shard_map/attend/pallas_call | solution.py:117
  46.5 2.1 %collective-permute-start.14 = (bf16[128,1024]{1,0:T(8,128)(2,1)S(1)}, bf16[128,1024]{1,0:T(8,128)(2,1)S(1)}, u32[]{:S(2)}, u32[]{:S(2)}) collective-permute-start(bf16[128,1024]{1,0:T(8,128)(2,1)S(1)} %get-tuple-element.78), channel_id=1, source_target_pairs={{0,2},{1,3},{2,0},{3,1},{4,6},{5,7},{6,4},{7,5},{8,10},{9,11},{10,... | collective-permute-start | bytes 786440 | tf_op jit(solution)/shard_map/ppermute | solution.py:249
  48.6 1.3 %collective-permute-start.15 = (bf16[128,1024]{1,0:T(8,128)(2,1)S(1)}, bf16[128,1024]{1,0:T(8,128)(2,1)S(1)}, u32[]{:S(2)}, u32[]{:S(2)}) collective-permute-start(bf16[128,1024]{1,0:T(8,128)(2,1)S(1)} %get-tuple-element.79), channel_id=1, source_target_pairs={{0,1},{1,2},{2,3},{3,0},{4,5},{5,6},{6,7},{7,4},{8,9},{9,10},{10,1... | collective-permute-start | bytes 786440 | tf_op jit(solution)/shard_map/ppermute | solution.py:249
  49.9 11.3 %attend.3 = (bf16[128,1024]{1,0:T(8,128)(2,1)S(1)}, bf16[128,1024]{1,0:T(8,128)(2,1)S(1)}, bf16[128,1024]{1,0:T(8,128)(2,1)S(1)}, bf16[128,1024]{1,0:T(8,128)(2,...) custom-call(s32[4]{0:T(128)S(1)} %and_select_fusion.pos_ref, ...), custom_call_target="tpu_custom_call" | custom-call | flops 7247757312 | bytes 4194304 | tf_op jit(solution)/shard_map/attend/pallas_call | solution.py:117
  61.2 1.6 %collective-permute-done.15.refs_3_ = bf16[128,1024]{1,0:T(8,128)(2,1)S(1)} collective-permute-done((bf16[128,1024]{1,0:T(8,128)(2,1)S(1)}, bf16[128,1024]{1,0:T(8,128)(2,1)S(1)}, u32[]{:S(2)}, u32[]{:S(2)}) %collective-permute-start.15) | collective-permute-done | bytes 262176 | tf_op jit(solution)/shard_map/ppermute | solution.py:249
  62.8 5.2 %collective-permute-start.19 = (bf16[512,512]{1,0:T(8,128)(2,1)S(1)}, bf16[512,512]{1,0:T(8,128)(2,1)S(1)}, u32[]{:S(2)}, u32[]{:S(2)}) collective-permute-start(bf16[512,512]{1,0:T(8,128)(2,1)S(1)} %get-tuple-element.92), channel_id=1, source_target_pairs={{4,0},{5,1},{6,2},{7,3},{8,4},{9,5},{10,6},{11,7},{12,8},{13,9},{1... | collective-permute-start | bytes 1572872 | tf_op jit(solution)/shard_map/ppermute | solution.py:257
  68.0 3.5 %collective-permute-start.20 = (bf16[512,512]{1,0:T(8,128)(2,1)S(1)}, bf16[512,512]{1,0:T(8,128)(2,1)S(1)}, u32[]{:S(2)}, u32[]{:S(2)}) collective-permute-start(bf16[512,512]{1,0:T(8,128)(2,1)S(1)} %get-tuple-element.93), channel_id=1, source_target_pairs={{8,0},{9,1},{10,2},{11,3},{12,4},{13,5},{14,6},{15,7},{16,8},{17,9... | collective-permute-start | bytes 1572872 | tf_op jit(solution)/shard_map/ppermute | solution.py:257
  73.7 10.6 %collective-permute-done.19.one = bf16[512,512]{1,0:T(8,128)(2,1)S(1)} collective-permute-done((bf16[512,512]{1,0:T(8,128)(2,1)S(1)}, bf16[512,512]{1,0:T(8,128)(2,1)S(1)}, u32[]{:S(2)}, u32[]{:S(2)}) %collective-permute-start.19) | collective-permute-done | bytes 524320 | tf_op jit(solution)/shard_map/ppermute | solution.py:257
  85.5 1.4 %collective-permute-start.22 = (bf16[128,512]{1,0:T(8,128)(2,1)S(1)}, bf16[128,512]{1,0:T(8,128)(2,1)S(1)}, u32[]{:S(2)}, u32[]{:S(2)}) collective-permute-start(bf16[128,512]{1,0:T(8,128)(2,1)S(1)} %get-tuple-element.96), channel_id=1, source_target_pairs={{0,2},{1,3},{2,0},{3,1},{4,6},{5,7},{6,4},{7,5},{8,10},{9,11},{10,... | collective-permute-start | bytes 393224 | tf_op jit(solution)/shard_map/ppermute | solution.py:249
  89.0 1.6 %collective-permute-done.21.refs_7_ = bf16[128,512]{1,0:T(8,128)(2,1)S(1)} collective-permute-done((bf16[128,512]{1,0:T(8,128)(2,1)S(1)}, bf16[128,512]{1,0:T(8,128)(2,1)S(1)}, u32[]{:S(2)}, u32[]{:S(2)}) %collective-permute-start.21) | collective-permute-done | bytes 131104 | tf_op jit(solution)/shard_map/ppermute | solution.py:249
  90.7 2.2 %collective-permute-done.22.refs_8_ = bf16[128,512]{1,0:T(8,128)(2,1)S(1)} collective-permute-done((bf16[128,512]{1,0:T(8,128)(2,1)S(1)}, bf16[128,512]{1,0:T(8,128)(2,1)S(1)}, u32[]{:S(2)}, u32[]{:S(2)}) %collective-permute-start.22) | collective-permute-done | bytes 131104 | tf_op jit(solution)/shard_map/ppermute | solution.py:249
  93.9 1.3 %assemble.1 = (bf16[128,4096]{1,0:T(8,128)(2,1)}, bf16[128,4096]{1,0:T(8,128)(2,1)}, bf16[128,1024]{1,0:T(8,128)(2,1)}, bf16[128,1024]{1,0:T(8,128)(2,1)}) custom-call(s32[1]{0:T(128)} %bitcast.here_ref, bf16[128,4096]{1,0:T(8,128)(2,1)} %get-tuple-element.84.refs_0_, ...), custom_call_target="tpu_custom_call", output_to_operand_aliasing={{0}: (1, {}), {1}: (2, {})} | custom-call | bytes 4194304 | tf_op jit(solution)/shard_map/assemble/pallas_call | solution.py:117
  (58 shorter events, 11.3 us)
Async XLA Ops:
  2.5 11.3 %collective-permute-start = (bf16[128,512]{1,0:T(8,128)(2,1)}, bf16[128,512]{1,0:T(8,128)(2,1)S(1)}, u32[]{:S(2)}, u32[]{:S(2)}) collective-permute-start(bf16[128,512]{1,0:T(8,128)(2,1)} %get-tuple-element.56), channel_id=1, source_target_pairs={{0,1},{1,2},{2,3},{3,0},{4,5},{5,6},{6,7},{7,4},{8,9},{9,10},{10,1... | collective-permute-start | bytes 393224 | tf_op jit(solution)/shard_map/ppermute | solution.py:249
  4.0 11.8 %collective-permute-start.1 = (bf16[128,512]{1,0:T(8,128)(2,1)}, bf16[128,512]{1,0:T(8,128)(2,1)S(1)}, u32[]{:S(2)}, u32[]{:S(2)}) collective-permute-start(bf16[128,512]{1,0:T(8,128)(2,1)} %get-tuple-element.57), channel_id=1, source_target_pairs={{0,2},{1,3},{2,0},{3,1},{4,6},{5,7},{6,4},{7,5},{8,10},{9,11},{10,... | collective-permute-start | bytes 393224 | tf_op jit(solution)/shard_map/ppermute | solution.py:249
  6.8 9.1 %collective-permute-start.2 = (bf16[128,512]{1,0:T(8,128)(2,1)}, bf16[128,512]{1,0:T(8,128)(2,1)S(1)}, u32[]{:S(2)}, u32[]{:S(2)}) collective-permute-start(bf16[128,512]{1,0:T(8,128)(2,1)} %get-tuple-element.58), channel_id=1, source_target_pairs={{0,3},{1,0},{2,1},{3,2},{4,7},{5,4},{6,5},{7,6},{8,11},{9,8},{10,9... | collective-permute-start | bytes 393224 | tf_op jit(solution)/shard_map/ppermute | solution.py:249
  11.2 14.2 %collective-permute-start.8 = (bf16[128,1024]{1,0:T(8,128)(2,1)}, bf16[128,1024]{1,0:T(8,128)(2,1)S(1)}, u32[]{:S(2)}, u32[]{:S(2)}) collective-permute-start(bf16[128,1024]{1,0:T(8,128)(2,1)} %get-tuple-element.64), channel_id=1, source_target_pairs={{0,1},{1,2},{2,3},{3,0},{4,5},{5,6},{6,7},{7,4},{8,9},{9,10},{10,1... | collective-permute-start | bytes 786440 | tf_op jit(solution)/shard_map/ppermute | solution.py:249
  11.8 15.6 %collective-permute-start.9 = (bf16[128,1024]{1,0:T(8,128)(2,1)}, bf16[128,1024]{1,0:T(8,128)(2,1)S(1)}, u32[]{:S(2)}, u32[]{:S(2)}) collective-permute-start(bf16[128,1024]{1,0:T(8,128)(2,1)} %get-tuple-element.65), channel_id=1, source_target_pairs={{0,2},{1,3},{2,0},{3,1},{4,6},{5,7},{6,4},{7,5},{8,10},{9,11},{10,... | collective-permute-start | bytes 786440 | tf_op jit(solution)/shard_map/ppermute | solution.py:249
  14.0 16.9 %collective-permute-start.10 = (bf16[128,1024]{1,0:T(8,128)(2,1)S(1)}, bf16[128,1024]{1,0:T(8,128)(2,1)S(1)}, u32[]{:S(2)}, u32[]{:S(2)}) collective-permute-start(bf16[128,1024]{1,0:T(8,128)(2,1)S(1)} %copy-done.7), channel_id=1, source_target_pairs={{0,3},{1,0},{2,1},{3,2},{4,7},{5,4},{6,5},{7,6},{8,11},{9,8},{10,9... | collective-permute-start | bytes 786440 | tf_op jit(solution)/shard_map/ppermute | solution.py:249
  16.0 15.1 %collective-permute-start.12 = (bf16[512,256]{1,0:T(8,128)(2,1)S(1)}, bf16[512,256]{1,0:T(8,128)(2,1)S(1)}, u32[]{:S(2)}, u32[]{:S(2)}) collective-permute-start(bf16[512,256]{1,0:T(8,128)(2,1)S(1)} %pad_maximum_fusion.refs_4_), channel_id=1, source_target_pairs={{0,8},{1,9},{2,10},{3,11},{4,12},{5,13},{6,14},{7,15},{8,16},{9,17... | collective-permute-start | bytes 786440 | tf_op jit(solution)/shard_map/ppermute | solution.py:257
  18.0 14.2 %collective-permute-start.11 = (bf16[512,256]{1,0:T(8,128)(2,1)S(1)}, bf16[512,256]{1,0:T(8,128)(2,1)S(1)}, u32[]{:S(2)}, u32[]{:S(2)}) collective-permute-start(bf16[512,256]{1,0:T(8,128)(2,1)S(1)} %pad_maximum_fusion.refs_4_), channel_id=1, source_target_pairs={{0,4},{1,5},{2,6},{3,7},{4,8},{5,9},{6,10},{7,11},{8,12},{9,13},{1... | collective-permute-start | bytes 786440 | tf_op jit(solution)/shard_map/ppermute | solution.py:257
  25.5 20.4 %collective-permute-start.7 = (bf16[512,256]{1,0:T(8,128)(2,1)S(1)}, bf16[512,256]{1,0:T(8,128)(2,1)S(1)}, u32[]{:S(2)}, u32[]{:S(2)}) collective-permute-start(bf16[512,256]{1,0:T(8,128)(2,1)S(1)} %pad_maximum_fusion.1.refs_4_), channel_id=1, source_target_pairs={{0,8},{1,9},{2,10},{3,11},{4,12},{5,13},{6,14},{7,15},{8,16},{9,17... | collective-permute-start | bytes 786440 | tf_op jit(solution)/shard_map/ppermute | solution.py:257
  27.4 19.1 %collective-permute-start.6 = (bf16[512,256]{1,0:T(8,128)(2,1)S(1)}, bf16[512,256]{1,0:T(8,128)(2,1)S(1)}, u32[]{:S(2)}, u32[]{:S(2)}) collective-permute-start(bf16[512,256]{1,0:T(8,128)(2,1)S(1)} %pad_maximum_fusion.1.refs_4_), channel_id=1, source_target_pairs={{0,4},{1,5},{2,6},{3,7},{4,8},{5,9},{6,10},{7,11},{8,12},{9,13},{1... | collective-permute-start | bytes 786440 | tf_op jit(solution)/shard_map/ppermute | solution.py:257
  30.9 17.7 %collective-permute-start.3 = (bf16[128,1024]{1,0:T(8,128)(2,1)S(1)}, bf16[128,1024]{1,0:T(8,128)(2,1)S(1)}, u32[]{:S(2)}, u32[]{:S(2)}) collective-permute-start(bf16[128,1024]{1,0:T(8,128)(2,1)S(1)} %copy-done.6), channel_id=1, source_target_pairs={{0,1},{1,2},{2,3},{3,0},{4,5},{5,6},{6,7},{7,4},{8,9},{9,10},{10,1... | collective-permute-start | bytes 786440 | tf_op jit(solution)/shard_map/ppermute | solution.py:249
  31.0 18.9 %collective-permute-start.4 = (bf16[128,1024]{1,0:T(8,128)(2,1)S(1)}, bf16[128,1024]{1,0:T(8,128)(2,1)S(1)}, u32[]{:S(2)}, u32[]{:S(2)}) collective-permute-start(bf16[128,1024]{1,0:T(8,128)(2,1)S(1)} %copy-done.5), channel_id=1, source_target_pairs={{0,2},{1,3},{2,0},{3,1},{4,6},{5,7},{6,4},{7,5},{8,10},{9,11},{10,... | collective-permute-start | bytes 786440 | tf_op jit(solution)/shard_map/ppermute | solution.py:249
  32.2 17.7 %collective-permute-start.5 = (bf16[128,1024]{1,0:T(8,128)(2,1)S(1)}, bf16[128,1024]{1,0:T(8,128)(2,1)S(1)}, u32[]{:S(2)}, u32[]{:S(2)}) collective-permute-start(bf16[128,1024]{1,0:T(8,128)(2,1)S(1)} %copy-done.4), channel_id=1, source_target_pairs={{0,3},{1,0},{2,1},{3,2},{4,7},{5,4},{6,5},{7,6},{8,11},{9,8},{10,9... | collective-permute-start | bytes 786440 | tf_op jit(solution)/shard_map/ppermute | solution.py:249
  45.9 15.3 %collective-permute-start.13 = (bf16[128,1024]{1,0:T(8,128)(2,1)S(1)}, bf16[128,1024]{1,0:T(8,128)(2,1)S(1)}, u32[]{:S(2)}, u32[]{:S(2)}) collective-permute-start(bf16[128,1024]{1,0:T(8,128)(2,1)S(1)} %get-tuple-element.77), channel_id=1, source_target_pairs={{0,3},{1,0},{2,1},{3,2},{4,7},{5,4},{6,5},{7,6},{8,11},{9,8},{10,9... | collective-permute-start | bytes 786440 | tf_op jit(solution)/shard_map/ppermute | solution.py:249
  46.5 14.7 %collective-permute-start.14 = (bf16[128,1024]{1,0:T(8,128)(2,1)S(1)}, bf16[128,1024]{1,0:T(8,128)(2,1)S(1)}, u32[]{:S(2)}, u32[]{:S(2)}) collective-permute-start(bf16[128,1024]{1,0:T(8,128)(2,1)S(1)} %get-tuple-element.78), channel_id=1, source_target_pairs={{0,2},{1,3},{2,0},{3,1},{4,6},{5,7},{6,4},{7,5},{8,10},{9,11},{10,... | collective-permute-start | bytes 786440 | tf_op jit(solution)/shard_map/ppermute | solution.py:249
  48.6 14.2 %collective-permute-start.15 = (bf16[128,1024]{1,0:T(8,128)(2,1)S(1)}, bf16[128,1024]{1,0:T(8,128)(2,1)S(1)}, u32[]{:S(2)}, u32[]{:S(2)}) collective-permute-start(bf16[128,1024]{1,0:T(8,128)(2,1)S(1)} %get-tuple-element.79), channel_id=1, source_target_pairs={{0,1},{1,2},{2,3},{3,0},{4,5},{5,6},{6,7},{7,4},{8,9},{9,10},{10,1... | collective-permute-start | bytes 786440 | tf_op jit(solution)/shard_map/ppermute | solution.py:249
  62.8 21.4 %collective-permute-start.19 = (bf16[512,512]{1,0:T(8,128)(2,1)S(1)}, bf16[512,512]{1,0:T(8,128)(2,1)S(1)}, u32[]{:S(2)}, u32[]{:S(2)}) collective-permute-start(bf16[512,512]{1,0:T(8,128)(2,1)S(1)} %get-tuple-element.92), channel_id=1, source_target_pairs={{4,0},{5,1},{6,2},{7,3},{8,4},{9,5},{10,6},{11,7},{12,8},{13,9},{1... | collective-permute-start | bytes 1572872 | tf_op jit(solution)/shard_map/ppermute | solution.py:257
  68.0 16.3 %collective-permute-start.20 = (bf16[512,512]{1,0:T(8,128)(2,1)S(1)}, bf16[512,512]{1,0:T(8,128)(2,1)S(1)}, u32[]{:S(2)}, u32[]{:S(2)}) collective-permute-start(bf16[512,512]{1,0:T(8,128)(2,1)S(1)} %get-tuple-element.93), channel_id=1, source_target_pairs={{8,0},{9,1},{10,2},{11,3},{12,4},{13,5},{14,6},{15,7},{16,8},{17,9... | collective-permute-start | bytes 1572872 | tf_op jit(solution)/shard_map/ppermute | solution.py:257
  71.5 15.4 %collective-permute-start.16 = (bf16[128,1024]{1,0:T(8,128)(2,1)S(1)}, bf16[128,1024]{1,0:T(8,128)(2,1)S(1)}, u32[]{:S(2)}, u32[]{:S(2)}) collective-permute-start(bf16[128,1024]{1,0:T(8,128)(2,1)S(1)} %get-tuple-element.87), channel_id=1, source_target_pairs={{0,3},{1,0},{2,1},{3,2},{4,7},{5,4},{6,5},{7,6},{8,11},{9,8},{10,9... | collective-permute-start | bytes 786440 | tf_op jit(solution)/shard_map/ppermute | solution.py:249
  72.3 16.8 %collective-permute-start.17 = (bf16[128,1024]{1,0:T(8,128)(2,1)S(1)}, bf16[128,1024]{1,0:T(8,128)(2,1)S(1)}, u32[]{:S(2)}, u32[]{:S(2)}) collective-permute-start(bf16[128,1024]{1,0:T(8,128)(2,1)S(1)} %get-tuple-element.88), channel_id=1, source_target_pairs={{0,2},{1,3},{2,0},{3,1},{4,6},{5,7},{6,4},{7,5},{8,10},{9,11},{10,... | collective-permute-start | bytes 786440 | tf_op jit(solution)/shard_map/ppermute | solution.py:249
  73.5 15.5 %collective-permute-start.18 = (bf16[128,1024]{1,0:T(8,128)(2,1)S(1)}, bf16[128,1024]{1,0:T(8,128)(2,1)S(1)}, u32[]{:S(2)}, u32[]{:S(2)}) collective-permute-start(bf16[128,1024]{1,0:T(8,128)(2,1)S(1)} %get-tuple-element.89), channel_id=1, source_target_pairs={{0,1},{1,2},{2,3},{3,0},{4,5},{5,6},{6,7},{7,4},{8,9},{9,10},{10,1... | collective-permute-start | bytes 786440 | tf_op jit(solution)/shard_map/ppermute | solution.py:249
  84.5 6.2 %collective-permute-start.21 = (bf16[128,512]{1,0:T(8,128)(2,1)S(1)}, bf16[128,512]{1,0:T(8,128)(2,1)S(1)}, u32[]{:S(2)}, u32[]{:S(2)}) collective-permute-start(bf16[128,512]{1,0:T(8,128)(2,1)S(1)} %get-tuple-element.95), channel_id=1, source_target_pairs={{0,3},{1,0},{2,1},{3,2},{4,7},{5,4},{6,5},{7,6},{8,11},{9,8},{10,9... | collective-permute-start | bytes 393224 | tf_op jit(solution)/shard_map/ppermute | solution.py:249
  85.5 7.4 %collective-permute-start.22 = (bf16[128,512]{1,0:T(8,128)(2,1)S(1)}, bf16[128,512]{1,0:T(8,128)(2,1)S(1)}, u32[]{:S(2)}, u32[]{:S(2)}) collective-permute-start(bf16[128,512]{1,0:T(8,128)(2,1)S(1)} %get-tuple-element.96), channel_id=1, source_target_pairs={{0,2},{1,3},{2,0},{3,1},{4,6},{5,7},{6,4},{7,5},{8,10},{9,11},{10,... | collective-permute-start | bytes 393224 | tf_op jit(solution)/shard_map/ppermute | solution.py:249
  87.0 7.0 %collective-permute-start.23 = (bf16[128,512]{1,0:T(8,128)(2,1)S(1)}, bf16[128,512]{1,0:T(8,128)(2,1)S(1)}, u32[]{:S(2)}, u32[]{:S(2)}) collective-permute-start(bf16[128,512]{1,0:T(8,128)(2,1)S(1)} %get-tuple-element.97), channel_id=1, source_target_pairs={{0,1},{1,2},{2,3},{3,0},{4,5},{5,6},{6,7},{7,4},{8,9},{9,10},{10,1... | collective-permute-start | bytes 393224 | tf_op jit(solution)/shard_map/ppermute | solution.py:249
  (8 other events, 75.2 us)

commit v3 on v2

--- a/solution.py
+++ b/solution.py
@@ -30,7 +30,7 @@
     qin, (kvo, kv1, kv2) = refs[:4], refs[4:7]
     earlier, refs = refs[7 : 7 + n_earlier], refs[7 + n_earlier :]
     outs, (dko, dk1, dk2) = refs[:4], refs[4:7]
-    kx, vx, acck, accv, qs, dos, res, qn, gn, dots, invs, s_scr, p_scr, d_scr = refs[7:]
+    kx, vx, acck, accv, qs, dos, qn, gn, dots, invs, s_scr, p_scr, d_scr = refs[7:]
 
     for src, base in ((kv2, 0), (kv1, ROWS), (kvo, 2 * ROWS)):
         for d in range(RING):
@@ -52,6 +52,11 @@
     row_id = lax.broadcasted_iota(jnp.int32, (TOK, TOK), 0)
     col_id = lax.broadcasted_iota(jnp.int32, (TOK, TOK), 1)
     lower = col_id <= row_id
+
+    def put(ref, row, base, value):
+        for i in range(value.shape[0] // TOK):
+            at = base + (row // TOK + i) * HEAD_DIM
+            ref[:, at : at + HEAD_DIM] = value[TOK * i : TOK * (i + 1)]
 
     def step(d, carry):
         start = pl.multiple_of(TOK * pos_ref[d], TOK)
@@ -73,7 +78,7 @@
             out = jnp.dot(p_scr[sl], vx[span], preferred_element_type=F32)
             inv = 1.0 / out[:, HEAD_DIM:]
             attn = (out[:, :HEAD_DIM] * inv).astype(BF)
-            res[d, sl, :HEAD_DIM] = attn
+            put(outs[d], j, 0, attn)
             grad = dos[d, sl].astype(F32)
             dots[sl] = jnp.sum(grad * attn.astype(F32), axis=1, keepdims=True)
             invs[sl] = inv * SCALE
@@ -86,18 +91,14 @@
         for j in range(0, ROWS, 256):
             sl = slice(j, j + 256)
             dq = jnp.dot(d_scr[sl], kx[span, :HEAD_DIM], preferred_element_type=F32)
-            res[d, sl, HEAD_DIM:] = (dq * invs[sl]).astype(BF)
+            put(outs[d], j, HALF, (dq * invs[sl]).astype(BF))
         acck[:, span] += lax.dot_general(qn[...], d_scr[...], TN, preferred_element_type=F32)
         accv[:, span] += lax.dot_general(gn[...], p_scr[...], TN, preferred_element_type=F32)
         return carry
 
-    lax.fori_loop(0, RING, step, 0)
-
-    for d in range(RING):
-        for j in range(GROUP):
-            sl = slice(TOK * j, TOK * (j + 1))
-            outs[d][:, HEAD_DIM * j : HEAD_DIM * (j + 1)] = res[d, sl, :HEAD_DIM]
-            outs[d][:, HALF + HEAD_DIM * j : HALF + HEAD_DIM * (j + 1)] = res[d, sl, HEAD_DIM:]
+    for d in range(RING):
+        step(d, 0)
+
     for dst, src in zip((dk1, dk2), earlier):
         dst[:, : src.shape[1]] = src[...]
     for dst, base in ((dk2, 0), (dk1, ROWS), (dko, 2 * ROWS)):
@@ -109,16 +110,28 @@
             dst[sl, at + HEAD_DIM :] = accv[:, row].T.astype(dst.dtype)
 
 
-def call(body, name, shapes, args, scratch=(), flops=0, limit=60, space=pltpu.VMEM, aliases=None):
+def call(
+    body,
+    name,
+    shapes,
+    args,
+    scratch=(),
+    flops=0,
+    limit=60,
+    space=pltpu.VMEM,
+    aliases=None,
+    raw=False,
+):
     at = pl.BlockSpec(memory_space=space)
     vm = pl.BlockSpec(memory_space=pltpu.VMEM)
+    hbm = pl.BlockSpec(memory_space=pl.ANY)
     sm = pl.BlockSpec(memory_space=pltpu.SMEM)
     return list(
         pl.pallas_call(
             body,
             out_shape=[jax.ShapeDtypeStruct(shape, dtype) for shape, dtype in shapes],
             in_specs=[
-                sm if arg.ndim == 1 else at if i in (aliases or {}) else vm
+                sm if arg.ndim == 1 else hbm if raw or i in (aliases or {}) else vm
                 for i, arg in enumerate(args)
             ],
             out_specs=[at] * len(shapes),
@@ -142,7 +155,6 @@
         ((HEAD_DIM, EXT), F32),
         ((RING, ROWS, 2 * HEAD_DIM), BF),
         ((RING, ROWS, HEAD_DIM), BF),
-        ((RING, ROWS, 2 * HEAD_DIM), BF),
         ((ROWS, HEAD_DIM), BF),
         ((ROWS, HEAD_DIM), BF),
         ((ROWS, 1), F32),
@@ -164,28 +176,39 @@
     )
 
 
-def ring_slice(here_ref, steps, width):
-    at = lax.rem(here_ref[0] + (steps + RING), RING)
-    return pl.ds(pl.multiple_of(at * width, width), width)
-
-
-def pack_kv(here_ref, k_ref, v_ref, *outs):
-    for d in range(RING):
-        cols = ring_slice(here_ref, d, KV * HEAD_DIM)
-        for ref, base in ((k_ref, 0), (v_ref, HEAD_DIM)):
-            value = ref[:, cols]
-            for g in range(KV):
+def columns(index, width):
+    return pl.ds(pl.multiple_of(index * width, width), width)
+
+
+def run_copies(pairs, sem):
+    copies = [pltpu.make_async_copy(src, dst, sem.at[i]) for i, (src, dst) in enumerate(pairs)]
+    for copy in copies:
+        copy.start()
+    for copy in copies:
+        copy.wait()
+
+
+def pack_kv(here_ref, k_ref, v_ref, *refs):
+    outs, sem = refs[:RING], refs[RING]
+    pairs = []
+    for d in range(RING):
+        for g in range(KV):
+            cols = columns(jnp.bitwise_xor(here_ref[0], d) * KV + g, HEAD_DIM)
+            for ref, base in ((k_ref, 0), (v_ref, HEAD_DIM)):
                 at = 2 * g * HEAD_DIM + base
-                outs[d][:, at : at + HEAD_DIM] = value[:, g * HEAD_DIM : (g + 1) * HEAD_DIM]
-
-
-def pack_q(here_ref, q_ref, d_ref, *outs):
-    for d in range(RING):
-        cols = ring_slice(here_ref, d, KV * HALF)
-        for ref, base in ((q_ref, 0), (d_ref, HALF)):
-            value = ref[:, cols]
-            for g in range(KV):
-                outs[g * RING + d][:, base : base + HALF] = value[:, g * HALF : (g + 1) * HALF]
+                pairs.append((ref.at[:, cols], outs[d].at[:, at : at + HEAD_DIM]))
+    run_copies(pairs, sem)
+
+
+def pack_q(here_ref, q_ref, d_ref, *refs):
+    outs, sem = refs[: KV * RING], refs[KV * RING]
+    pairs = []
+    for g in range(KV):
+        for d in range(RING):
+            cols = columns(jnp.bitwise_xor(here_ref[0], d) * KV + g, HALF)
+            for ref, base in ((q_ref, 0), (d_ref, HALF)):
+                pairs.append((ref.at[:, cols], outs[g * RING + d].at[:, base : base + HALF]))
+    run_copies(pairs, sem)
 
 
 def add_kv(own0, own1, one, two, *outs):
@@ -197,14 +220,10 @@
             outs[d][:, cols] = total.astype(BF)
 
 
-def columns(index, width):
-    return pl.ds(pl.multiple_of(index * width, width), width)
-
-
 def place_wide(g, here_ref, parts, attn, gq, sem):
     copies = []
     for d in range(RING):
-        cols = columns(lax.rem(here_ref[0] + d, RING) * KV + g, HALF)
+        cols = columns(jnp.bitwise_xor(here_ref[0], d) * KV + g, HALF)
         for dst, base in ((attn, 0), (gq, HALF)):
             src = parts[d].at[:, base : base + HALF]
             copies.append(pltpu.make_async_copy(src, dst.at[:, cols], sem.at[len(copies)]))
@@ -226,7 +245,7 @@
     copies = place_wide(1, here_ref, parts, attn, gq, sem)
     for d in range(RING):
         for g in range(KV):
-            cols = columns(lax.rem(here_ref[0] + d, RING) * KV + g, HEAD_DIM)
+            cols = columns(jnp.bitwise_xor(here_ref[0], d) * KV + g, HEAD_DIM)
             for dst, base in ((gk, 2 * g * HEAD_DIM), (gv, (2 * g + 1) * HEAD_DIM)):
                 src = kvs[d].at[:, base : base + HEAD_DIM]
                 copies.append(pltpu.make_async_copy(src, dst.at[:, cols], sem.at[len(copies)]))
@@ -244,9 +263,8 @@
     here = jnp.full((1,), index, jnp.int32)
     half = (lax.axis_index("blk") * heads + head) // RING
 
-    def along_ring(value, steps):
-        pairs = [(i, i // RING * RING + (i + steps) % RING) for i in range(heads)]
-        return lax.ppermute(value, "head", pairs)
+    def along_ring(value, d):
+        return lax.ppermute(value, "head", [(i, i ^ d) for i in range(heads)])
 
     def along_halves(value, steps):
         pairs = [
@@ -256,21 +274,36 @@
         ]
         return lax.ppermute(value, ("blk", "head"), pairs)
 
-    def around(parts, sign):
-        return parts[:1] + [along_ring(parts[d], sign * d) for d in range(1, RING)]
+    def around(parts):
+        return parts[:1] + [along_ring(parts[d], d) for d in range(1, RING)]
 
     thin_part, wide_part = ((TOK, 2 * KV * HEAD_DIM), BF), ((TOK, 2 * HALF), BF)
-    kv = call(pack_kv, "pack_kv", [thin_part] * RING, (here, key_states, value_states))
-    packed = call(pack_q, "pack_q", [wide_part] * (KV * RING), (here, queries, grad_output))
-    kv = around(kv, 1)
-    first, second = around(packed[:RING], 1), packed[RING:]
+    sems = [pltpu.SemaphoreType.DMA((2 * KV * RING,))]
+    kv = call(
+        pack_kv,
+        "pack_kv",
+        [thin_part] * RING,
+        (here, key_states, value_states),
+        sems,
+        raw=True,
+    )
+    packed = call(
+        pack_q,
+        "pack_q",
+        [wide_part] * (KV * RING),
+        (here, queries, grad_output),
+        sems,
+        raw=True,
+    )
+    kv = around(kv)
+    first, second = around(packed[:RING]), packed[RING:]
     kvs = []
     for g in range(KV):
         cols = slice(2 * HEAD_DIM * g, 2 * HEAD_DIM * (g + 1))
         own = jnp.concatenate([part[:, cols] for part in kv], axis=0)
         kvs.append((own, along_halves(own, 1), along_halves(own, 2)))
     second, _ = lax.optimization_barrier((second, kvs[0][0]))
-    q_parts = (first, around(second, 1))
+    q_parts = (first, around(second))
 
     padded = jnp.concatenate([jnp.full((WINDOW,), HEAD_DIM - 1, jnp.int32), segment_ids])
     key_seg = lax.dynamic_slice_in_dim(padded, half * ROWS, EXT)
@@ -278,16 +311,16 @@
     kseg = (key_seg[:, None] == lanes).astype(BF)
     qseg = jnp.where(key_seg[WINDOW:, None] == lanes, 0.0, -BIG).astype(BF)
     steps = jnp.arange(RING, dtype=jnp.int32)
-    pos = (index - steps) % RING
+    pos = index ^ steps
 
     width = RING * KV * HALF
     wide_out, thin_out = ((TOK, width), BF), ((TOK, width // GROUP), BF)
     res0 = attend_call(0, pos, qseg, kseg, q_parts[0], kvs[0])
-    wide0 = around(res0[:RING], -1)
+    wide0 = around(res0[:RING])
     res1 = attend_call(1, pos, qseg, kseg, q_parts[1], kvs[1], res0[5:])
-    res1, wide0 = lax.optimization_barrier((res1, wide0))
     one, two = along_halves(res1[5], -1), along_halves(res1[6], -2)
-    wide1 = around(res1[:RING], -1)
+    last, wide0 = lax.optimization_barrier((res1[:RING], wide0))
+    wide1 = around(last)
     placed = call(
         assemble_first,
         "assemble_first",
@@ -298,7 +331,7 @@
         space=pl.ANY,
     )
     grads = call(add_kv, "add_kv", [thin_part] * RING, (res0[4], res1[4], one, two), limit=16)
-    grads = around(grads, -1)
+    grads = around(grads)
     return tuple(
         call(
             assemble,

time: 96.2 us -> 96.5 us (level)
  the two profiles are of different devices: /device:TPU:160 before, /device:TPU:96 now
where the time goes in v3:
time: 96.5 us; the launch traced here: 96.1 us
  starting transfers between devices  49.1 us (51%)
  Pallas kernels  28.5 us (30%)
  waiting for transfers between devices  15.8 us (16%)
  between operations  1.17 us (1%)
  local copies, waits for them, and re-layouts  1.09 us (1%)
    ppermute x18, starting transfers between devices, along_ring(): return lax.ppermute(value, 'head', [(i, i ^ d) for i in range(heads)])  28.7 us
    pallas_call x7, Pallas kernels, call(): pl.pallas_call(body, out_shape=[jax.ShapeDtypeStruct(shape, dtype) for sh...  28.5 us
    ppermute x6, starting transfers between devices, along_halves(): return lax.ppermute(value, ('blk', 'head'), pairs)  20.4 us
    ppermute x6, waiting for transfers between devices, along_halves(): return lax.ppermute(value, ('blk', 'head'), pairs)  9.41 us
    ppermute x18, waiting for transfers between devices, along_ring(): return lax.ppermute(value, 'head', [(i, i ^ d) for i in range(heads)])  6.44 us
  transfers between devices with their start and end apart: 24, of which 4 were waited for; matrix products, arithmetic and copies ran while one was open for 1% of the time, Pallas kernels for 26%

profile of v3, /device:TPU:96, one launch (start us, length us, event | category | flops | bytes accessed | tf_op | source)
XLA Modules:
  0.0 96.1 jit_solution(9590704818681866475)
XLA Ops:
  0.6 2.0 %pack_kv.1 = (bf16[128,512]{1,0:T(8,128)(2,1)}, bf16[128,512]{1,0:T(8,128)(2,1)}, bf16[128,512]{1,0:T(8,128)(2,1)}, bf16[128,512]{1,0:T(8,128)(2,1)}) custom-call(s32[1]{0:T(128)} %bitcast.here_ref, bf16[128,1024]{1,0:T(8,128)(2,1)} %k_ref.1, bf16[128,1024]{1,0:T(8,128)(2,1)} %v_ref.1), custom_call_target="tpu_custom_call" | custom-call | bytes 4194304 | tf_op jit(solution)/shard_map/pack_kv/pallas_call | solution.py:130
  2.6 1.6 %collective-permute-start = (bf16[128,512]{1,0:T(8,128)(2,1)}, bf16[128,512]{1,0:T(8,128)(2,1)S(1)}, u32[]{:S(2)}, u32[]{:S(2)}) collective-permute-start(bf16[128,512]{1,0:T(8,128)(2,1)} %get-tuple-element.53), channel_id=1, source_target_pairs={{0,1},{1,0},{2,3},{3,2},{4,5},{5,4},{6,7},{7,6},{8,9},{9,8},{10,11... | collective-permute-start | bytes 393224 | tf_op jit(solution)/shard_map/ppermute | solution.py:267
  4.2 2.7 %collective-permute-start.1 = (bf16[128,512]{1,0:T(8,128)(2,1)}, bf16[128,512]{1,0:T(8,128)(2,1)S(1)}, u32[]{:S(2)}, u32[]{:S(2)}) collective-permute-start(bf16[128,512]{1,0:T(8,128)(2,1)} %get-tuple-element.54), channel_id=1, source_target_pairs={{0,2},{1,3},{2,0},{3,1},{4,6},{5,7},{6,4},{7,5},{8,10},{9,11},{10,... | collective-permute-start | bytes 393224 | tf_op jit(solution)/shard_map/ppermute | solution.py:267
  7.4 3.1 %pack_q.1 = (bf16[128,1024]{1,0:T(8,128)(2,1)}, bf16[128,1024]{1,0:T(8,128)(2,1)}, bf16[128,1024]{1,0:T(8,128)(2,1)}, bf16[128,1024]{1,0:T(8,128)(2,1)}, bf16[12...) custom-call(s32[1]{0:T(128)} %bitcast.here_ref, ...), custom_call_target="tpu_custom_call" | custom-call | bytes 4194304 | tf_op jit(solution)/shard_map/pack_q/pallas_call | solution.py:130
  10.9 3.9 %collective-permute-start.9 = (bf16[128,1024]{1,0:T(8,128)(2,1)}, bf16[128,1024]{1,0:T(8,128)(2,1)S(1)}, u32[]{:S(2)}, u32[]{:S(2)}) collective-permute-start(bf16[128,1024]{1,0:T(8,128)(2,1)} %get-tuple-element.62), channel_id=1, source_target_pairs={{0,2},{1,3},{2,0},{3,1},{4,6},{5,7},{6,4},{7,5},{8,10},{9,11},{10,... | collective-permute-start | bytes 786440 | tf_op jit(solution)/shard_map/ppermute | solution.py:267
  15.2 0.6 copy-done.3
  16.7 2.1 %collective-permute-start.12 = (bf16[512,256]{1,0:T(8,128)(2,1)S(1)}, bf16[512,256]{1,0:T(8,128)(2,1)S(1)}, u32[]{:S(2)}, u32[]{:S(2)}) collective-permute-start(bf16[512,256]{1,0:T(8,128)(2,1)S(1)} %pad_maximum_fusion.refs_4_), channel_id=1, source_target_pairs={{0,8},{1,9},{2,10},{3,11},{4,12},{5,13},{6,14},{7,15},{8,16},{9,17... | collective-permute-start | bytes 786440 | tf_op jit(solution)/shard_map/ppermute | solution.py:275
  18.8 3.5 %collective-permute-start.11 = (bf16[512,256]{1,0:T(8,128)(2,1)S(1)}, bf16[512,256]{1,0:T(8,128)(2,1)S(1)}, u32[]{:S(2)}, u32[]{:S(2)}) collective-permute-start(bf16[512,256]{1,0:T(8,128)(2,1)S(1)} %pad_maximum_fusion.refs_4_), channel_id=1, source_target_pairs={{0,4},{1,5},{2,6},{3,7},{4,8},{5,9},{6,10},{7,11},{8,12},{9,13},{1... | collective-permute-start | bytes 786440 | tf_op jit(solution)/shard_map/ppermute | solution.py:275
  22.5 4.2 %collective-permute-start.7 = (bf16[512,256]{1,0:T(8,128)(2,1)S(1)}, bf16[512,256]{1,0:T(8,128)(2,1)S(1)}, u32[]{:S(2)}, u32[]{:S(2)}) collective-permute-start(bf16[512,256]{1,0:T(8,128)(2,1)S(1)} %pad_maximum_fusion.1.refs_4_), channel_id=1, source_target_pairs={{0,8},{1,9},{2,10},{3,11},{4,12},{5,13},{6,14},{7,15},{8,16},{9,17... | collective-permute-start | bytes 786440 | tf_op jit(solution)/shard_map/ppermute | solution.py:275
  26.7 3.2 %collective-permute-start.6 = (bf16[512,256]{1,0:T(8,128)(2,1)S(1)}, bf16[512,256]{1,0:T(8,128)(2,1)S(1)}, u32[]{:S(2)}, u32[]{:S(2)}) collective-permute-start(bf16[512,256]{1,0:T(8,128)(2,1)S(1)} %pad_maximum_fusion.1.refs_4_), channel_id=1, source_target_pairs={{0,4},{1,5},{2,6},{3,7},{4,8},{5,9},{6,10},{7,11},{8,12},{9,13},{1... | collective-permute-start | bytes 786440 | tf_op jit(solution)/shard_map/ppermute | solution.py:275
  30.0 4.2 %collective-permute-start.4 = (bf16[128,1024]{1,0:T(8,128)(2,1)S(1)}, bf16[128,1024]{1,0:T(8,128)(2,1)S(1)}, u32[]{:S(2)}, u32[]{:S(2)}) collective-permute-start(bf16[128,1024]{1,0:T(8,128)(2,1)S(1)} %copy-done.5), channel_id=1, source_target_pairs={{0,2},{1,3},{2,0},{3,1},{4,6},{5,7},{6,4},{7,5},{8,10},{9,11},{10,... | collective-permute-start | bytes 786440 | tf_op jit(solution)/shard_map/ppermute | solution.py:267
  34.7 10.4 %attend.2 = (bf16[128,1024]{1,0:T(8,128)(2,1)S(1)}, bf16[128,1024]{1,0:T(8,128)(2,1)S(1)}, bf16[128,1024]{1,0:T(8,128)(2,1)S(1)}, bf16[128,1024]{1,0:T(8,128)(2,...) custom-call(s32[4]{0:T(128)S(1)} %iota_xor_fusion.pos_ref, ...), custom_call_target="tpu_custom_call" | custom-call | flops 7247757312 | bytes 4194304 | tf_op jit(solution)/shard_map/attend/pallas_call | solution.py:130
  45.2 4.2 %collective-permute-start.14 = (bf16[128,1024]{1,0:T(8,128)(2,1)S(1)}, bf16[128,1024]{1,0:T(8,128)(2,1)S(1)}, u32[]{:S(2)}, u32[]{:S(2)}) collective-permute-start(bf16[128,1024]{1,0:T(8,128)(2,1)S(1)} %get-tuple-element.72), channel_id=1, source_target_pairs={{0,2},{1,3},{2,0},{3,1},{4,6},{5,7},{6,4},{7,5},{8,10},{9,11},{10,... | collective-permute-start | bytes 786440 | tf_op jit(solution)/shard_map/ppermute | solution.py:267
  49.9 10.5 %attend.3 = (bf16[128,1024]{1,0:T(8,128)(2,1)S(1)}, bf16[128,1024]{1,0:T(8,128)(2,1)S(1)}, bf16[128,1024]{1,0:T(8,128)(2,1)S(1)}, bf16[128,1024]{1,0:T(8,128)(2,...) custom-call(s32[4]{0:T(128)S(1)} %iota_xor_fusion.pos_ref, ...), custom_call_target="tpu_custom_call" | custom-call | flops 7247757312 | bytes 4194304 | tf_op jit(solution)/shard_map/attend/pallas_call | solution.py:130
  60.4 5.6 %collective-permute-start.19 = (bf16[512,512]{1,0:T(8,128)(2,1)S(1)}, bf16[512,512]{1,0:T(8,128)(2,1)S(1)}, u32[]{:S(2)}, u32[]{:S(2)}) collective-permute-start(bf16[512,512]{1,0:T(8,128)(2,1)S(1)} %get-tuple-element.86), channel_id=1, source_target_pairs={{4,0},{5,1},{6,2},{7,3},{8,4},{9,5},{10,6},{11,7},{12,8},{13,9},{1... | collective-permute-start | bytes 1572872 | tf_op jit(solution)/shard_map/ppermute | solution.py:275
  66.0 1.9 %collective-permute-start.20 = (bf16[512,512]{1,0:T(8,128)(2,1)S(1)}, bf16[512,512]{1,0:T(8,128)(2,1)S(1)}, u32[]{:S(2)}, u32[]{:S(2)}) collective-permute-start(bf16[512,512]{1,0:T(8,128)(2,1)S(1)} %get-tuple-element.87), channel_id=1, source_target_pairs={{8,0},{9,1},{10,2},{11,3},{12,4},{13,5},{14,6},{15,7},{16,8},{17,9... | collective-permute-start | bytes 1572872 | tf_op jit(solution)/shard_map/ppermute | solution.py:275
  68.1 3.3 %collective-permute-start.17 = (bf16[128,1024]{1,0:T(8,128)(2,1)S(1)}, bf16[128,1024]{1,0:T(8,128)(2,1)S(1)}, u32[]{:S(2)}, u32[]{:S(2)}) collective-permute-start(bf16[128,1024]{1,0:T(8,128)(2,1)S(1)} %get-tuple-element.82), channel_id=1, source_target_pairs={{0,2},{1,3},{2,0},{3,1},{4,6},{5,7},{6,4},{7,5},{8,10},{9,11},{10,... | collective-permute-start | bytes 786440 | tf_op jit(solution)/shard_map/ppermute | solution.py:267
  71.4 1.4 %collective-permute-start.18 = (bf16[128,1024]{1,0:T(8,128)(2,1)S(1)}, bf16[128,1024]{1,0:T(8,128)(2,1)S(1)}, u32[]{:S(2)}, u32[]{:S(2)}) collective-permute-start(bf16[128,1024]{1,0:T(8,128)(2,1)S(1)} %get-tuple-element.83), channel_id=1, source_target_pairs={{0,3},{1,2},{2,1},{3,0},{4,7},{5,6},{6,5},{7,4},{8,11},{9,10},{10,... | collective-permute-start | bytes 786440 | tf_op jit(solution)/shard_map/ppermute | solution.py:267
  72.8 9.4 %collective-permute-done.19.one = bf16[512,512]{1,0:T(8,128)(2,1)S(1)} collective-permute-done((bf16[512,512]{1,0:T(8,128)(2,1)S(1)}, bf16[512,512]{1,0:T(8,128)(2,1)S(1)}, u32[]{:S(2)}, u32[]{:S(2)}) %collective-permute-start.19) | collective-permute-done | bytes 524320 | tf_op jit(solution)/shard_map/ppermute | solution.py:275
  82.5 4.2 %collective-permute-start.22 = (bf16[128,512]{1,0:T(8,128)(2,1)S(1)}, bf16[128,512]{1,0:T(8,128)(2,1)S(1)}, u32[]{:S(2)}, u32[]{:S(2)}) collective-permute-start(bf16[128,512]{1,0:T(8,128)(2,1)S(1)} %get-tuple-element.90), channel_id=1, source_target_pairs={{0,2},{1,3},{2,0},{3,1},{4,6},{5,7},{6,4},{7,5},{8,10},{9,11},{10,... | collective-permute-start | bytes 393224 | tf_op jit(solution)/shard_map/ppermute | solution.py:267
  87.1 1.0 %assemble_first.1 = (bf16[128,4096]{1,0:T(8,128)(2,1)}, bf16[128,4096]{1,0:T(8,128)(2,1)}) custom-call(s32[1]{0:T(128)} %bitcast.here_ref, bf16[128,1024]{1,0:T(8,128)(2,1)S(1)} %get-tuple-element.74.refs_0_, bf16[128,1024]{1,0:T(8,128)(2,1)S(1)} %collective-permute-done.13.refs_1_, bf16[128,1024]{1,0:T(8,128)(2,1)S(1)} %collective-permute-done.14.refs_2_, ...), custom_call_target="tpu_custom_call" | custom-call | bytes 4194304 | tf_op jit(solution)/shard_map/assemble_first/pallas_call | solution.py:130
  88.6 4.0 %collective-permute-done.22.refs_8_ = bf16[128,512]{1,0:T(8,128)(2,1)S(1)} collective-permute-done((bf16[128,512]{1,0:T(8,128)(2,1)S(1)}, bf16[128,512]{1,0:T(8,128)(2,1)S(1)}, u32[]{:S(2)}, u32[]{:S(2)}) %collective-permute-start.22) | collective-permute-done | bytes 131104 | tf_op jit(solution)/shard_map/ppermute | solution.py:267
  92.6 2.0 %collective-permute-done.23.refs_9_ = bf16[128,512]{1,0:T(8,128)(2,1)S(1)} collective-permute-done((bf16[128,512]{1,0:T(8,128)(2,1)S(1)}, bf16[128,512]{1,0:T(8,128)(2,1)S(1)}, u32[]{:S(2)}, u32[]{:S(2)}) %collective-permute-start.23) | collective-permute-done | bytes 131104 | tf_op jit(solution)/shard_map/ppermute | solution.py:267
  94.6 1.3 %assemble.1 = (bf16[128,4096]{1,0:T(8,128)(2,1)}, bf16[128,4096]{1,0:T(8,128)(2,1)}, bf16[128,1024]{1,0:T(8,128)(2,1)}, bf16[128,1024]{1,0:T(8,128)(2,1)}) custom-call(s32[1]{0:T(128)} %bitcast.here_ref, bf16[128,4096]{1,0:T(8,128)(2,1)} %get-tuple-element.78.refs_0_, ...), custom_call_target="tpu_custom_call", output_to_operand_aliasing={{0}: (1, {}), {1}: (2, {})} | custom-call | bytes 4194304 | tf_op jit(solution)/shard_map/assemble/pallas_call | solution.py:130
  (58 shorter events, 4.7 us)
Async XLA Ops:
  2.6 13.3 %collective-permute-start = (bf16[128,512]{1,0:T(8,128)(2,1)}, bf16[128,512]{1,0:T(8,128)(2,1)S(1)}, u32[]{:S(2)}, u32[]{:S(2)}) collective-permute-start(bf16[128,512]{1,0:T(8,128)(2,1)} %get-tuple-element.53), channel_id=1, source_target_pairs={{0,1},{1,0},{2,3},{3,2},{4,5},{5,4},{6,7},{7,6},{8,9},{9,8},{10,11... | collective-permute-start | bytes 393224 | tf_op jit(solution)/shard_map/ppermute | solution.py:267
  4.2 12.4 %collective-permute-start.1 = (bf16[128,512]{1,0:T(8,128)(2,1)}, bf16[128,512]{1,0:T(8,128)(2,1)S(1)}, u32[]{:S(2)}, u32[]{:S(2)}) collective-permute-start(bf16[128,512]{1,0:T(8,128)(2,1)} %get-tuple-element.54), channel_id=1, source_target_pairs={{0,2},{1,3},{2,0},{3,1},{4,6},{5,7},{6,4},{7,5},{8,10},{9,11},{10,... | collective-permute-start | bytes 393224 | tf_op jit(solution)/shard_map/ppermute | solution.py:267
  6.9 9.7 %collective-permute-start.2 = (bf16[128,512]{1,0:T(8,128)(2,1)}, bf16[128,512]{1,0:T(8,128)(2,1)S(1)}, u32[]{:S(2)}, u32[]{:S(2)}) collective-permute-start(bf16[128,512]{1,0:T(8,128)(2,1)} %get-tuple-element.55), channel_id=1, source_target_pairs={{0,3},{1,2},{2,1},{3,0},{4,7},{5,6},{6,5},{7,4},{8,11},{9,10},{10,... | collective-permute-start | bytes 393224 | tf_op jit(solution)/shard_map/ppermute | solution.py:267
  10.5 12.0 %collective-permute-start.8 = (bf16[128,1024]{1,0:T(8,128)(2,1)}, bf16[128,1024]{1,0:T(8,128)(2,1)S(1)}, u32[]{:S(2)}, u32[]{:S(2)}) collective-permute-start(bf16[128,1024]{1,0:T(8,128)(2,1)} %get-tuple-element.61), channel_id=1, source_target_pairs={{0,1},{1,0},{2,3},{3,2},{4,5},{5,4},{6,7},{7,6},{8,9},{9,8},{10,11... | collective-permute-start | bytes 786440 | tf_op jit(solution)/shard_map/ppermute | solution.py:267
  10.9 15.8 %collective-permute-start.9 = (bf16[128,1024]{1,0:T(8,128)(2,1)}, bf16[128,1024]{1,0:T(8,128)(2,1)S(1)}, u32[]{:S(2)}, u32[]{:S(2)}) collective-permute-start(bf16[128,1024]{1,0:T(8,128)(2,1)} %get-tuple-element.62), channel_id=1, source_target_pairs={{0,2},{1,3},{2,0},{3,1},{4,6},{5,7},{6,4},{7,5},{8,10},{9,11},{10,... | collective-permute-start | bytes 786440 | tf_op jit(solution)/shard_map/ppermute | solution.py:267
  16.1 13.7 %collective-permute-start.10 = (bf16[128,1024]{1,0:T(8,128)(2,1)S(1)}, bf16[128,1024]{1,0:T(8,128)(2,1)S(1)}, u32[]{:S(2)}, u32[]{:S(2)}) collective-permute-start(bf16[128,1024]{1,0:T(8,128)(2,1)S(1)} %copy-done.7), channel_id=1, source_target_pairs={{0,3},{1,2},{2,1},{3,0},{4,7},{5,6},{6,5},{7,4},{8,11},{9,10},{10,... | collective-permute-start | bytes 786440 | tf_op jit(solution)/shard_map/ppermute | solution.py:267
  16.7 13.2 %collective-permute-start.12 = (bf16[512,256]{1,0:T(8,128)(2,1)S(1)}, bf16[512,256]{1,0:T(8,128)(2,1)S(1)}, u32[]{:S(2)}, u32[]{:S(2)}) collective-permute-start(bf16[512,256]{1,0:T(8,128)(2,1)S(1)} %pad_maximum_fusion.refs_4_), channel_id=1, source_target_pairs={{0,8},{1,9},{2,10},{3,11},{4,12},{5,13},{6,14},{7,15},{8,16},{9,17... | collective-permute-start | bytes 786440 | tf_op jit(solution)/shard_map/ppermute | solution.py:275
  18.8 15.4 %collective-permute-start.11 = (bf16[512,256]{1,0:T(8,128)(2,1)S(1)}, bf16[512,256]{1,0:T(8,128)(2,1)S(1)}, u32[]{:S(2)}, u32[]{:S(2)}) collective-permute-start(bf16[512,256]{1,0:T(8,128)(2,1)S(1)} %pad_maximum_fusion.refs_4_), channel_id=1, source_target_pairs={{0,4},{1,5},{2,6},{3,7},{4,8},{5,9},{6,10},{7,11},{8,12},{9,13},{1... | collective-permute-start | bytes 786440 | tf_op jit(solution)/shard_map/ppermute | solution.py:275
  22.5 22.6 %collective-permute-start.7 = (bf16[512,256]{1,0:T(8,128)(2,1)S(1)}, bf16[512,256]{1,0:T(8,128)(2,1)S(1)}, u32[]{:S(2)}, u32[]{:S(2)}) collective-permute-start(bf16[512,256]{1,0:T(8,128)(2,1)S(1)} %pad_maximum_fusion.1.refs_4_), channel_id=1, source_target_pairs={{0,8},{1,9},{2,10},{3,11},{4,12},{5,13},{6,14},{7,15},{8,16},{9,17... | collective-permute-start | bytes 786440 | tf_op jit(solution)/shard_map/ppermute | solution.py:275
  26.7 18.5 %collective-permute-start.6 = (bf16[512,256]{1,0:T(8,128)(2,1)S(1)}, bf16[512,256]{1,0:T(8,128)(2,1)S(1)}, u32[]{:S(2)}, u32[]{:S(2)}) collective-permute-start(bf16[512,256]{1,0:T(8,128)(2,1)S(1)} %pad_maximum_fusion.1.refs_4_), channel_id=1, source_target_pairs={{0,4},{1,5},{2,6},{3,7},{4,8},{5,9},{6,10},{7,11},{8,12},{9,13},{1... | collective-permute-start | bytes 786440 | tf_op jit(solution)/shard_map/ppermute | solution.py:275
  29.9 19.6 %collective-permute-start.3 = (bf16[128,1024]{1,0:T(8,128)(2,1)S(1)}, bf16[128,1024]{1,0:T(8,128)(2,1)S(1)}, u32[]{:S(2)}, u32[]{:S(2)}) collective-permute-start(bf16[128,1024]{1,0:T(8,128)(2,1)S(1)} %copy-done.6), channel_id=1, source_target_pairs={{0,1},{1,0},{2,3},{3,2},{4,5},{5,4},{6,7},{7,6},{8,9},{9,8},{10,11... | collective-permute-start | bytes 786440 | tf_op jit(solution)/shard_map/ppermute | solution.py:267
  30.0 19.9 %collective-permute-start.4 = (bf16[128,1024]{1,0:T(8,128)(2,1)S(1)}, bf16[128,1024]{1,0:T(8,128)(2,1)S(1)}, u32[]{:S(2)}, u32[]{:S(2)}) collective-permute-start(bf16[128,1024]{1,0:T(8,128)(2,1)S(1)} %copy-done.5), channel_id=1, source_target_pairs={{0,2},{1,3},{2,0},{3,1},{4,6},{5,7},{6,4},{7,5},{8,10},{9,11},{10,... | collective-permute-start | bytes 786440 | tf_op jit(solution)/shard_map/ppermute | solution.py:267
  34.2 15.7 %collective-permute-start.5 = (bf16[128,1024]{1,0:T(8,128)(2,1)S(1)}, bf16[128,1024]{1,0:T(8,128)(2,1)S(1)}, u32[]{:S(2)}, u32[]{:S(2)}) collective-permute-start(bf16[128,1024]{1,0:T(8,128)(2,1)S(1)} %copy-done.4), channel_id=1, source_target_pairs={{0,3},{1,2},{2,1},{3,0},{4,7},{5,6},{6,5},{7,4},{8,11},{9,10},{10,... | collective-permute-start | bytes 786440 | tf_op jit(solution)/shard_map/ppermute | solution.py:267
  45.1 22.8 %collective-permute-start.13 = (bf16[128,1024]{1,0:T(8,128)(2,1)S(1)}, bf16[128,1024]{1,0:T(8,128)(2,1)S(1)}, u32[]{:S(2)}, u32[]{:S(2)}) collective-permute-start(bf16[128,1024]{1,0:T(8,128)(2,1)S(1)} %get-tuple-element.71), channel_id=1, source_target_pairs={{0,1},{1,0},{2,3},{3,2},{4,5},{5,4},{6,7},{7,6},{8,9},{9,8},{10,11... | collective-permute-start | bytes 786440 | tf_op jit(solution)/shard_map/ppermute | solution.py:267
  45.2 22.7 %collective-permute-start.14 = (bf16[128,1024]{1,0:T(8,128)(2,1)S(1)}, bf16[128,1024]{1,0:T(8,128)(2,1)S(1)}, u32[]{:S(2)}, u32[]{:S(2)}) collective-permute-start(bf16[128,1024]{1,0:T(8,128)(2,1)S(1)} %get-tuple-element.72), channel_id=1, source_target_pairs={{0,2},{1,3},{2,0},{3,1},{4,6},{5,7},{6,4},{7,5},{8,10},{9,11},{10,... | collective-permute-start | bytes 786440 | tf_op jit(solution)/shard_map/ppermute | solution.py:267
  49.4 18.6 %collective-permute-start.15 = (bf16[128,1024]{1,0:T(8,128)(2,1)S(1)}, bf16[128,1024]{1,0:T(8,128)(2,1)S(1)}, u32[]{:S(2)}, u32[]{:S(2)}) collective-permute-start(bf16[128,1024]{1,0:T(8,128)(2,1)S(1)} %get-tuple-element.73), channel_id=1, source_target_pairs={{0,3},{1,2},{2,1},{3,0},{4,7},{5,6},{6,5},{7,4},{8,11},{9,10},{10,... | collective-permute-start | bytes 786440 | tf_op jit(solution)/shard_map/ppermute | solution.py:267
  60.4 21.8 %collective-permute-start.19 = (bf16[512,512]{1,0:T(8,128)(2,1)S(1)}, bf16[512,512]{1,0:T(8,128)(2,1)S(1)}, u32[]{:S(2)}, u32[]{:S(2)}) collective-permute-start(bf16[512,512]{1,0:T(8,128)(2,1)S(1)} %get-tuple-element.86), channel_id=1, source_target_pairs={{4,0},{5,1},{6,2},{7,3},{8,4},{9,5},{10,6},{11,7},{12,8},{13,9},{1... | collective-permute-start | bytes 1572872 | tf_op jit(solution)/shard_map/ppermute | solution.py:275
  66.0 16.1 %collective-permute-start.20 = (bf16[512,512]{1,0:T(8,128)(2,1)S(1)}, bf16[512,512]{1,0:T(8,128)(2,1)S(1)}, u32[]{:S(2)}, u32[]{:S(2)}) collective-permute-start(bf16[512,512]{1,0:T(8,128)(2,1)S(1)} %get-tuple-element.87), channel_id=1, source_target_pairs={{8,0},{9,1},{10,2},{11,3},{12,4},{13,5},{14,6},{15,7},{16,8},{17,9... | collective-permute-start | bytes 1572872 | tf_op jit(solution)/shard_map/ppermute | solution.py:275
  68.0 18.7 %collective-permute-start.16 = (bf16[128,1024]{1,0:T(8,128)(2,1)S(1)}, bf16[128,1024]{1,0:T(8,128)(2,1)S(1)}, u32[]{:S(2)}, u32[]{:S(2)}) collective-permute-start(bf16[128,1024]{1,0:T(8,128)(2,1)S(1)} %get-tuple-element.81), channel_id=1, source_target_pairs={{0,1},{1,0},{2,3},{3,2},{4,5},{5,4},{6,7},{7,6},{8,9},{9,8},{10,11... | collective-permute-start | bytes 786440 | tf_op jit(solution)/shard_map/ppermute | solution.py:267
  68.1 20.1 %collective-permute-start.17 = (bf16[128,1024]{1,0:T(8,128)(2,1)S(1)}, bf16[128,1024]{1,0:T(8,128)(2,1)S(1)}, u32[]{:S(2)}, u32[]{:S(2)}) collective-permute-start(bf16[128,1024]{1,0:T(8,128)(2,1)S(1)} %get-tuple-element.82), channel_id=1, source_target_pairs={{0,2},{1,3},{2,0},{3,1},{4,6},{5,7},{6,4},{7,5},{8,10},{9,11},{10,... | collective-permute-start | bytes 786440 | tf_op jit(solution)/shard_map/ppermute | solution.py:267
  71.4 16.8 %collective-permute-start.18 = (bf16[128,1024]{1,0:T(8,128)(2,1)S(1)}, bf16[128,1024]{1,0:T(8,128)(2,1)S(1)}, u32[]{:S(2)}, u32[]{:S(2)}) collective-permute-start(bf16[128,1024]{1,0:T(8,128)(2,1)S(1)} %get-tuple-element.83), channel_id=1, source_target_pairs={{0,3},{1,2},{2,1},{3,0},{4,7},{5,6},{6,5},{7,4},{8,11},{9,10},{10,... | collective-permute-start | bytes 786440 | tf_op jit(solution)/shard_map/ppermute | solution.py:267
  82.4 6.3 %collective-permute-start.21 = (bf16[128,512]{1,0:T(8,128)(2,1)S(1)}, bf16[128,512]{1,0:T(8,128)(2,1)S(1)}, u32[]{:S(2)}, u32[]{:S(2)}) collective-permute-start(bf16[128,512]{1,0:T(8,128)(2,1)S(1)} %get-tuple-element.89), channel_id=1, source_target_pairs={{0,1},{1,0},{2,3},{3,2},{4,5},{5,4},{6,7},{7,6},{8,9},{9,8},{10,11... | collective-permute-start | bytes 393224 | tf_op jit(solution)/shard_map/ppermute | solution.py:267
  82.5 10.1 %collective-permute-start.22 = (bf16[128,512]{1,0:T(8,128)(2,1)S(1)}, bf16[128,512]{1,0:T(8,128)(2,1)S(1)}, u32[]{:S(2)}, u32[]{:S(2)}) collective-permute-start(bf16[128,512]{1,0:T(8,128)(2,1)S(1)} %get-tuple-element.90), channel_id=1, source_target_pairs={{0,2},{1,3},{2,0},{3,1},{4,6},{5,7},{6,4},{7,5},{8,10},{9,11},{10,... | collective-permute-start | bytes 393224 | tf_op jit(solution)/shard_map/ppermute | solution.py:267
  86.7 7.9 %collective-permute-start.23 = (bf16[128,512]{1,0:T(8,128)(2,1)S(1)}, bf16[128,512]{1,0:T(8,128)(2,1)S(1)}, u32[]{:S(2)}, u32[]{:S(2)}) collective-permute-start(bf16[128,512]{1,0:T(8,128)(2,1)S(1)} %get-tuple-element.91), channel_id=1, source_target_pairs={{0,3},{1,2},{2,1},{3,0},{4,7},{5,6},{6,5},{7,4},{8,11},{9,10},{10,... | collective-permute-start | bytes 393224 | tf_op jit(solution)/shard_map/ppermute | solution.py:267
  (8 other events, 74.9 us)

commit v4 on v3

--- a/solution.py
+++ b/solution.py
@@ -267,11 +267,8 @@
         return lax.ppermute(value, "head", [(i, i ^ d) for i in range(heads)])
 
     def along_halves(value, steps):
-        pairs = [
-            (i * RING + x, (i + steps) * RING + x)
-            for i in range(max(0, -steps), min(halves, halves - steps))
-            for x in range(RING)
-        ]
+        count = halves * RING
+        pairs = [(i, (i + steps * RING) % count) for i in range(count)]
         return lax.ppermute(value, ("blk", "head"), pairs)
 
     def around(parts):

time: 96.5 us -> 91.2 us (0.945)
  the two profiles are of different devices: /device:TPU:96 before, /device:TPU:160 now
where the time goes in v4:
time: 91.2 us; the launch traced here: 90.1 us
  starting transfers between devices  37.4 us (41%)
  Pallas kernels  28.5 us (31%)
  waiting for transfers between devices  21.6 us (24%)
  local copies, waits for them, and re-layouts  1.09 us (1%)
  between operations  1.09 us (1%)
    ppermute x18, starting transfers between devices, along_ring(): return lax.ppermute(value, 'head', [(i, i ^ d) for i in range(heads)])  28.6 us
    pallas_call x7, Pallas kernels, call(): pl.pallas_call(body, out_shape=[jax.ShapeDtypeStruct(shape, dtype) for sh...  28.5 us
    ppermute x18, waiting for transfers between devices, along_ring(): return lax.ppermute(value, 'head', [(i, i ^ d) for i in range(heads)])  10.9 us
    ppermute x6, waiting for transfers between devices, along_halves(): return lax.ppermute(value, ('blk', 'head'), pairs)  10.7 us
    ppermute x6, starting transfers between devices, along_halves(): return lax.ppermute(value, ('blk', 'head'), pairs)  8.83 us
  transfers between devices with their start and end apart: 24, of which 7 were waited for; matrix products, arithmetic and copies ran while one was open for 1% of the time, Pallas kernels for 28%

profile of v4, /device:TPU:160, one launch (start us, length us, event | category | flops | bytes accessed | tf_op | source)
XLA Modules:
  0.0 90.1 jit_solution(15243488156935646547)
XLA Ops:
  0.6 2.0 %pack_kv.1 = (bf16[128,512]{1,0:T(8,128)(2,1)}, bf16[128,512]{1,0:T(8,128)(2,1)}, bf16[128,512]{1,0:T(8,128)(2,1)}, bf16[128,512]{1,0:T(8,128)(2,1)}) custom-call(s32[1]{0:T(128)} %bitcast.here_ref, bf16[128,1024]{1,0:T(8,128)(2,1)} %k_ref.1, bf16[128,1024]{1,0:T(8,128)(2,1)} %v_ref.1), custom_call_target="tpu_custom_call" | custom-call | bytes 4194304 | tf_op jit(solution)/shard_map/pack_kv/pallas_call | solution.py:130
  2.6 1.6 %collective-permute-start = (bf16[128,512]{1,0:T(8,128)(2,1)}, bf16[128,512]{1,0:T(8,128)(2,1)S(1)}, u32[]{:S(2)}, u32[]{:S(2)}) collective-permute-start(bf16[128,512]{1,0:T(8,128)(2,1)} %get-tuple-element.53), channel_id=1, source_target_pairs={{0,1},{1,0},{2,3},{3,2},{4,5},{5,4},{6,7},{7,6},{8,9},{9,8},{10,11... | collective-permute-start | bytes 393224 | tf_op jit(solution)/shard_map/ppermute | solution.py:267
  4.2 2.7 %collective-permute-start.1 = (bf16[128,512]{1,0:T(8,128)(2,1)}, bf16[128,512]{1,0:T(8,128)(2,1)S(1)}, u32[]{:S(2)}, u32[]{:S(2)}) collective-permute-start(bf16[128,512]{1,0:T(8,128)(2,1)} %get-tuple-element.54), channel_id=1, source_target_pairs={{0,2},{1,3},{2,0},{3,1},{4,6},{5,7},{6,4},{7,5},{8,10},{9,11},{10,... | collective-permute-start | bytes 393224 | tf_op jit(solution)/shard_map/ppermute | solution.py:267
  7.4 3.1 %pack_q.1 = (bf16[128,1024]{1,0:T(8,128)(2,1)}, bf16[128,1024]{1,0:T(8,128)(2,1)}, bf16[128,1024]{1,0:T(8,128)(2,1)}, bf16[128,1024]{1,0:T(8,128)(2,1)}, bf16[12...) custom-call(s32[1]{0:T(128)} %bitcast.here_ref, ...), custom_call_target="tpu_custom_call" | custom-call | bytes 4194304 | tf_op jit(solution)/shard_map/pack_q/pallas_call | solution.py:130
  10.9 3.9 %collective-permute-start.9 = (bf16[128,1024]{1,0:T(8,128)(2,1)}, bf16[128,1024]{1,0:T(8,128)(2,1)S(1)}, u32[]{:S(2)}, u32[]{:S(2)}) collective-permute-start(bf16[128,1024]{1,0:T(8,128)(2,1)} %get-tuple-element.62), channel_id=1, source_target_pairs={{0,2},{1,3},{2,0},{3,1},{4,6},{5,7},{6,4},{7,5},{8,10},{9,11},{10,... | collective-permute-start | bytes 786440 | tf_op jit(solution)/shard_map/ppermute | solution.py:267
  16.8 1.7 %collective-permute-start.11 = (bf16[512,256]{1,0:T(8,128)(2,1)S(1)}, bf16[512,256]{1,0:T(8,128)(2,1)S(1)}, u32[]{:S(2)}, u32[]{:S(2)}) collective-permute-start(bf16[512,256]{1,0:T(8,128)(2,1)S(1)} %pad_maximum_fusion.refs_4_), channel_id=1, source_target_pairs={{0,4},{1,5},{2,6},{3,7},{4,8},{5,9},{6,10},{7,11},{8,12},{9,13},{1... | collective-permute-start | bytes 786440 | tf_op jit(solution)/shard_map/ppermute | solution.py:272
  20.8 5.1 %collective-permute-done.9.refs_2_ = bf16[128,1024]{1,0:T(8,128)(2,1)S(1)} collective-permute-done((bf16[128,1024]{1,0:T(8,128)(2,1)}, bf16[128,1024]{1,0:T(8,128)(2,1)S(1)}, u32[]{:S(2)}, u32[]{:S(2)}) %collective-permute-start.9) | collective-permute-done | bytes 262176 | tf_op jit(solution)/shard_map/ppermute | solution.py:267
  25.9 1.6 %collective-permute-start.6 = (bf16[512,256]{1,0:T(8,128)(2,1)S(1)}, bf16[512,256]{1,0:T(8,128)(2,1)S(1)}, u32[]{:S(2)}, u32[]{:S(2)}) collective-permute-start(bf16[512,256]{1,0:T(8,128)(2,1)S(1)} %pad_maximum_fusion.1.refs_4_), channel_id=1, source_target_pairs={{0,4},{1,5},{2,6},{3,7},{4,8},{5,9},{6,10},{7,11},{8,12},{9,13},{1... | collective-permute-start | bytes 786440 | tf_op jit(solution)/shard_map/ppermute | solution.py:272
  27.5 2.0 %collective-permute-done.10.refs_3_ = bf16[128,1024]{1,0:T(8,128)(2,1)S(1)} collective-permute-done((bf16[128,1024]{1,0:T(8,128)(2,1)S(1)}, bf16[128,1024]{1,0:T(8,128)(2,1)S(1)}, u32[]{:S(2)}, u32[]{:S(2)}) %collective-permute-start.10) | collective-permute-done | bytes 262176 | tf_op jit(solution)/shard_map/ppermute | solution.py:267
  29.5 1.9 %collective-permute-start.4 = (bf16[128,1024]{1,0:T(8,128)(2,1)S(1)}, bf16[128,1024]{1,0:T(8,128)(2,1)S(1)}, u32[]{:S(2)}, u32[]{:S(2)}) collective-permute-start(bf16[128,1024]{1,0:T(8,128)(2,1)S(1)} %copy-done.5), channel_id=1, source_target_pairs={{0,2},{1,3},{2,0},{3,1},{4,6},{5,7},{6,4},{7,5},{8,10},{9,11},{10,... | collective-permute-start | bytes 786440 | tf_op jit(solution)/shard_map/ppermute | solution.py:267
  31.5 2.8 %collective-permute-start.5 = (bf16[128,1024]{1,0:T(8,128)(2,1)S(1)}, bf16[128,1024]{1,0:T(8,128)(2,1)S(1)}, u32[]{:S(2)}, u32[]{:S(2)}) collective-permute-start(bf16[128,1024]{1,0:T(8,128)(2,1)S(1)} %copy-done.4), channel_id=1, source_target_pairs={{0,3},{1,2},{2,1},{3,0},{4,7},{5,6},{6,5},{7,4},{8,11},{9,10},{10,... | collective-permute-start | bytes 786440 | tf_op jit(solution)/shard_map/ppermute | solution.py:267
  34.2 10.4 %attend.2 = (bf16[128,1024]{1,0:T(8,128)(2,1)S(1)}, bf16[128,1024]{1,0:T(8,128)(2,1)S(1)}, bf16[128,1024]{1,0:T(8,128)(2,1)S(1)}, bf16[128,1024]{1,0:T(8,128)(2,...) custom-call(s32[4]{0:T(128)S(1)} %iota_xor_fusion.pos_ref, ...), custom_call_target="tpu_custom_call" | custom-call | flops 7247757312 | bytes 4194304 | tf_op jit(solution)/shard_map/attend/pallas_call | solution.py:130
  44.8 1.9 %collective-permute-start.14 = (bf16[128,1024]{1,0:T(8,128)(2,1)S(1)}, bf16[128,1024]{1,0:T(8,128)(2,1)S(1)}, u32[]{:S(2)}, u32[]{:S(2)}) collective-permute-start(bf16[128,1024]{1,0:T(8,128)(2,1)S(1)} %get-tuple-element.72), channel_id=1, source_target_pairs={{0,2},{1,3},{2,0},{3,1},{4,6},{5,7},{6,4},{7,5},{8,10},{9,11},{10,... | collective-permute-start | bytes 786440 | tf_op jit(solution)/shard_map/ppermute | solution.py:267
  46.7 2.8 %collective-permute-start.15 = (bf16[128,1024]{1,0:T(8,128)(2,1)S(1)}, bf16[128,1024]{1,0:T(8,128)(2,1)S(1)}, u32[]{:S(2)}, u32[]{:S(2)}) collective-permute-start(bf16[128,1024]{1,0:T(8,128)(2,1)S(1)} %get-tuple-element.73), channel_id=1, source_target_pairs={{0,3},{1,2},{2,1},{3,0},{4,7},{5,6},{6,5},{7,4},{8,11},{9,10},{10,... | collective-permute-start | bytes 786440 | tf_op jit(solution)/shard_map/ppermute | solution.py:267
  49.5 10.5 %attend.3 = (bf16[128,1024]{1,0:T(8,128)(2,1)S(1)}, bf16[128,1024]{1,0:T(8,128)(2,1)S(1)}, bf16[128,1024]{1,0:T(8,128)(2,1)S(1)}, bf16[128,1024]{1,0:T(8,128)(2,...) custom-call(s32[4]{0:T(128)S(1)} %iota_xor_fusion.pos_ref, ...), custom_call_target="tpu_custom_call" | custom-call | flops 7247757312 | bytes 4194304 | tf_op jit(solution)/shard_map/attend/pallas_call | solution.py:130
  59.9 3.0 %collective-permute-start.19 = (bf16[512,512]{1,0:T(8,128)(2,1)S(1)}, bf16[512,512]{1,0:T(8,128)(2,1)S(1)}, u32[]{:S(2)}, u32[]{:S(2)}) collective-permute-start(bf16[512,512]{1,0:T(8,128)(2,1)S(1)} %get-tuple-element.86), channel_id=1, source_target_pairs={{0,252},{1,253},{2,254},{3,255},{4,0},{5,1},{6,2},{7,3},{8,4},{9,5... | collective-permute-start | bytes 1572872 | tf_op jit(solution)/shard_map/ppermute | solution.py:272
  62.9 1.8 %collective-permute-start.20 = (bf16[512,512]{1,0:T(8,128)(2,1)S(1)}, bf16[512,512]{1,0:T(8,128)(2,1)S(1)}, u32[]{:S(2)}, u32[]{:S(2)}) collective-permute-start(bf16[512,512]{1,0:T(8,128)(2,1)S(1)} %get-tuple-element.87), channel_id=1, source_target_pairs={{0,248},{1,249},{2,250},{3,251},{4,252},{5,253},{6,254},{7,255},{8... | collective-permute-start | bytes 1572872 | tf_op jit(solution)/shard_map/ppermute | solution.py:272
  64.8 1.9 %collective-permute-start.17 = (bf16[128,1024]{1,0:T(8,128)(2,1)S(1)}, bf16[128,1024]{1,0:T(8,128)(2,1)S(1)}, u32[]{:S(2)}, u32[]{:S(2)}) collective-permute-start(bf16[128,1024]{1,0:T(8,128)(2,1)S(1)} %get-tuple-element.82), channel_id=1, source_target_pairs={{0,2},{1,3},{2,0},{3,1},{4,6},{5,7},{6,4},{7,5},{8,10},{9,11},{10,... | collective-permute-start | bytes 786440 | tf_op jit(solution)/shard_map/ppermute | solution.py:267
  66.7 2.7 %collective-permute-start.18 = (bf16[128,1024]{1,0:T(8,128)(2,1)S(1)}, bf16[128,1024]{1,0:T(8,128)(2,1)S(1)}, u32[]{:S(2)}, u32[]{:S(2)}) collective-permute-start(bf16[128,1024]{1,0:T(8,128)(2,1)S(1)} %get-tuple-element.83), channel_id=1, source_target_pairs={{0,3},{1,2},{2,1},{3,0},{4,7},{5,6},{6,5},{7,4},{8,11},{9,10},{10,... | collective-permute-start | bytes 786440 | tf_op jit(solution)/shard_map/ppermute | solution.py:267
  69.5 7.9 %collective-permute-done.19.one = bf16[512,512]{1,0:T(8,128)(2,1)S(1)} collective-permute-done((bf16[512,512]{1,0:T(8,128)(2,1)S(1)}, bf16[512,512]{1,0:T(8,128)(2,1)S(1)}, u32[]{:S(2)}, u32[]{:S(2)}) %collective-permute-start.19) | collective-permute-done | bytes 524320 | tf_op jit(solution)/shard_map/ppermute | solution.py:272
  77.4 2.8 %collective-permute-done.20.two = bf16[512,512]{1,0:T(8,128)(2,1)S(1)} collective-permute-done((bf16[512,512]{1,0:T(8,128)(2,1)S(1)}, bf16[512,512]{1,0:T(8,128)(2,1)S(1)}, u32[]{:S(2)}, u32[]{:S(2)}) %collective-permute-start.20) | collective-permute-done | bytes 524320 | tf_op jit(solution)/shard_map/ppermute | solution.py:272
  80.5 1.9 %collective-permute-start.22 = (bf16[128,512]{1,0:T(8,128)(2,1)S(1)}, bf16[128,512]{1,0:T(8,128)(2,1)S(1)}, u32[]{:S(2)}, u32[]{:S(2)}) collective-permute-start(bf16[128,512]{1,0:T(8,128)(2,1)S(1)} %get-tuple-element.90), channel_id=1, source_target_pairs={{0,2},{1,3},{2,0},{3,1},{4,6},{5,7},{6,4},{7,5},{8,10},{9,11},{10,... | collective-permute-start | bytes 393224 | tf_op jit(solution)/shard_map/ppermute | solution.py:267
  82.4 2.8 %collective-permute-start.23 = (bf16[128,512]{1,0:T(8,128)(2,1)S(1)}, bf16[128,512]{1,0:T(8,128)(2,1)S(1)}, u32[]{:S(2)}, u32[]{:S(2)}) collective-permute-start(bf16[128,512]{1,0:T(8,128)(2,1)S(1)} %get-tuple-element.91), channel_id=1, source_target_pairs={{0,3},{1,2},{2,1},{3,0},{4,7},{5,6},{6,5},{7,4},{8,11},{9,10},{10,... | collective-permute-start | bytes 393224 | tf_op jit(solution)/shard_map/ppermute | solution.py:267
  87.0 1.6 %collective-permute-done.23.refs_9_ = bf16[128,512]{1,0:T(8,128)(2,1)S(1)} collective-permute-done((bf16[128,512]{1,0:T(8,128)(2,1)S(1)}, bf16[128,512]{1,0:T(8,128)(2,1)S(1)}, u32[]{:S(2)}, u32[]{:S(2)}) %collective-permute-start.23) | collective-permute-done | bytes 131104 | tf_op jit(solution)/shard_map/ppermute | solution.py:267
  (58 shorter events, 8.7 us)
Async XLA Ops:
  2.6 13.3 %collective-permute-start = (bf16[128,512]{1,0:T(8,128)(2,1)}, bf16[128,512]{1,0:T(8,128)(2,1)S(1)}, u32[]{:S(2)}, u32[]{:S(2)}) collective-permute-start(bf16[128,512]{1,0:T(8,128)(2,1)} %get-tuple-element.53), channel_id=1, source_target_pairs={{0,1},{1,0},{2,3},{3,2},{4,5},{5,4},{6,7},{7,6},{8,9},{9,8},{10,11... | collective-permute-start | bytes 393224 | tf_op jit(solution)/shard_map/ppermute | solution.py:267
  4.2 12.4 %collective-permute-start.1 = (bf16[128,512]{1,0:T(8,128)(2,1)}, bf16[128,512]{1,0:T(8,128)(2,1)S(1)}, u32[]{:S(2)}, u32[]{:S(2)}) collective-permute-start(bf16[128,512]{1,0:T(8,128)(2,1)} %get-tuple-element.54), channel_id=1, source_target_pairs={{0,2},{1,3},{2,0},{3,1},{4,6},{5,7},{6,4},{7,5},{8,10},{9,11},{10,... | collective-permute-start | bytes 393224 | tf_op jit(solution)/shard_map/ppermute | solution.py:267
  6.9 9.7 %collective-permute-start.2 = (bf16[128,512]{1,0:T(8,128)(2,1)}, bf16[128,512]{1,0:T(8,128)(2,1)S(1)}, u32[]{:S(2)}, u32[]{:S(2)}) collective-permute-start(bf16[128,512]{1,0:T(8,128)(2,1)} %get-tuple-element.55), channel_id=1, source_target_pairs={{0,3},{1,2},{2,1},{3,0},{4,7},{5,6},{6,5},{7,4},{8,11},{9,10},{10,... | collective-permute-start | bytes 393224 | tf_op jit(solution)/shard_map/ppermute | solution.py:267
  10.5 9.5 %collective-permute-start.8 = (bf16[128,1024]{1,0:T(8,128)(2,1)}, bf16[128,1024]{1,0:T(8,128)(2,1)S(1)}, u32[]{:S(2)}, u32[]{:S(2)}) collective-permute-start(bf16[128,1024]{1,0:T(8,128)(2,1)} %get-tuple-element.61), channel_id=1, source_target_pairs={{0,1},{1,0},{2,3},{3,2},{4,5},{5,4},{6,7},{7,6},{8,9},{9,8},{10,11... | collective-permute-start | bytes 786440 | tf_op jit(solution)/shard_map/ppermute | solution.py:267
  10.9 15.1 %collective-permute-start.9 = (bf16[128,1024]{1,0:T(8,128)(2,1)}, bf16[128,1024]{1,0:T(8,128)(2,1)S(1)}, u32[]{:S(2)}, u32[]{:S(2)}) collective-permute-start(bf16[128,1024]{1,0:T(8,128)(2,1)} %get-tuple-element.62), channel_id=1, source_target_pairs={{0,2},{1,3},{2,0},{3,1},{4,6},{5,7},{6,4},{7,5},{8,10},{9,11},{10,... | collective-permute-start | bytes 786440 | tf_op jit(solution)/shard_map/ppermute | solution.py:267
  16.1 13.4 %collective-permute-start.10 = (bf16[128,1024]{1,0:T(8,128)(2,1)S(1)}, bf16[128,1024]{1,0:T(8,128)(2,1)S(1)}, u32[]{:S(2)}, u32[]{:S(2)}) collective-permute-start(bf16[128,1024]{1,0:T(8,128)(2,1)S(1)} %copy-done.7), channel_id=1, source_target_pairs={{0,3},{1,2},{2,1},{3,0},{4,7},{5,6},{6,5},{7,4},{8,11},{9,10},{10,... | collective-permute-start | bytes 786440 | tf_op jit(solution)/shard_map/ppermute | solution.py:267
  16.7 12.8 %collective-permute-start.12 = (bf16[512,256]{1,0:T(8,128)(2,1)S(1)}, bf16[512,256]{1,0:T(8,128)(2,1)S(1)}, u32[]{:S(2)}, u32[]{:S(2)}) collective-permute-start(bf16[512,256]{1,0:T(8,128)(2,1)S(1)} %pad_maximum_fusion.refs_4_), channel_id=1, source_target_pairs={{0,8},{1,9},{2,10},{3,11},{4,12},{5,13},{6,14},{7,15},{8,16},{9,17... | collective-permute-start | bytes 786440 | tf_op jit(solution)/shard_map/ppermute | solution.py:272
  16.8 14.6 %collective-permute-start.11 = (bf16[512,256]{1,0:T(8,128)(2,1)S(1)}, bf16[512,256]{1,0:T(8,128)(2,1)S(1)}, u32[]{:S(2)}, u32[]{:S(2)}) collective-permute-start(bf16[512,256]{1,0:T(8,128)(2,1)S(1)} %pad_maximum_fusion.refs_4_), channel_id=1, source_target_pairs={{0,4},{1,5},{2,6},{3,7},{4,8},{5,9},{6,10},{7,11},{8,12},{9,13},{1... | collective-permute-start | bytes 786440 | tf_op jit(solution)/shard_map/ppermute | solution.py:272
  20.0 24.6 %collective-permute-start.7 = (bf16[512,256]{1,0:T(8,128)(2,1)S(1)}, bf16[512,256]{1,0:T(8,128)(2,1)S(1)}, u32[]{:S(2)}, u32[]{:S(2)}) collective-permute-start(bf16[512,256]{1,0:T(8,128)(2,1)S(1)} %pad_maximum_fusion.1.refs_4_), channel_id=1, source_target_pairs={{0,8},{1,9},{2,10},{3,11},{4,12},{5,13},{6,14},{7,15},{8,16},{9,17... | collective-permute-start | bytes 786440 | tf_op jit(solution)/shard_map/ppermute | solution.py:272
  25.9 18.8 %collective-permute-start.6 = (bf16[512,256]{1,0:T(8,128)(2,1)S(1)}, bf16[512,256]{1,0:T(8,128)(2,1)S(1)}, u32[]{:S(2)}, u32[]{:S(2)}) collective-permute-start(bf16[512,256]{1,0:T(8,128)(2,1)S(1)} %pad_maximum_fusion.1.refs_4_), channel_id=1, source_target_pairs={{0,4},{1,5},{2,6},{3,7},{4,8},{5,9},{6,10},{7,11},{8,12},{9,13},{1... | collective-permute-start | bytes 786440 | tf_op jit(solution)/shard_map/ppermute | solution.py:272
  29.5 17.2 %collective-permute-start.3 = (bf16[128,1024]{1,0:T(8,128)(2,1)S(1)}, bf16[128,1024]{1,0:T(8,128)(2,1)S(1)}, u32[]{:S(2)}, u32[]{:S(2)}) collective-permute-start(bf16[128,1024]{1,0:T(8,128)(2,1)S(1)} %copy-done.6), channel_id=1, source_target_pairs={{0,1},{1,0},{2,3},{3,2},{4,5},{5,4},{6,7},{7,6},{8,9},{9,8},{10,11... | collective-permute-start | bytes 786440 | tf_op jit(solution)/shard_map/ppermute | solution.py:267
  29.5 19.9 %collective-permute-start.4 = (bf16[128,1024]{1,0:T(8,128)(2,1)S(1)}, bf16[128,1024]{1,0:T(8,128)(2,1)S(1)}, u32[]{:S(2)}, u32[]{:S(2)}) collective-permute-start(bf16[128,1024]{1,0:T(8,128)(2,1)S(1)} %copy-done.5), channel_id=1, source_target_pairs={{0,2},{1,3},{2,0},{3,1},{4,6},{5,7},{6,4},{7,5},{8,10},{9,11},{10,... | collective-permute-start | bytes 786440 | tf_op jit(solution)/shard_map/ppermute | solution.py:267
  31.5 18.0 %collective-permute-start.5 = (bf16[128,1024]{1,0:T(8,128)(2,1)S(1)}, bf16[128,1024]{1,0:T(8,128)(2,1)S(1)}, u32[]{:S(2)}, u32[]{:S(2)}) collective-permute-start(bf16[128,1024]{1,0:T(8,128)(2,1)S(1)} %copy-done.4), channel_id=1, source_target_pairs={{0,3},{1,2},{2,1},{3,0},{4,7},{5,6},{6,5},{7,4},{8,11},{9,10},{10,... | collective-permute-start | bytes 786440 | tf_op jit(solution)/shard_map/ppermute | solution.py:267
  44.7 20.0 %collective-permute-start.13 = (bf16[128,1024]{1,0:T(8,128)(2,1)S(1)}, bf16[128,1024]{1,0:T(8,128)(2,1)S(1)}, u32[]{:S(2)}, u32[]{:S(2)}) collective-permute-start(bf16[128,1024]{1,0:T(8,128)(2,1)S(1)} %get-tuple-element.71), channel_id=1, source_target_pairs={{0,1},{1,0},{2,3},{3,2},{4,5},{5,4},{6,7},{7,6},{8,9},{9,8},{10,11... | collective-permute-start | bytes 786440 | tf_op jit(solution)/shard_map/ppermute | solution.py:267
  44.8 19.9 %collective-permute-start.14 = (bf16[128,1024]{1,0:T(8,128)(2,1)S(1)}, bf16[128,1024]{1,0:T(8,128)(2,1)S(1)}, u32[]{:S(2)}, u32[]{:S(2)}) collective-permute-start(bf16[128,1024]{1,0:T(8,128)(2,1)S(1)} %get-tuple-element.72), channel_id=1, source_target_pairs={{0,2},{1,3},{2,0},{3,1},{4,6},{5,7},{6,4},{7,5},{8,10},{9,11},{10,... | collective-permute-start | bytes 786440 | tf_op jit(solution)/shard_map/ppermute | solution.py:267
  46.7 18.0 %collective-permute-start.15 = (bf16[128,1024]{1,0:T(8,128)(2,1)S(1)}, bf16[128,1024]{1,0:T(8,128)(2,1)S(1)}, u32[]{:S(2)}, u32[]{:S(2)}) collective-permute-start(bf16[128,1024]{1,0:T(8,128)(2,1)S(1)} %get-tuple-element.73), channel_id=1, source_target_pairs={{0,3},{1,2},{2,1},{3,0},{4,7},{5,6},{6,5},{7,4},{8,11},{9,10},{10,... | collective-permute-start | bytes 786440 | tf_op jit(solution)/shard_map/ppermute | solution.py:267
  59.9 17.4 %collective-permute-start.19 = (bf16[512,512]{1,0:T(8,128)(2,1)S(1)}, bf16[512,512]{1,0:T(8,128)(2,1)S(1)}, u32[]{:S(2)}, u32[]{:S(2)}) collective-permute-start(bf16[512,512]{1,0:T(8,128)(2,1)S(1)} %get-tuple-element.86), channel_id=1, source_target_pairs={{0,252},{1,253},{2,254},{3,255},{4,0},{5,1},{6,2},{7,3},{8,4},{9,5... | collective-permute-start | bytes 1572872 | tf_op jit(solution)/shard_map/ppermute | solution.py:272
  62.9 17.3 %collective-permute-start.20 = (bf16[512,512]{1,0:T(8,128)(2,1)S(1)}, bf16[512,512]{1,0:T(8,128)(2,1)S(1)}, u32[]{:S(2)}, u32[]{:S(2)}) collective-permute-start(bf16[512,512]{1,0:T(8,128)(2,1)S(1)} %get-tuple-element.87), channel_id=1, source_target_pairs={{0,248},{1,249},{2,250},{3,251},{4,252},{5,253},{6,254},{7,255},{8... | collective-permute-start | bytes 1572872 | tf_op jit(solution)/shard_map/ppermute | solution.py:272
  64.7 17.7 %collective-permute-start.16 = (bf16[128,1024]{1,0:T(8,128)(2,1)S(1)}, bf16[128,1024]{1,0:T(8,128)(2,1)S(1)}, u32[]{:S(2)}, u32[]{:S(2)}) collective-permute-start(bf16[128,1024]{1,0:T(8,128)(2,1)S(1)} %get-tuple-element.81), channel_id=1, source_target_pairs={{0,1},{1,0},{2,3},{3,2},{4,5},{5,4},{6,7},{7,6},{8,9},{9,8},{10,11... | collective-permute-start | bytes 786440 | tf_op jit(solution)/shard_map/ppermute | solution.py:267
  64.8 21.4 %collective-permute-start.17 = (bf16[128,1024]{1,0:T(8,128)(2,1)S(1)}, bf16[128,1024]{1,0:T(8,128)(2,1)S(1)}, u32[]{:S(2)}, u32[]{:S(2)}) collective-permute-start(bf16[128,1024]{1,0:T(8,128)(2,1)S(1)} %get-tuple-element.82), channel_id=1, source_target_pairs={{0,2},{1,3},{2,0},{3,1},{4,6},{5,7},{6,4},{7,5},{8,10},{9,11},{10,... | collective-permute-start | bytes 786440 | tf_op jit(solution)/shard_map/ppermute | solution.py:267
  66.7 19.5 %collective-permute-start.18 = (bf16[128,1024]{1,0:T(8,128)(2,1)S(1)}, bf16[128,1024]{1,0:T(8,128)(2,1)S(1)}, u32[]{:S(2)}, u32[]{:S(2)}) collective-permute-start(bf16[128,1024]{1,0:T(8,128)(2,1)S(1)} %get-tuple-element.83), channel_id=1, source_target_pairs={{0,3},{1,2},{2,1},{3,0},{4,7},{5,6},{6,5},{7,4},{8,11},{9,10},{10,... | collective-permute-start | bytes 786440 | tf_op jit(solution)/shard_map/ppermute | solution.py:267
  80.4 5.8 %collective-permute-start.21 = (bf16[128,512]{1,0:T(8,128)(2,1)S(1)}, bf16[128,512]{1,0:T(8,128)(2,1)S(1)}, u32[]{:S(2)}, u32[]{:S(2)}) collective-permute-start(bf16[128,512]{1,0:T(8,128)(2,1)S(1)} %get-tuple-element.89), channel_id=1, source_target_pairs={{0,1},{1,0},{2,3},{3,2},{4,5},{5,4},{6,7},{7,6},{8,9},{9,8},{10,11... | collective-permute-start | bytes 393224 | tf_op jit(solution)/shard_map/ppermute | solution.py:267
  80.5 6.6 %collective-permute-start.22 = (bf16[128,512]{1,0:T(8,128)(2,1)S(1)}, bf16[128,512]{1,0:T(8,128)(2,1)S(1)}, u32[]{:S(2)}, u32[]{:S(2)}) collective-permute-start(bf16[128,512]{1,0:T(8,128)(2,1)S(1)} %get-tuple-element.90), channel_id=1, source_target_pairs={{0,2},{1,3},{2,0},{3,1},{4,6},{5,7},{6,4},{7,5},{8,10},{9,11},{10,... | collective-permute-start | bytes 393224 | tf_op jit(solution)/shard_map/ppermute | solution.py:267
  82.4 6.2 %collective-permute-start.23 = (bf16[128,512]{1,0:T(8,128)(2,1)S(1)}, bf16[128,512]{1,0:T(8,128)(2,1)S(1)}, u32[]{:S(2)}, u32[]{:S(2)}) collective-permute-start(bf16[128,512]{1,0:T(8,128)(2,1)S(1)} %get-tuple-element.91), channel_id=1, source_target_pairs={{0,3},{1,2},{2,1},{3,0},{4,7},{5,6},{6,5},{7,4},{8,11},{9,10},{10,... | collective-permute-start | bytes 393224 | tf_op jit(solution)/shard_map/ppermute | solution.py:267
  (8 other events, 78.6 us)
